TPU v7x, 256 devices: a whole 4x4x8 slice. The times are simulated.
256 devices in a mesh: seq: 32 (over x, y, core), head: 8 (over z).
Axes of the slice: x: 4, y: 4, z: 8, core: 2. Of those that a mesh axis runs over, the one named last changes fastest.
Arguments:
- layer_input: bfloat16 [32768, 6144], P('seq', 'head'), may hold values from -6 to 6
- queries: bfloat16 [32768, 4096], P('seq', 'head'), may hold values from -6 to 6
- keys: bfloat16 [32768, 4096], P('seq', 'head'), may hold values from -6 to 6
- values: bfloat16 [32768, 4096], P('seq', 'head'), may hold values from -6 to 6
- out_grad: bfloat16 [32768, 4096], P('seq', 'head'), may hold values from -6 to 6
Outputs:
- query_grad: bfloat16 [32768, 4096], P('seq', 'head')
- key_grad: bfloat16 [32768, 4096], P('seq', 'head')
- weight_grad: float32 [6144, 4096], P('seq', 'head')
All inputs are finite; a program needn't handle non-finite values.
Results may differ from a plain program's by a relative error of at most 0.024.
Values may be sent and summed in bfloat16 or wider, within the bound.
No kernel may reach another device: no remote copies, remote signals or barrier semaphores. Data moves between devices by JAX's collectives and lax.ppermute only.
A program may use at most 128 MiB of HBM per device.

v0:
```python
import math

import jax
import jax.numpy as jnp
from jax import lax
from jax.sharding import PartitionSpec as P

DH = 128
BLOCK = 512


def prefix(value, axis, combine, identity, reverse):
    length, index = (lax.axis_size(axis), lax.axis_index(axis))
    everything = lax.all_gather(value.astype(jnp.bfloat16), axis)
    start = jnp.broadcast_to(jnp.asarray(identity, value.dtype), value.shape)

    def hop(k, before):
        at = length - 1 - k if reverse else k
        reached = at > index if reverse else at < index
        new = combine(before, everything[at].astype(value.dtype))
        return jnp.where(reached, new, before)

    return lax.fori_loop(0, length, hop, start)


def add_states(earlier, later):
    return earlier + later


def per_device(layer_input, queries, keys, values, out_grad):
    tok_rows, features = queries.shape
    head_count = features // DH
    block_count = tok_rows // BLOCK
    seq_count = lax.axis_size("seq")
    scaling = 1.0 / math.sqrt(DH * tok_rows * seq_count)
    shape = (block_count, BLOCK, head_count, DH)
    query_b = queries.reshape(shape)
    key_b = keys.reshape(shape)
    value_b = values.reshape(shape)
    grad_b = out_grad.reshape(shape)
    kv_blocks = jnp.einsum("nshd,nshe->nhde", key_b, value_b, preferred_element_type=jnp.float32)
    grad_blocks = jnp.einsum("nshd,nshe->nhde", query_b, grad_b, preferred_element_type=jnp.float32)
    kv_local = jnp.sum(kv_blocks, 0)
    grad_local = jnp.sum(grad_blocks, 0)
    zero_state = jnp.zeros_like(kv_local)
    kv_prefix = prefix(kv_local, "seq", add_states, zero_state, False)
    grad_later = prefix(grad_local, "seq", add_states, zero_state, True)
    before = kv_prefix[None] + jnp.cumsum(kv_blocks, 0) - kv_blocks
    after = grad_later[None] + grad_local[None] - jnp.cumsum(grad_blocks, 0)
    before16 = before.astype(jnp.bfloat16)
    after16 = after.astype(jnp.bfloat16)
    rows_idx = lax.broadcasted_iota(jnp.int32, (BLOCK, BLOCK), 0)
    cols_idx = lax.broadcasted_iota(jnp.int32, (BLOCK, BLOCK), 1)
    lower_mask = (cols_idx <= rows_idx)[None, None]
    upper_mask = (cols_idx >= rows_idx)[None, None]
    lower = jnp.where(
        lower_mask,
        jnp.einsum("nshd,nthd->nhst", grad_b, value_b, preferred_element_type=jnp.float32),
        0.0,
    ).astype(jnp.bfloat16)
    upper = jnp.where(
        upper_mask,
        jnp.einsum("nshd,nthd->nhst", value_b, grad_b, preferred_element_type=jnp.float32),
        0.0,
    ).astype(jnp.bfloat16)
    cross = jnp.where(
        upper_mask,
        jnp.einsum("nshd,nthd->nhst", key_b, query_b, preferred_element_type=jnp.float32),
        0.0,
    ).astype(jnp.bfloat16)
    query_grad = jnp.einsum("nhst,nthd->nshd", lower, key_b, preferred_element_type=jnp.float32)
    query_grad = query_grad + jnp.einsum(
        "nshe,nhde->nshd", grad_b, before16, preferred_element_type=jnp.float32
    )
    key_grad = jnp.einsum("nhst,nthd->nshd", upper, query_b, preferred_element_type=jnp.float32)
    key_grad = key_grad + jnp.einsum(
        "nshe,nhde->nshd", value_b, after16, preferred_element_type=jnp.float32
    )
    value_grad = jnp.einsum("nhst,nthe->nshe", cross, grad_b, preferred_element_type=jnp.float32)
    value_grad = value_grad + jnp.einsum(
        "nshd,nhde->nshe", key_b, after16, preferred_element_type=jnp.float32
    )
    query_grad = (query_grad * scaling).reshape(tok_rows, features).astype(jnp.bfloat16)
    key_grad = (key_grad * scaling).reshape(tok_rows, features).astype(jnp.bfloat16)
    value_grad = (value_grad * scaling).reshape(tok_rows, features).astype(jnp.bfloat16)
    weight_scale = 1.0 / math.sqrt(tok_rows * seq_count)
    gathered = lax.all_gather(layer_input, "head", axis=1, tiled=True)
    weight_grad = lax.psum_scatter(
        (
            jnp.einsum("tc,tf->cf", gathered, value_grad, preferred_element_type=jnp.float32)
            * weight_scale
        ).astype(jnp.bfloat16),
        "seq",
        scatter_dimension=0,
        tiled=True,
    ).astype(jnp.float32)
    return (query_grad, key_grad, weight_grad)


def solution(mesh):
    return jax.shard_map(
        per_device,
        mesh=mesh,
        in_specs=(
            P("seq", "head"),
            P("seq", "head"),
            P("seq", "head"),
            P("seq", "head"),
            P("seq", "head"),
        ),
        out_specs=(P("seq", "head"), P("seq", "head"), P("seq", "head")),
        check_vma=False,
    )
```

profile of v0, /device:TPU:5, one launch (start us, length us, event | category | flops | bytes accessed | tf_op | source)
XLA Modules:
  0.0 356.4 jit_solution(12201040976996624617)
XLA Ops:
  7.2 1.4 reshape.61
  8.6 1.3 reshape.64
  10.0 1.4 fusion.58
  13.3 1.3 reshape.63
  14.6 2.0 fusion.57
  18.3 47.6 %all-gather.10.cloned.1.call-done = bf16[128,128,128]{2,1,0:T(8,128)(2,1)} async-done(((bf16[4,128,128]{2,1,0:T(8,128)(2,1)}), bf16[128,128,128]{2,1,0:T(8,128)(2,1)}) %all-gather.10.cloned.1.call-update) | async-done | bytes 4194320 | tf_op jit(solution)/shard_map/all_gather | solution.py:14
  65.9 34.2 %while.31 = (s32[]{:T(128)}, f32[4,128,128]{2,1,0:T(8,128)S(1)}, s32[]{:T(128)}, bf16[32,4,128,128]{3,2,1,0:T(8,128)(2,1)}, s32[]{:T(128)}, /*index=5*/s32[]{:T(128)}, s32[]{:T(128)}, s32[]{:T(128)}) while((s32[]{:T(128)}, f32[4,128,128]{2,1,0:T(8,128)S(1)}, s32[]{:T(128)}, bf16[32,4,128,128]{3,2,1,0:T(8,128)(2,1)}, s32[]{:T(128)}, ...), condition=%wide.region_6.7_spmd.clone, body=%wide.region_5.6_spmd.clone.sunk | while | flops 262152 | bytes 655515 | solution.py:23
  69.1 1.0 add_select_fusion.5
  70.2 1.0 add_select_fusion.5
  71.3 1.0 add_select_fusion.5
  72.3 1.0 add_select_fusion.5
  73.4 1.0 add_select_fusion.5
  74.5 1.0 add_select_fusion.5
  75.5 1.0 add_select_fusion.5
  78.7 1.1 add_select_fusion.5
  79.8 1.1 add_select_fusion.5
  80.9 1.0 add_select_fusion.5
  82.0 1.0 add_select_fusion.5
  86.2 1.0 add_select_fusion.5
  87.3 1.0 add_select_fusion.5
  88.4 1.0 add_select_fusion.5
  89.4 1.0 add_select_fusion.5
  91.6 1.0 add_select_fusion.5
  92.6 1.0 add_select_fusion.5
  95.8 1.0 add_select_fusion.5
  96.9 1.0 add_select_fusion.5
  101.1 1.2 fusion.24
  103.0 3.0 fusion.34
  106.0 5.3 %fusion.17 = bf16[2,512,4,128]{3,1,2,0:T(8,128)(2,1)} fusion(f32[2,4,128,512]{2,3,1,0:T(8,128)} %fusion.34, pred[512,512]{1,0:T(8,128)(4,1)} %iota_compare_fusion, bf16[2,512,4,128]{3,2,1,0:T(4,128)(2,1)} %copy-done.5, bf16[2,512,4,128]{3,2,1,0:T(4,128)(2,1)S(1)} %copy-done.1, bf16[2,512,4,128]{3,2,1,0:T(4,128)(2,1)S(1)} %reshape.61), kind=kOutput, calls=%fused_computation.21 | convolution fusion | flops 1079508992 | bytes 6553600 | tf_op jit(solution)/shard_map/nhst,nthe->nshe/dot_general | solution.py:79
  111.3 3.1 copy.63
  114.4 2.7 fusion.39
  117.2 83.8 %all-gather.6.cloned.1.call-done = bf16[1024,6144]{1,0:T(8,128)(2,1)} async-done(((bf16[1024,768]{1,0:T(8,128)(2,1)}), bf16[1024,6144]{1,0:T(8,128)(2,1)}) %all-gather.6.cloned.1.call-update) | async-done | bytes 12582928 | tf_op jit(solution)/shard_map/all_gather | solution.py:87
  201.0 11.7 %fusion = bf16[6144,512]{0,1:T(8,128)(2,1)} fusion(bf16[1024,6144]{1,0:T(8,128)(2,1)} %all-gather.6.cloned.1.call-done, bf16[128,8,4,128]{3,2,1,0:T(4,128)(2,1)} %bitcast.60), kind=kOutput, calls=%fused_computation.6 | convolution fusion | flops 6448742400 | bytes 19922944 | tf_op jit(solution)/shard_map/tc,tf->cf/dot_general | solution.py:90
  212.7 8.7 %copy.69 = bf16[6144,512]{1,0:T(8,128)(2,1)} copy(bf16[6144,512]{0,1:T(8,128)(2,1)} %fusion) | data formatting | bytes 12582912
  221.4 5.4 %fusion.19 = bf16[2,512,4,128]{3,1,2,0:T(8,128)(2,1)} fusion(f32[2,4,128,512]{2,3,1,0:T(8,128)} %fusion.39, pred[512,512]{1,0:T(8,128)(4,1)} %iota_compare_fusion, bf16[2,512,4,128]{3,2,1,0:T(4,128)(2,1)} %copy-done.5, bf16[2,512,4,128]{3,2,1,0:T(4,128)(2,1)S(1)} %reshape.62, bf16[2,512,4,128]{3,2,1,0:T(4,128)(2,1)S(1)} %reshape.61), kind=kOutput, calls=%fused_computation.24 | convolution fusion | flops 1079508992 | bytes 6553600 | tf_op jit(solution)/shard_map/nhst,nthd->nshd/dot_general | solution.py:75
  226.8 3.1 copy.56
  229.9 23.0 %all-gather.8.cloned.1.call-done = bf16[128,128,128]{2,1,0:T(8,128)(2,1)} async-done(((bf16[4,128,128]{2,1,0:T(8,128)(2,1)}), bf16[128,128,128]{2,1,0:T(8,128)(2,1)}) %all-gather.8.cloned.1.call-update) | async-done | bytes 4194320 | tf_op jit(solution)/shard_map/all_gather | solution.py:14
  252.9 34.2 %while.30 = (s32[]{:T(128)}, f32[4,128,128]{2,1,0:T(8,128)S(1)}, s32[]{:T(128)}, bf16[32,4,128,128]{3,2,1,0:T(8,128)(2,1)}, s32[]{:T(128)}, /*index=5*/s32[]{:T(128)}) while((s32[]{:T(128)}, f32[4,128,128]{2,1,0:T(8,128)S(1)}, s32[]{:T(128)}, bf16[32,4,128,128]{3,2,1,0:T(8,128)(2,1)}, s32[]{:T(128)}, /*index=5*/s32[]{:T(128)}) %tuple.91), condition=%wide.region_2.3_spmd.clone, body=%wide.region_1.0_spmd.clone.sunk | while | flops 262148 | bytes 655453 | solution.py:23
  266.7 1.0 add_select_fusion.4
  267.8 1.0 add_select_fusion.4
  268.8 1.0 add_select_fusion.4
  269.9 1.0 add_select_fusion.4
  271.0 1.0 add_select_fusion.4
  272.0 1.0 add_select_fusion.4
  273.1 1.0 add_select_fusion.4
  274.2 1.0 add_select_fusion.4
  275.2 1.1 add_select_fusion.4
  276.3 1.0 add_select_fusion.4
  277.4 1.0 add_select_fusion.4
  278.5 1.0 add_select_fusion.4
  279.5 1.0 add_select_fusion.4
  280.6 1.1 add_select_fusion.4
  281.7 1.0 add_select_fusion.4
  282.7 1.0 add_select_fusion.4
  283.8 1.0 add_select_fusion.4
  284.9 1.0 add_select_fusion.4
  285.9 1.0 add_select_fusion.4
  287.2 1.3 fusion.23
  288.5 1.8 fusion.50
  290.3 5.1 %fusion.21 = bf16[2,512,4,128]{3,1,2,0:T(8,128)(2,1)} fusion(f32[2,4,128,512]{2,3,1,0:T(8,128)} %fusion.50, pred[512,512]{1,0:T(8,128)(4,1)} %iota_compare_fusion.1, bf16[2,512,4,128]{3,2,1,0:T(4,128)(2,1)S(1)} %copy-done.1, bf16[2,512,4,128]{3,2,1,0:T(4,128)(2,1)S(1)} %reshape.62, bf16[2,512,4,128]{3,2,1,0:T(4,128)(2,1)S(1)} %reshape.61), kind=kOutput, calls=%fused_computation.27 | convolution fusion | flops 1079508992 | bytes 6553600 | tf_op jit(solution)/shard_map/nhst,nthd->nshd/dot_general | solution.py:71
  295.4 2.1 copy.48
  297.5 2.9 copy_bitcast_fusion
  300.4 47.5 %reduce-scatter.4.cloned.1.call-done = bf16[192,512]{1,0:T(8,128)(2,1)} async-done(((bf16[6144,512]{1,0:T(8,128)(2,1)}), bf16[192,512]{1,0:T(8,128)(2,1)}) %reduce-scatter.4.cloned.1.call-update) | async-done | bytes 196624
  347.9 1.1 copy.70
  (54 shorter events, 33.0 us)
Async XLA Ops:
  7.2 5.8 %copy-start.4 = (bf16[1024,512]{1,0:T(8,128)(2,1)S(1)}, bf16[1024,512]{1,0:T(8,128)(2,1)}, u32[]{:S(2)}) copy-start(bf16[1024,512]{1,0:T(8,128)(2,1)} %param.12) | copy-start | bytes 3145732
  7.2 58.7 %all-gather.10.cloned.1.call-start = ((), (), s32[]{:S(2)}) async-start(), calls=%async_computation.3 | async-start | bytes 4325376 | tf_op jit(solution)/shard_map/all_gather | solution.py:14
  10.0 2.9 copy-start.5
  11.4 1.5 copy-start.3
  12.1 188.9 %all-gather.6.cloned.1.call-start = ((), (), s32[]{:S(2)}) async-start(), calls=%async_computation.1 | async-start | bytes 14155776 | tf_op jit(solution)/shard_map/all_gather | solution.py:87
  12.9 240.0 %all-gather.8.cloned.1.call-start = ((), (), s32[]{:S(2)}) async-start(), calls=%async_computation.2 | async-start | bytes 4325376 | tf_op jit(solution)/shard_map/all_gather | solution.py:14
  14.6 2.1 copy-start
  16.7 331.2 %reduce-scatter.4.cloned.1.call-start = ((), (), s32[]{:S(2)}) async-start(), calls=%async_computation.4 | async-start | bytes 6488064
  101.1 4.9 %copy-start.1 = (bf16[2,512,4,128]{3,2,1,0:T(4,128)(2,1)S(1)}, bf16[2,512,4,128]{3,2,1,0:T(4,128)(2,1)}, u32[]{:S(2)}) copy-start(bf16[2,512,4,128]{3,2,1,0:T(4,128)(2,1)} %copy-done) | copy-start | bytes 3145732
  102.3 0.7 copy-start.2
Sparse Core Ops, SparseCore 0:
  12.3 53.6 all-gather.9
  67.7 133.2 all-gather.5
  203.5 49.3 all-gather.7
  256.8 91.0 reduce-scatter.3
where the time goes:
time: 361 us; the launch traced here: 356 us
  waiting for transfers between devices  203 us (56%)
  other arithmetic  72.4 us (20%)
  matrix products  38.4 us (11%)
  local copies, waits for them, and re-layouts  26.9 us (7%)
  between operations  13.9 us (4%)
    all_gather x1, waiting for transfers between devices, per_device(): gathered = lax.all_gather(layer_input, 'head', axis=1, tiled=True)  83.8 us
    all_gather x2, waiting for transfers between devices, prefix(): everything = lax.all_gather(value.astype(jnp.bfloat16), axis)  70.7 us
    select_n x64, other arithmetic, hop(): return jnp.where(reached, new, before)  66.6 us
    unnamed x5, waiting for transfers between devices  48.3 us
    dot_general x1, matrix products, per_device(): jnp.einsum('tc,tf->cf', gathered, value_grad, preferred_element_type=jnp....  11.7 us
    unnamed x15, local copies, waits for them, and re-layouts  11.3 us
  transfers between devices with their start and end apart: 4, of which 4 were waited for; matrix products, arithmetic and copies ran while one was open for 37% of the time, Pallas kernels for 0%

commit v1 on v0

v1 whole, which is shorter than its diff:
```python
import functools
import math

import jax
import jax.numpy as jnp
from jax import lax
from jax.experimental import pallas as pl
from jax.experimental.pallas import tpu as pltpu
from jax.sharding import PartitionSpec as P

DH = 128
BLOCK = 512
HALF = BLOCK // 2
NX, NY, NC = 4, 4, 2
BF16 = jnp.bfloat16
F32 = jnp.float32

NN = (((1,), (0,)), ((), ()))
NT = (((1,), (1,)), ((), ()))
TN = (((0,), (0,)), ((), ()))


def dot(a, b, dims):
    return lax.dot_general(a, b, dims, preferred_element_type=F32)


def params(mib):
    return pltpu.CompilerParams(vmem_limit_bytes=mib * 1024 * 1024)


def states_kernel(q_ref, k_ref, v_ref, o_ref, kv_ref, g_ref, tot_ref):
    kv = []
    g = []
    for b in range(2):
        rows = pl.ds(b * BLOCK, BLOCK)
        kv.append(dot(k_ref[rows, :], v_ref[rows, :], TN))
        g.append(dot(q_ref[rows, :], o_ref[rows, :], TN))
    kv_ref[0] = kv[0]
    g_ref[0] = g[1]
    tot_ref[0, 0] = (g[0] + g[1]).astype(BF16)
    tot_ref[1, 0] = (kv[0] + kv[1]).astype(BF16)


def local_states(q, k, v, o):
    heads = q.shape[1] // DH
    by_head = pl.BlockSpec((q.shape[0], DH), lambda h: (0, h))
    state = pl.BlockSpec((1, DH, DH), lambda h: (h, 0, 0))
    return pl.pallas_call(
        states_kernel,
        grid=(heads,),
        in_specs=[by_head] * 4,
        out_specs=[state, state, pl.BlockSpec((2, 1, DH, DH), lambda h: (0, h, 0, 0))],
        out_shape=[
            jax.ShapeDtypeStruct((heads, DH, DH), F32),
            jax.ShapeDtypeStruct((heads, DH, DH), F32),
            jax.ShapeDtypeStruct((2, heads, DH, DH), BF16),
        ],
        compiler_params=params(32),
        cost_estimate=pl.CostEstimate(flops=3 * 10**8, bytes_accessed=5 * 10**6, transcendentals=0),
        name="states",
    )(q, k, v, o)


def keep(s0, t0, rows, cols, upper):
    s = lax.broadcasted_iota(jnp.int32, (rows, cols), 0) + s0
    t = lax.broadcasted_iota(jnp.int32, (rows, cols), 1) + t0
    return t >= s if upper else t <= s


def upper_product(a, b, c):
    top = dot(a[:HALF], b, NT)
    top = jnp.where(keep(0, 0, HALF, BLOCK, True), top, 0.0).astype(BF16)
    low = dot(a[HALF:], b[HALF:], NT)
    low = jnp.where(keep(0, 0, HALF, HALF, True), low, 0.0).astype(BF16)
    return jnp.concatenate([dot(top, c, NN), dot(low, c[HALF:], NN)], 0)


def lower_product(a, b, c):
    top = dot(a[:HALF], b[:HALF], NT)
    top = jnp.where(keep(0, 0, HALF, HALF, False), top, 0.0).astype(BF16)
    low = dot(a[HALF:], b, NT)
    low = jnp.where(keep(HALF, 0, HALF, BLOCK, False), low, 0.0).astype(BF16)
    return jnp.concatenate([dot(top, c[:HALF], NN), dot(low, c, NN)], 0)


def value_kernel(scaling, *refs):
    ins, outs = refs[:10], refs[10:]
    for half in range(2):
        q_ref, k_ref, o_ref, later_ref, g_ref = ins[5 * half : 5 * half + 5]
        later = later_ref[0].astype(F32)
        for b in range(2):
            rows = pl.ds(b * BLOCK, BLOCK)
            k = k_ref[rows, :]
            after = (later + g_ref[0]) if b == 0 else later
            total = upper_product(k, q_ref[rows, :], o_ref[rows, :])
            total = total + dot(k, after.astype(BF16), NN)
            outs[half][rows, :] = (total * scaling).astype(BF16)


def value_gradient(q, k, o, later, g, scaling):
    rows = q.shape[0]
    specs = []
    for half in range(2):
        by_head = pl.BlockSpec((rows, DH), lambda h, half=half: (0, 2 * half + h))
        state = pl.BlockSpec((1, DH, DH), lambda h, half=half: (2 * half + h, 0, 0))
        specs += [by_head, by_head, by_head, state, state]
    out = pl.BlockSpec((rows, DH), lambda h: (0, h))
    return pl.pallas_call(
        functools.partial(value_kernel, scaling),
        grid=(2,),
        in_specs=specs,
        out_specs=[out, out],
        out_shape=[jax.ShapeDtypeStruct((rows, 2 * DH), BF16)] * 2,
        compiler_params=params(40),
        cost_estimate=pl.CostEstimate(flops=2 * 10**9, bytes_accessed=5 * 10**6, transcendentals=0),
        name="value_gradient",
    )(q, k, o, later, g, q, k, o, later, g)


def query_key_kernel(scaling, q_ref, k_ref, v_ref, o_ref, later_ref, g_ref, before_ref, kv_ref, dq_ref, dk_ref):
    later = later_ref[0].astype(F32)
    earlier = before_ref[0].astype(F32)
    for b in range(2):
        rows = pl.ds(b * BLOCK, BLOCK)
        q, k, v, o = q_ref[rows, :], k_ref[rows, :], v_ref[rows, :], o_ref[rows, :]
        after = (later + g_ref[0]) if b == 0 else later
        before = earlier if b == 0 else (earlier + kv_ref[0])
        dq = lower_product(o, v, k) + dot(o, before.astype(BF16), NT)
        dk = upper_product(v, o, q) + dot(v, after.astype(BF16), NT)
        dq_ref[rows, :] = (dq * scaling).astype(BF16)
        dk_ref[rows, :] = (dk * scaling).astype(BF16)


def query_key_gradients(q, k, v, o, later, g, before, kv, scaling):
    rows = q.shape[0]
    heads = q.shape[1] // DH
    by_head = pl.BlockSpec((rows, DH), lambda h: (0, h))
    state = pl.BlockSpec((1, DH, DH), lambda h: (h, 0, 0))
    return pl.pallas_call(
        functools.partial(query_key_kernel, scaling),
        grid=(heads,),
        in_specs=[by_head] * 4 + [state] * 4,
        out_specs=[by_head, by_head],
        out_shape=[jax.ShapeDtypeStruct(q.shape, BF16)] * 2,
        compiler_params=params(40),
        cost_estimate=pl.CostEstimate(flops=4 * 10**9, bytes_accessed=7 * 10**6, transcendentals=0),
        name="query_key_gradients",
    )(q, k, v, o, later, g, before, kv)


def terms_kernel(scale, pairs, n_x, n_v, core_ref, *refs):
    xs, vs = refs[:n_x], refs[n_x : n_x + n_v]
    mine_ref, other_ref = refs[n_x + n_v :]
    first = core_ref[0] == 0
    for at, pair in enumerate(pairs):
        for h, (x, v) in enumerate(pair):
            term = dot(xs[x][...], vs[v][...], NN) * scale
            piece = term.shape[0] // 2
            top = term[:piece].astype(BF16)
            low = term[piece:].astype(BF16)
            mine_ref[0, h, at] = jnp.where(first, top, low)
            other_ref[0, h, at] = jnp.where(first, low, top)


def weight_terms(core, xs, vs, pairs, scale):
    rows, tokens = xs[0].shape
    cols = vs[0].shape[1]
    piece = rows // 4
    n = len(pairs)
    out = jax.ShapeDtypeStruct((2, 2, n, piece, cols), BF16)
    out_spec = pl.BlockSpec((1, 2, n, piece, cols), lambda r, c: (r, 0, 0, 0, 0))
    mine, other = pl.pallas_call(
        functools.partial(terms_kernel, scale, pairs, len(xs), len(vs)),
        grid_spec=pltpu.PrefetchScalarGridSpec(
            num_scalar_prefetch=1,
            grid=(2,),
            in_specs=[pl.BlockSpec((rows // 2, tokens), lambda r, c: (r, 0))] * len(xs)
            + [pl.BlockSpec((tokens, cols), lambda r, c: (0, 0))] * len(vs),
            out_specs=[out_spec, out_spec],
        ),
        out_shape=[out, out],
        compiler_params=params(40),
        cost_estimate=pl.CostEstimate(
            flops=n * 8 * 10**8, bytes_accessed=n * 3 * 10**6, transcendentals=0
        ),
        name="weight_terms",
    )(core, *xs, *vs)
    shape = (4, n, piece, cols)
    return mine.reshape(shape), other.reshape(shape)


def seq_index(x, y, c):
    return ((x % NX) * NY + (y % NY)) * NC + c


CHIPS = [(x, y, c) for x in range(NX) for y in range(NY) for c in range(NC)]
SWAP = [(seq_index(x, y, c), seq_index(x, y, 1 - c)) for x, y, c in CHIPS]


def y_shift(d):
    return [(seq_index(x, y, c), seq_index(x, y + d, c)) for x, y, c in CHIPS]


def x_to(targets, d):
    return [(seq_index(t - d, y, c), seq_index(t, y, c)) for t in targets for y in range(NY) for c in range(NC)]


def total(parts):
    acc = parts[0].astype(F32)
    for part in parts[1:]:
        acc = acc + part.astype(F32)
    return acc.astype(BF16)


def over_core_and_y(mine, other, y):
    received = lax.ppermute(other, "seq", SWAP)

    def of(at):
        at = lax.rem(at, NY)
        pick = functools.partial(lax.dynamic_index_in_dim, axis=0, keepdims=False)
        return total([pick(mine, at), pick(received, at)])

    parts = [lax.ppermute(of(y + d), "seq", y_shift(d)) for d in (2, 1, 3)]
    return total([of(y)] + parts)


def over_x(pieces, targets, x):
    parts = []
    for d in (2, 1, 3):
        send = pieces[0]
        for t, piece in zip(targets[1:], pieces[1:]):
            send = jnp.where(x == (t - d) % NX, piece, send)
        parts.append(lax.ppermute(send, "seq", x_to(targets, d)))
    own = pieces[0]
    for t, piece in zip(targets[1:], pieces[1:]):
        own = jnp.where(x == t, piece, own)
    return total([own] + parts)


SLOTS = {
    (0, 0): (0, 0, 0),
    (0, 1): (1, -1, 0),
    (1, 0): (-1, 1, 0),
    (1, 1): (4, None, None),
    (2, 0): (2, -1, 1),
    (2, 1): (-2, 1, -1),
    (3, 0): (3, -1, 2),
    (3, 1): (-3, 1, -2),
}


def owners(flip, nz):
    pairs = []
    for x, y, c in CHIPS:
        r2, h = divmod(y, 2)
        slot = h ^ flip
        for m in range(nz):
            d, di, dj = SLOTS[(x, slot)]
            if d == 4:
                di, dj = ((1, -3), (-1, 3))[h]
            i, j = (m + di) % nz, (m + dj) % nz
            pairs.append((seq_index(x, y, c) * nz + m, (4 * i + 2 * r2 + c) * nz + j))
    return pairs


def per_device(layer_input, queries, keys, values, out_grad):
    tok_rows, features = queries.shape
    heads = features // DH
    n_seq, n_z = lax.axis_size("seq"), lax.axis_size("head")
    scaling = 1.0 / math.sqrt(DH * tok_rows * n_seq)
    weight_scale = 1.0 / math.sqrt(tok_rows * n_seq)
    s = lax.axis_index("seq")
    z = lax.axis_index("head")
    x, y, c = s // (NY * NC), lax.rem(s // NC, NY), lax.rem(s, NC)
    up = [(i, (i + 1) % n_z) for i in range(n_z)]
    down = [(i, (i - 1) % n_z) for i in range(n_z)]

    x_prev = lax.ppermute(layer_input, "head", up)
    x_next = lax.ppermute(layer_input, "head", down)

    kv0, g1, sums = local_states(queries, keys, values, out_grad)
    spread = sums.reshape(2, n_seq, heads * DH // n_seq, DH)
    gathered = lax.all_to_all(spread, "seq", 1, 1)
    at = lax.broadcasted_iota(jnp.int32, (n_seq, n_seq), 0)
    of = lax.broadcasted_iota(jnp.int32, (n_seq, n_seq), 1)
    chosen = jnp.stack([of > at, of < at]).astype(BF16)
    sums = jnp.einsum("kts,ksab->ktab", chosen, gathered, preferred_element_type=F32).astype(BF16)
    sums = lax.all_to_all(sums, "seq", 1, 1).reshape(2, heads, DH, DH)
    later, before = sums[0], sums[1]

    va, vb = value_gradient(queries, keys, out_grad, later, g1, scaling)
    ups, downs = [(va, vb)], [(va, vb)]
    for step in range(2):
        a, b = ups[-1]
        ups.append((lax.ppermute(a, "head", up), lax.ppermute(b, "head", up)))
        a, b = downs[-1]
        b = lax.ppermute(b, "head", down)
        downs.append((lax.ppermute(a, "head", down), b))
    up3 = lax.ppermute(ups[2][0], "head", up)
    down3 = lax.ppermute(downs[2][1], "head", down)

    query_grad, key_grad = query_key_gradients(
        queries, keys, values, out_grad, later, g1, before, kv0, scaling
    )

    core = c.astype(jnp.int32).reshape(1)
    xt, xt_prev, xt_next = layer_input.T, x_prev.T, x_next.T

    terms = weight_terms(
        core, [xt, xt_prev, xt_next], [va, vb], [[(i, 0), (i, 1)] for i in range(3)], weight_scale
    )
    p0 = over_core_and_y(*terms, y)
    near = [xt_prev, xt_next]
    ring = [[(0, 0), (0, 1)], [(1, 2), (1, 3)]]
    p1 = over_core_and_y(*weight_terms(core, near, [*downs[1], *ups[1]], ring, weight_scale), y)
    p2 = over_core_and_y(*weight_terms(core, near, [*downs[2], *ups[2]], ring, weight_scale), y)
    p3 = over_core_and_y(*weight_terms(core, near, [up3, down3], [[(1, 0), (0, 1)]], weight_scale), y)

    r0 = over_x([p0[:2], jnp.concatenate([p0[2:], p0[2:]], 0)], [0, 1], x)
    r1 = over_x([p1], [2], x)
    r2 = over_x([p2], [3], x)
    r3 = over_x([p3], [1], x)
    slot0 = jnp.where(x <= 1, r0[0], jnp.where(x == 2, r1[0], r2[0]))
    slot1 = jnp.where(x == 0, r0[1], jnp.where(x == 1, r3[0], jnp.where(x == 2, r1[1], r2[1])))

    h = lax.rem(y, 2)
    first = jnp.where(h == 0, slot0, slot1)
    second = jnp.where(h == 0, slot1, slot0)
    first = lax.ppermute(first, ("seq", "head"), owners(0, n_z))
    second = lax.ppermute(second, ("seq", "head"), owners(1, n_z))
    d = lax.rem(z - s // 4 + n_z, n_z)
    slot_one = (d == 1) | ((d >= 4) & (d <= 6))
    left = jnp.where(slot_one, second, first)
    right = jnp.where(slot_one, first, second)
    weight_grad = jnp.concatenate([left, right], 1).astype(F32)
    return (query_grad, key_grad, weight_grad)


def solution(mesh):
    return jax.shard_map(
        per_device,
        mesh=mesh,
        in_specs=(P("seq", "head"),) * 5,
        out_specs=(P("seq", "head"),) * 3,
        check_vma=False,
    )
```

time: 361 us -> 228 us (0.63)
  the two profiles are of different devices: /device:TPU:5 before, /device:TPU:70 now
where the time goes in v1:
time: 228 us; the launch traced here: 227 us
  starting transfers between devices  86.3 us (38%)
  waiting for transfers between devices  83.7 us (37%)
  Pallas kernels  26.8 us (12%)
  local copies, waits for them, and re-layouts  19.4 us (9%)
  other arithmetic  9.1 us (4%)
    ppermute x4, waiting for transfers between devices, per_device(): ups.append((lax.ppermute(a, 'head', up), lax.ppermute(b, 'head', up)))  38.9 us
    ppermute x12, starting transfers between devices, over_x(): parts.append(lax.ppermute(send, 'seq', x_to(targets, d)))  19.2 us
    ppermute x12, starting transfers between devices, over_core_and_y(): parts = [lax.ppermute(of(y + d), 'seq', y_shift(d)) for d in (2, 1, 3)]  18.2 us
    unnamed x61, local copies, waits for them, and re-layouts  16.2 us
    pallas_call x4, Pallas kernels, weight_terms(): pl.pallas_call(functools.partial(terms_kernel, scale, pairs, len(xs), len...  15 us
    ppermute x12, waiting for transfers between devices, over_core_and_y(): parts = [lax.ppermute(of(y + d), 'seq', y_shift(d)) for d in (2, 1, 3)]  13.4 us
    ppermute x1, starting transfers between devices, per_device(): first = lax.ppermute(first, ('seq', 'head'), owners(0, n_z))  13.1 us
    ppermute x4, starting transfers between devices, per_device(): ups.append((lax.ppermute(a, 'head', up), lax.ppermute(b, 'head', up)))  11.3 us
  transfers between devices with their start and end apart: 44, of which 17 were waited for; matrix products, arithmetic and copies ran while one was open for 5% of the time, Pallas kernels for 11%

profile of v1, /device:TPU:70, one launch (start us, length us, event | category | flops | bytes accessed | tf_op | source)
XLA Modules:
  0.0 226.9 jit_solution(7063466860923725684)
XLA Ops:
  0.6 1.2 copy-done.2
  1.9 1.2 copy-done.5
  3.1 1.2 copy-done.8
  4.3 1.2 copy-done.10
  5.5 2.2 states.1
  9.3 7.8 %all-to-all-start = ((bf16[2,32,16,128]{3,2,0,1:T(8,128)(2,1)}), bf16[2,32,16,128]{3,2,0,1:T(8,128)(2,1)S(1)}, u32[]{:S(2)}, u32[]{:S(2)}) async-start(bf16[2,32,16,128]{3,2,0,1:T(8,128)(2,1)} %copy.19), calls=%async_computation | async-start | bytes 524288 | tf_op jit(solution)/shard_map/all_to_all | solution.py:283
  17.0 7.0 %all-to-all-done = bf16[2,32,16,128]{3,2,0,1:T(8,128)(2,1)S(1)} async-done(((bf16[2,32,16,128]{3,2,0,1:T(8,128)(2,1)}), bf16[2,32,16,128]{3,2,0,1:T(8,128)(2,1)S(1)}, u32[]{:S(2)}, u32[]{:S(2)}) %all-to-all-start) | async-done | bytes 262176 | tf_op jit(solution)/shard_map/all_to_all | solution.py:283
  25.0 6.5 %all-to-all-start.1 = ((bf16[2,32,16,128]{3,2,0,1:T(8,128)(2,1)}), bf16[2,32,16,128]{3,2,0,1:T(8,128)(2,1)}, u32[]{:S(2)}, u32[]{:S(2)}) async-start(bf16[2,32,16,128]{3,2,0,1:T(8,128)(2,1)} %copy.21), calls=%async_computation.1 | async-start | bytes 524288 | tf_op jit(solution)/shard_map/all_to_all | solution.py:288
  31.5 1.6 copy.22
  33.2 1.9 collective-permute-start
  35.2 3.3 %all-to-all-done.1 = bf16[2,32,16,128]{3,2,0,1:T(8,128)(2,1)} async-done(((bf16[2,32,16,128]{3,2,0,1:T(8,128)(2,1)}), bf16[2,32,16,128]{3,2,0,1:T(8,128)(2,1)}, u32[]{:S(2)}, u32[]{:S(2)}) %all-to-all-start.1) | async-done | bytes 262176 | tf_op jit(solution)/shard_map/all_to_all | solution.py:288
  38.5 1.6 fusion.37
  40.2 1.3 copy-done.3
  41.4 1.2 copy-done.6
  42.7 1.2 copy-done.11
  43.9 3.2 %value_gradient.1 = (bf16[1024,256]{1,0:T(8,128)(2,1)S(1)}, bf16[1024,256]{1,0:T(8,128)(2,1)S(1)}) custom-call(bf16[1024,512]{1,0:T(8,128)(2,1)S(1)} %copy-done.3, bf16[1024,512]{1,0:T(8,128)(2,1)S(1)} %copy-done.6, bf16[1024,512]{1,0:T(8,128)(2,1)S(1)} %copy-done.11, bf16[4,128,128]{2,1,0:T(8,128)(2,1)S(1)} %bitcast.93, ...), custom_call_target="tpu_custom_call" | custom-call | flops 2000000000 | bytes 5000000 | tf_op jit(solution)/shard_map/value_gradient/pallas_call | solution.py:108
  47.1 2.0 collective-permute-start.9
  50.1 31.0 %collective-permute-done.9.refs_4_ = bf16[1024,256]{1,0:T(8,128)(2,1)S(1)} collective-permute-done((bf16[1024,256]{1,0:T(8,128)(2,1)S(1)}, bf16[1024,256]{1,0:T(8,128)(2,1)S(1)}, u32[]{:S(2)}, u32[]{:S(2)}) %collective-permute-start.9) | collective-permute-done | bytes 524320 | tf_op jit(solution)/shard_map/ppermute | solution.py:295
  81.1 2.6 %collective-permute-start.23 = (bf16[1024,256]{1,0:T(8,128)(2,1)S(1)}, bf16[1024,256]{1,0:T(8,128)(2,1)}, u32[]{:S(2)}, u32[]{:S(2)}) collective-permute-start(bf16[1024,256]{1,0:T(8,128)(2,1)S(1)} %get-tuple-element.24.refs_4_), channel_id=1, source_target_pairs={{0,1},{1,2},{2,3},{3,4},{4,5},{5,6},{6,7},{7,0},{8,9},{9,10},{10,1... | collective-permute-start | bytes 1572872 | tf_op jit(solution)/shard_map/ppermute | solution.py:295
  85.0 3.2 %collective-permute-start.10 = (bf16[1024,256]{1,0:T(8,128)(2,1)S(1)}, bf16[1024,256]{1,0:T(8,128)(2,1)}, u32[]{:S(2)}, u32[]{:S(2)}) collective-permute-start(bf16[1024,256]{1,0:T(8,128)(2,1)S(1)} %collective-permute-done.9.refs_4_), channel_id=1, source_target_pairs={{0,1},{1,2},{2,3},{3,4},{4,5},{5,6},{6,7},{7,0},{8,9},{9,10},{10,1... | collective-permute-start | bytes 1572872 | tf_op jit(solution)/shard_map/ppermute | solution.py:295
  89.0 6.4 %collective-permute-done.22.refs_2_ = bf16[1024,256]{1,0:T(8,128)(2,1)} collective-permute-done((bf16[1024,256]{1,0:T(8,128)(2,1)S(1)}, bf16[1024,256]{1,0:T(8,128)(2,1)}, u32[]{:S(2)}, u32[]{:S(2)}) %collective-permute-start.22) | collective-permute-done | bytes 524320 | tf_op jit(solution)/shard_map/ppermute | solution.py:298
  96.0 2.2 collective-permute-start.31
  98.3 7.4 %collective-permute-done.10.refs_4_ = bf16[1024,256]{1,0:T(8,128)(2,1)} collective-permute-done((bf16[1024,256]{1,0:T(8,128)(2,1)S(1)}, bf16[1024,256]{1,0:T(8,128)(2,1)}, u32[]{:S(2)}, u32[]{:S(2)}) %collective-permute-start.10) | collective-permute-done | bytes 524320 | tf_op jit(solution)/shard_map/ppermute | solution.py:295
  105.7 3.6 %collective-permute-start.32 = (bf16[1024,256]{1,0:T(8,128)(2,1)}, bf16[1024,256]{1,0:T(8,128)(2,1)}, u32[]{:S(2)}, u32[]{:S(2)}) collective-permute-start(bf16[1024,256]{1,0:T(8,128)(2,1)} %collective-permute-done.23.refs_5_), channel_id=1, source_target_pairs={{0,1},{1,2},{2,3},{3,4},{4,5},{5,6},{6,7},{7,0},{8,9},{9,10},{10,1... | collective-permute-start | bytes 1572872 | tf_op jit(solution)/shard_map/ppermute | solution.py:295
  109.2 2.3 %collective-permute-done.13.refs_3_ = bf16[1024,256]{1,0:T(8,128)(2,1)} collective-permute-done((bf16[1024,256]{1,0:T(8,128)(2,1)}, bf16[1024,256]{1,0:T(8,128)(2,1)}, u32[]{:S(2)}, u32[]{:S(2)}) %collective-permute-start.13) | collective-permute-done | bytes 524320 | tf_op jit(solution)/shard_map/ppermute | solution.py:297
  111.5 3.2 %collective-permute-start.11 = (bf16[1024,256]{1,0:T(8,128)(2,1)}, bf16[1024,256]{1,0:T(8,128)(2,1)S(1)}, u32[]{:S(2)}, u32[]{:S(2)}) collective-permute-start(bf16[1024,256]{1,0:T(8,128)(2,1)} %collective-permute-done.10.refs_4_), channel_id=1, source_target_pairs={{0,1},{1,2},{2,3},{3,4},{4,5},{5,6},{6,7},{7,0},{8,9},{9,10},{10,1... | collective-permute-start | bytes 1572872 | tf_op jit(solution)/shard_map/ppermute | solution.py:299
  114.8 1.0 copy-done.24
  115.8 4.1 %weight_terms.6 = (bf16[2,2,2,192,256]{4,3,2,1,0:T(8,128)(2,1)S(1)}, bf16[2,2,2,192,256]{4,3,2,1,0:T(8,128)(2,1)}) custom-call(s32[1]{0:T(128)} %bitcast.5.core_ref, bf16[768,1024]{1,0:T(8,128)(2,1)S(1)} %bitcast.75, bf16[768,1024]{1,0:T(8,128)(2,1)S(1)} %bitcast.79, bf16[1024,256]{1,0:T(8,128)(2,1)} %collective-permute-done.22.refs_2_, ...), custom_call_target="tpu_custom_call" | custom-call | flops 1600000000 | bytes 6000000 | tf_op jit(solution)/shard_map/weight_terms/pallas_call | solution.py:172
  119.9 0.9 copy-done.15
  120.8 2.0 collective-permute-done.31.refs_2_
  122.8 4.3 %weight_terms.7 = (bf16[2,2,2,192,256]{4,3,2,1,0:T(8,128)(2,1)S(1)}, bf16[2,2,2,192,256]{4,3,2,1,0:T(8,128)(2,1)}) custom-call(s32[1]{0:T(128)} %bitcast.5.core_ref, bf16[768,1024]{1,0:T(8,128)(2,1)S(1)} %bitcast.76, bf16[768,1024]{1,0:T(8,128)(2,1)S(1)} %bitcast.80, bf16[1024,256]{1,0:T(8,128)(2,1)} %collective-permute-done.31.refs_2_, ...), custom_call_target="tpu_custom_call" | custom-call | flops 1600000000 | bytes 6000000 | tf_op jit(solution)/shard_map/weight_terms/pallas_call | solution.py:172
  127.0 0.9 copy-done.13
  127.9 4.8 %weight_terms.4 = (bf16[2,2,3,192,256]{4,3,2,1,0:T(8,128)(2,1)S(1)}, bf16[2,2,3,192,256]{4,3,2,1,0:T(8,128)(2,1)}) custom-call(s32[1]{0:T(128)} %bitcast.5.core_ref, bf16[768,1024]{1,0:T(8,128)(2,1)} %bitcast.6.refs_0_, bf16[768,1024]{1,0:T(8,128)(2,1)S(1)} %bitcast.77, bf16[768,1024]{1,0:T(8,128)(2,1)S(1)} %bitcast.81, bf16[1024,256]{1,0:T(8,128)(2,1)S(1)} %copy-done.20, ...), custom_call_target="tpu_custom_call" | custom-call | flops 2400000000 | bytes 9000000 | tf_op jit(solution)/shard_map/weight_terms/pallas_call | solution.py:172
  133.2 1.9 weight_terms.5
  135.2 1.6 fusion.15
  136.7 3.1 %collective-permute-start.25 = (bf16[2,192,256]{2,1,0:T(8,128)(2,1)S(1)}, bf16[2,192,256]{2,1,0:T(8,128)(2,1)S(1)}, u32[]{:S(2)}, u32[]{:S(2)}) collective-permute-start(bf16[2,192,256]{2,1,0:T(8,128)(2,1)S(1)} %get-tuple-element.39), channel_id=1, source_target_pairs={{0,32},{8,40},{16,48},{24,56},{32,0},{40,8},{48,16},{56,24},{64,96... | collective-permute-start | bytes 589832 | tf_op jit(solution)/shard_map/ppermute | solution.py:223
  140.4 2.7 %collective-permute-start.27 = (bf16[2,192,256]{2,1,0:T(8,128)(2,1)S(1)}, bf16[2,192,256]{2,1,0:T(8,128)(2,1)S(1)}, u32[]{:S(2)}, u32[]{:S(2)}) collective-permute-start(bf16[2,192,256]{2,1,0:T(8,128)(2,1)S(1)} %get-tuple-element.40), channel_id=1, source_target_pairs={{0,48},{8,56},{16,0},{24,8},{32,16},{40,24},{48,32},{56,40},{64,11... | collective-permute-start | bytes 589832 | tf_op jit(solution)/shard_map/ppermute | solution.py:223
  143.1 1.3 fusion.19
  144.5 1.5 collective-permute-done.25
  146.0 1.5 collective-permute-start.35
  147.6 2.8 %collective-permute-done.26 = bf16[2,192,256]{2,1,0:T(8,128)(2,1)S(1)} collective-permute-done((bf16[2,192,256]{2,1,0:T(8,128)(2,1)S(1)}, bf16[2,192,256]{2,1,0:T(8,128)(2,1)S(1)}, u32[]{:S(2)}, u32[]{:S(2)}) %collective-permute-start.26) | collective-permute-done | bytes 196640 | tf_op jit(solution)/shard_map/ppermute | solution.py:223
  150.8 3.0 %collective-permute-start.16 = (bf16[1,192,256]{2,1,0:T(8,128)(2,1)S(1)}, bf16[1,192,256]{2,1,0:T(8,128)(2,1)S(1)}, u32[]{:S(2)}, u32[]{:S(2)}) collective-permute-start(bf16[1,192,256]{2,1,0:T(8,128)(2,1)S(1)} %get-tuple-element.45), channel_id=1, source_target_pairs={{0,32},{8,40},{16,48},{24,56},{32,0},{40,8},{48,16},{56,24},{64,96... | collective-permute-start | bytes 294920 | tf_op jit(solution)/shard_map/ppermute | solution.py:223
  153.9 1.1 fusion.8
  155.0 1.0 collective-permute-start.17
  156.0 3.9 %collective-permute-done.35 = bf16[2,192,256]{2,1,0:T(8,128)(2,1)S(1)} collective-permute-done((bf16[2,192,256]{2,1,0:T(8,128)(2,1)S(1)}, bf16[2,192,256]{2,1,0:T(8,128)(2,1)S(1)}, u32[]{:S(2)}, u32[]{:S(2)}) %collective-permute-start.35) | collective-permute-done | bytes 196640 | tf_op jit(solution)/shard_map/ppermute | solution.py:223
  160.5 1.1 fusion.5
  162.3 1.4 fusion.10
  163.7 4.0 %collective-permute-start.30 = (bf16[2,192,256]{2,1,0:T(8,128)(2,1)S(1)}, bf16[2,192,256]{2,1,0:T(8,128)(2,1)S(1)}, u32[]{:S(2)}, u32[]{:S(2)}) collective-permute-start(bf16[2,192,256]{2,1,0:T(8,128)(2,1)S(1)} %fusion.8), channel_id=1, source_target_pairs={{192,128},{200,136},{208,144},{216,152},{224,160},{232,168},{240,1... | collective-permute-start | bytes 589832 | tf_op jit(solution)/shard_map/ppermute | solution.py:233
  167.7 2.6 %collective-permute-start.3 = (bf16[3,192,256]{2,1,0:T(8,128)(2,1)S(1)}, bf16[3,192,256]{2,1,0:T(8,128)(2,1)S(1)}, u32[]{:S(2)}, u32[]{:S(2)}) collective-permute-start(bf16[3,192,256]{2,1,0:T(8,128)(2,1)S(1)} %get-tuple-element.36), channel_id=1, source_target_pairs={{0,32},{8,40},{16,48},{24,56},{32,0},{40,8},{48,16},{56,24},{64,96... | collective-permute-start | bytes 884744 | tf_op jit(solution)/shard_map/ppermute | solution.py:223
  170.4 3.1 %collective-permute-start.5 = (bf16[3,192,256]{2,1,0:T(8,128)(2,1)S(1)}, bf16[3,192,256]{2,1,0:T(8,128)(2,1)S(1)}, u32[]{:S(2)}, u32[]{:S(2)}) collective-permute-start(bf16[3,192,256]{2,1,0:T(8,128)(2,1)S(1)} %get-tuple-element.37), channel_id=1, source_target_pairs={{0,48},{8,56},{16,0},{24,8},{32,16},{40,24},{48,32},{56,40},{64,11... | collective-permute-start | bytes 884744 | tf_op jit(solution)/shard_map/ppermute | solution.py:223
  173.6 1.3 collective-permute-start.37
  174.9 1.3 collective-permute-start.38
  176.3 2.9 %collective-permute-done.3 = bf16[3,192,256]{2,1,0:T(8,128)(2,1)S(1)} collective-permute-done((bf16[3,192,256]{2,1,0:T(8,128)(2,1)S(1)}, bf16[3,192,256]{2,1,0:T(8,128)(2,1)S(1)}, u32[]{:S(2)}, u32[]{:S(2)}) %collective-permute-start.3) | collective-permute-done | bytes 294944 | tf_op jit(solution)/shard_map/ppermute | solution.py:223
  179.2 1.3 collective-permute-start.39
  180.5 2.3 %collective-permute-done.4 = bf16[3,192,256]{2,1,0:T(8,128)(2,1)S(1)} collective-permute-done((bf16[3,192,256]{2,1,0:T(8,128)(2,1)S(1)}, bf16[3,192,256]{2,1,0:T(8,128)(2,1)S(1)}, u32[]{:S(2)}, u32[]{:S(2)}) %collective-permute-start.4) | collective-permute-done | bytes 294944 | tf_op jit(solution)/shard_map/ppermute | solution.py:223
  182.8 3.3 %collective-permute-start.19 = (bf16[1,192,256]{2,1,0:T(8,128)(2,1)S(1)}, bf16[1,192,256]{2,1,0:T(8,128)(2,1)S(1)}, u32[]{:S(2)}, u32[]{:S(2)}) collective-permute-start(bf16[1,192,256]{2,1,0:T(8,128)(2,1)S(1)} %fusion.24), channel_id=1, source_target_pairs={{192,64},{200,72},{208,80},{216,88},{224,96},{232,104},{240,112},{... | collective-permute-start | bytes 294920 | tf_op jit(solution)/shard_map/ppermute | solution.py:233
  186.8 1.2 fusion.2
  188.1 2.1 collective-permute-start.6
  190.2 2.5 %collective-permute-start.7 = (bf16[2,192,256]{2,1,0:T(8,128)(2,1)S(1)}, bf16[2,192,256]{2,1,0:T(8,128)(2,1)S(1)}, u32[]{:S(2)}, u32[]{:S(2)}) collective-permute-start(bf16[2,192,256]{2,1,0:T(8,128)(2,1)S(1)} %get-tuple-element.49), channel_id=1, source_target_pairs={{192,0},{200,8},{208,16},{216,24},{224,32},{232,40},{240,48},{248,... | collective-permute-start | bytes 589832 | tf_op jit(solution)/shard_map/ppermute | solution.py:233
  194.7 4.6 %collective-permute-done.7 = bf16[2,192,256]{2,1,0:T(8,128)(2,1)S(1)} collective-permute-done((bf16[2,192,256]{2,1,0:T(8,128)(2,1)S(1)}, bf16[2,192,256]{2,1,0:T(8,128)(2,1)S(1)}, u32[]{:S(2)}, u32[]{:S(2)}) %collective-permute-start.7) | collective-permute-done | bytes 196640 | tf_op jit(solution)/shard_map/ppermute | solution.py:233
  199.7 13.1 %collective-permute-start.41 = (bf16[192,256]{1,0:T(8,128)(2,1)S(1)}, bf16[192,256]{1,0:T(8,128)(2,1)S(1)}, u32[]{:S(2)}, u32[]{:S(2)}) collective-permute-start(bf16[192,256]{1,0:T(8,128)(2,1)S(1)} %select_bitcast_fusion), channel_id=1, source_target_pairs={{0,0},{1,33},{2,66},{3,99},{4,132},{5,165},{6,198},{7,231},{8,8},{... | collective-permute-start | bytes 294920 | tf_op jit(solution)/shard_map/ppermute | solution.py:329
  212.8 2.1 collective-permute-start.40
  214.9 6.4 %query_key_gradients.1 = (bf16[1024,512]{1,0:T(8,128)(2,1)}, bf16[1024,512]{1,0:T(8,128)(2,1)}) custom-call(bf16[1024,512]{1,0:T(8,128)(2,1)S(1)} %copy-done.4, bf16[1024,512]{1,0:T(8,128)(2,1)S(1)} %copy-done.7, bf16[1024,512]{1,0:T(8,128)(2,1)S(1)} %copy-done.9, bf16[1024,512]{1,0:T(8,128)(2,1)S(1)} %copy-done.12, bf16[4,128,128]{2,1,0:T(8,128)(2,1)S(1)} %bitcast.95, ...), custom_call_target="tpu_custom_call" | custom-call | flops 4000000000 | bytes 7000000 | tf_op jit(solution)/shard_map/query_key_gradients/pallas_call | solution.py:139
  221.3 4.7 %collective-permute-done.40 = bf16[192,256]{1,0:T(8,128)(2,1)S(1)} collective-permute-done((bf16[192,256]{1,0:T(8,128)(2,1)S(1)}, bf16[192,256]{1,0:T(8,128)(2,1)S(1)}, u32[]{:S(2)}, u32[]{:S(2)}) %collective-permute-start.40) | collective-permute-done | bytes 98336 | tf_op jit(solution)/shard_map/ppermute | solution.py:330
  (114 shorter events, 13.7 us)
Async XLA Ops:
  0.6 1.2 copy-start.2
  1.9 1.2 copy-start.5
  3.1 1.2 copy-start.8
  8.5 31.7 %copy-start.27 = (f32[4,128,128]{2,1,0:T(8,128)}, f32[4,128,128]{2,1,0:T(8,128)S(1)}, u32[]{:S(2)}) copy-start(f32[4,128,128]{2,1,0:T(8,128)S(1)} %get-tuple-element.19.g_ref.refs_4_.refs_9_) | copy-start | bytes 786436
  9.3 22.3 %copy-start.29 = (bf16[1024,768]{1,0:T(8,128)(2,1)S(1)}, bf16[1024,768]{1,0:T(8,128)(2,1)}, u32[]{:S(2)}) copy-start(bf16[1024,768]{1,0:T(8,128)(2,1)} %param.5) | copy-start | bytes 4718596
  9.3 14.8 %all-to-all-start = ((bf16[2,32,16,128]{3,2,0,1:T(8,128)(2,1)}), bf16[2,32,16,128]{3,2,0,1:T(8,128)(2,1)S(1)}, u32[]{:S(2)}, u32[]{:S(2)}) async-start(bf16[2,32,16,128]{3,2,0,1:T(8,128)(2,1)} %copy.19), calls=%async_computation | async-start | bytes 524288 | tf_op jit(solution)/shard_map/all_to_all | solution.py:283
  25.0 13.5 %all-to-all-start.1 = ((bf16[2,32,16,128]{3,2,0,1:T(8,128)(2,1)}), bf16[2,32,16,128]{3,2,0,1:T(8,128)(2,1)}, u32[]{:S(2)}, u32[]{:S(2)}) async-start(bf16[2,32,16,128]{3,2,0,1:T(8,128)(2,1)} %copy.21), calls=%async_computation.1 | async-start | bytes 524288 | tf_op jit(solution)/shard_map/all_to_all | solution.py:288
  33.2 81.6 %collective-permute-start = (bf16[1024,768]{0,1:T(8,128)(2,1)}, bf16[1024,768]{0,1:T(8,128)(2,1)S(1)}, u32[]{:S(2)}, u32[]{:S(2)}) collective-permute-start(bf16[1024,768]{0,1:T(8,128)(2,1)} %copy.22), channel_id=1, source_target_pairs={{0,1},{1,2},{2,3},{3,4},{4,5},{5,6},{6,7},{7,0},{8,9},{9,10},{10,1... | collective-permute-start | bytes 4718600 | tf_op jit(solution)/shard_map/ppermute | solution.py:278
  35.1 79.7 %collective-permute-start.1 = (bf16[1024,768]{0,1:T(8,128)(2,1)}, bf16[1024,768]{0,1:T(8,128)(2,1)S(1)}, u32[]{:S(2)}, u32[]{:S(2)}) collective-permute-start(bf16[1024,768]{0,1:T(8,128)(2,1)} %copy.22), channel_id=1, source_target_pairs={{0,7},{1,0},{2,1},{3,2},{4,3},{5,4},{6,5},{7,6},{8,15},{9,8},{10,9... | collective-permute-start | bytes 4718600 | tf_op jit(solution)/shard_map/ppermute | solution.py:279
  40.2 6.9 %copy-start.17 = (bf16[1,32,16,128]{3,2,0,1:T(8,128)(2,1)}, bf16[1,32,16,128]{3,2,0,1:T(8,128)(2,1)S(1)}, u32[]{:S(2)}) copy-start(bf16[1,32,16,128]{3,2,0,1:T(8,128)(2,1)S(1)} %get-tuple-element.52) | copy-start | bytes 393220
  40.2 1.3 copy-start.3
  47.1 34.0 %collective-permute-start.9 = (bf16[1024,256]{1,0:T(8,128)(2,1)S(1)}, bf16[1024,256]{1,0:T(8,128)(2,1)S(1)}, u32[]{:S(2)}, u32[]{:S(2)}) collective-permute-start(bf16[1024,256]{1,0:T(8,128)(2,1)S(1)} %get-tuple-element.23.refs_3_), channel_id=1, source_target_pairs={{0,1},{1,2},{2,3},{3,4},{4,5},{5,6},{6,7},{7,0},{8,9},{9,10},{10,1... | collective-permute-start | bytes 1572872 | tf_op jit(solution)/shard_map/ppermute | solution.py:295
  49.1 35.9 %collective-permute-start.12 = (bf16[1024,256]{1,0:T(8,128)(2,1)S(1)}, bf16[1024,256]{1,0:T(8,128)(2,1)}, u32[]{:S(2)}, u32[]{:S(2)}) collective-permute-start(bf16[1024,256]{1,0:T(8,128)(2,1)S(1)} %get-tuple-element.24.refs_4_), channel_id=1, source_target_pairs={{0,7},{1,0},{2,1},{3,2},{4,3},{5,4},{6,5},{7,6},{8,15},{9,8},{10,9... | collective-permute-start | bytes 1572872 | tf_op jit(solution)/shard_map/ppermute | solution.py:297
  49.2 46.2 %collective-permute-start.22 = (bf16[1024,256]{1,0:T(8,128)(2,1)S(1)}, bf16[1024,256]{1,0:T(8,128)(2,1)}, u32[]{:S(2)}, u32[]{:S(2)}) collective-permute-start(bf16[1024,256]{1,0:T(8,128)(2,1)S(1)} %get-tuple-element.23.refs_3_), channel_id=1, source_target_pairs={{0,7},{1,0},{2,1},{3,2},{4,3},{5,4},{6,5},{7,6},{8,15},{9,8},{10,9... | collective-permute-start | bytes 1572872 | tf_op jit(solution)/shard_map/ppermute | solution.py:298
  81.1 15.0 %collective-permute-start.23 = (bf16[1024,256]{1,0:T(8,128)(2,1)S(1)}, bf16[1024,256]{1,0:T(8,128)(2,1)}, u32[]{:S(2)}, u32[]{:S(2)}) collective-permute-start(bf16[1024,256]{1,0:T(8,128)(2,1)S(1)} %get-tuple-element.24.refs_4_), channel_id=1, source_target_pairs={{0,1},{1,2},{2,3},{3,4},{4,5},{5,6},{6,7},{7,0},{8,9},{9,10},{10,1... | collective-permute-start | bytes 1572872 | tf_op jit(solution)/shard_map/ppermute | solution.py:295
  85.0 20.7 %collective-permute-start.10 = (bf16[1024,256]{1,0:T(8,128)(2,1)S(1)}, bf16[1024,256]{1,0:T(8,128)(2,1)}, u32[]{:S(2)}, u32[]{:S(2)}) collective-permute-start(bf16[1024,256]{1,0:T(8,128)(2,1)S(1)} %collective-permute-done.9.refs_4_), channel_id=1, source_target_pairs={{0,1},{1,2},{2,3},{3,4},{4,5},{5,6},{6,7},{7,0},{8,9},{9,10},{10,1... | collective-permute-start | bytes 1572872 | tf_op jit(solution)/shard_map/ppermute | solution.py:295
  95.4 16.1 %collective-permute-start.13 = (bf16[1024,256]{1,0:T(8,128)(2,1)}, bf16[1024,256]{1,0:T(8,128)(2,1)}, u32[]{:S(2)}, u32[]{:S(2)}) collective-permute-start(bf16[1024,256]{1,0:T(8,128)(2,1)} %collective-permute-done.12.refs_3_), channel_id=1, source_target_pairs={{0,7},{1,0},{2,1},{3,2},{4,3},{5,4},{6,5},{7,6},{8,15},{9,8},{10,9... | collective-permute-start | bytes 1572872 | tf_op jit(solution)/shard_map/ppermute | solution.py:297
  96.0 26.7 %collective-permute-start.31 = (bf16[1024,256]{1,0:T(8,128)(2,1)}, bf16[1024,256]{1,0:T(8,128)(2,1)}, u32[]{:S(2)}, u32[]{:S(2)}) collective-permute-start(bf16[1024,256]{1,0:T(8,128)(2,1)} %collective-permute-done.22.refs_2_), channel_id=1, source_target_pairs={{0,7},{1,0},{2,1},{3,2},{4,3},{5,4},{6,5},{7,6},{8,15},{9,8},{10,9... | collective-permute-start | bytes 1572872 | tf_op jit(solution)/shard_map/ppermute | solution.py:298
  105.7 17.1 %collective-permute-start.32 = (bf16[1024,256]{1,0:T(8,128)(2,1)}, bf16[1024,256]{1,0:T(8,128)(2,1)}, u32[]{:S(2)}, u32[]{:S(2)}) collective-permute-start(bf16[1024,256]{1,0:T(8,128)(2,1)} %collective-permute-done.23.refs_5_), channel_id=1, source_target_pairs={{0,1},{1,2},{2,3},{3,4},{4,5},{5,6},{6,7},{7,0},{8,9},{9,10},{10,1... | collective-permute-start | bytes 1572872 | tf_op jit(solution)/shard_map/ppermute | solution.py:295
  111.5 21.7 %collective-permute-start.11 = (bf16[1024,256]{1,0:T(8,128)(2,1)}, bf16[1024,256]{1,0:T(8,128)(2,1)S(1)}, u32[]{:S(2)}, u32[]{:S(2)}) collective-permute-start(bf16[1024,256]{1,0:T(8,128)(2,1)} %collective-permute-done.10.refs_4_), channel_id=1, source_target_pairs={{0,1},{1,2},{2,3},{3,4},{4,5},{5,6},{6,7},{7,0},{8,9},{9,10},{10,1... | collective-permute-start | bytes 1572872 | tf_op jit(solution)/shard_map/ppermute | solution.py:299
  114.8 18.4 %collective-permute-start.14 = (bf16[1024,256]{1,0:T(8,128)(2,1)}, bf16[1024,256]{1,0:T(8,128)(2,1)S(1)}, u32[]{:S(2)}, u32[]{:S(2)}) collective-permute-start(bf16[1024,256]{1,0:T(8,128)(2,1)} %collective-permute-done.13.refs_3_), channel_id=1, source_target_pairs={{0,7},{1,0},{2,1},{3,2},{4,3},{5,4},{6,5},{7,6},{8,15},{9,8},{10,9... | collective-permute-start | bytes 1572872 | tf_op jit(solution)/shard_map/ppermute | solution.py:300
  120.8 7.1 %copy-start.20 = (bf16[1024,256]{1,0:T(8,128)(2,1)S(1)}, bf16[1024,256]{1,0:T(8,128)(2,1)}, u32[]{:S(2)}) copy-start(bf16[1024,256]{1,0:T(8,128)(2,1)} %copy-done.19) | copy-start | bytes 1572868
  120.8 7.1 %copy-start.22 = (bf16[1024,256]{1,0:T(8,128)(2,1)S(1)}, bf16[1024,256]{1,0:T(8,128)(2,1)}, u32[]{:S(2)}) copy-start(bf16[1024,256]{1,0:T(8,128)(2,1)} %copy-done.21) | copy-start | bytes 1572868
  120.8 14.4 %collective-permute-start.24 = (bf16[4,2,192,256]{3,2,1,0:T(8,128)(2,1)}, bf16[4,2,192,256]{3,2,1,0:T(8,128)(2,1)}, u32[]{:S(2)}, u32[]{:S(2)}) collective-permute-start(bf16[4,2,192,256]{3,2,1,0:T(8,128)(2,1)} %bitcast.27), channel_id=1, source_target_pairs={{0,8},{8,0},{16,24},{24,16},{32,40},{40,32},{48,56},{56,48},{64,72... | collective-permute-start | bytes 2359304 | tf_op jit(solution)/shard_map/ppermute | solution.py:216
  127.9 12.5 %collective-permute-start.33 = (bf16[4,2,192,256]{3,2,1,0:T(8,128)(2,1)}, bf16[4,2,192,256]{3,2,1,0:T(8,128)(2,1)}, u32[]{:S(2)}, u32[]{:S(2)}) collective-permute-start(bf16[4,2,192,256]{3,2,1,0:T(8,128)(2,1)} %bitcast.33), channel_id=1, source_target_pairs={{0,8},{8,0},{16,24},{24,16},{32,40},{40,32},{48,56},{56,48},{64,72... | collective-permute-start | bytes 2359304 | tf_op jit(solution)/shard_map/ppermute | solution.py:216
  132.7 2.4 %copy-start = (bf16[2,2,3,192,256]{4,3,2,1,0:T(8,128)(2,1)}, bf16[2,2,3,192,256]{4,3,2,1,0:T(8,128)(2,1)S(1)}, u32[]{:S(2)}) copy-start(bf16[2,2,3,192,256]{4,3,2,1,0:T(8,128)(2,1)S(1)} %get-tuple-element.25) | copy-start | bytes 3538948
  132.7 28.9 %collective-permute-start.2 = (bf16[4,3,192,256]{3,2,1,0:T(8,128)(2,1)}, bf16[4,3,192,256]{3,2,1,0:T(8,128)(2,1)}, u32[]{:S(2)}, u32[]{:S(2)}) collective-permute-start(bf16[4,3,192,256]{3,2,1,0:T(8,128)(2,1)} %bitcast.10), channel_id=1, source_target_pairs={{0,8},{8,0},{16,24},{24,16},{32,40},{40,32},{48,56},{56,48},{64,72... | collective-permute-start | bytes 3538952 | tf_op jit(solution)/shard_map/ppermute | solution.py:216
  135.0 8.0 %copy-start.14 = (bf16[2,2,2,192,256]{4,3,2,1,0:T(8,128)(2,1)S(1)}, bf16[2,2,2,192,256]{4,3,2,1,0:T(8,128)(2,1)}, u32[]{:S(2)}) copy-start(bf16[2,2,2,192,256]{4,3,2,1,0:T(8,128)(2,1)} %copy-done.13) | copy-start | bytes 2359300
  135.0 9.3 %collective-permute-start.15 = (bf16[4,1,192,256]{3,2,1,0:T(8,128)(2,1)}, bf16[4,1,192,256]{3,2,1,0:T(8,128)(2,1)S(1)}, u32[]{:S(2)}, u32[]{:S(2)}) collective-permute-start(bf16[4,1,192,256]{3,2,1,0:T(8,128)(2,1)} %bitcast.18), channel_id=1, source_target_pairs={{0,8},{8,0},{16,24},{24,16},{32,40},{40,32},{48,56},{56,48},{64,72... | collective-permute-start | bytes 1179656 | tf_op jit(solution)/shard_map/ppermute | solution.py:216
  136.7 9.3 %collective-permute-start.25 = (bf16[2,192,256]{2,1,0:T(8,128)(2,1)S(1)}, bf16[2,192,256]{2,1,0:T(8,128)(2,1)S(1)}, u32[]{:S(2)}, u32[]{:S(2)}) collective-permute-start(bf16[2,192,256]{2,1,0:T(8,128)(2,1)S(1)} %get-tuple-element.39), channel_id=1, source_target_pairs={{0,32},{8,40},{16,48},{24,56},{32,0},{40,8},{48,16},{56,24},{64,96... | collective-permute-start | bytes 589832 | tf_op jit(solution)/shard_map/ppermute | solution.py:223
  139.8 10.5 %collective-permute-start.26 = (bf16[2,192,256]{2,1,0:T(8,128)(2,1)S(1)}, bf16[2,192,256]{2,1,0:T(8,128)(2,1)S(1)}, u32[]{:S(2)}, u32[]{:S(2)}) collective-permute-start(bf16[2,192,256]{2,1,0:T(8,128)(2,1)S(1)} %get-tuple-element.41), channel_id=1, source_target_pairs={{0,16},{8,24},{16,32},{24,40},{32,48},{40,56},{48,0},{56,8},{64,80... | collective-permute-start | bytes 589832 | tf_op jit(solution)/shard_map/ppermute | solution.py:223
  140.4 10.4 %collective-permute-start.27 = (bf16[2,192,256]{2,1,0:T(8,128)(2,1)S(1)}, bf16[2,192,256]{2,1,0:T(8,128)(2,1)S(1)}, u32[]{:S(2)}, u32[]{:S(2)}) collective-permute-start(bf16[2,192,256]{2,1,0:T(8,128)(2,1)S(1)} %get-tuple-element.40), channel_id=1, source_target_pairs={{0,48},{8,56},{16,0},{24,8},{32,16},{40,24},{48,32},{56,40},{64,11... | collective-permute-start | bytes 589832 | tf_op jit(solution)/shard_map/ppermute | solution.py:223
  144.3 10.7 %collective-permute-start.34 = (bf16[2,192,256]{2,1,0:T(8,128)(2,1)S(1)}, bf16[2,192,256]{2,1,0:T(8,128)(2,1)S(1)}, u32[]{:S(2)}, u32[]{:S(2)}) collective-permute-start(bf16[2,192,256]{2,1,0:T(8,128)(2,1)S(1)} %get-tuple-element.42), channel_id=1, source_target_pairs={{0,32},{8,40},{16,48},{24,56},{32,0},{40,8},{48,16},{56,24},{64,96... | collective-permute-start | bytes 589832 | tf_op jit(solution)/shard_map/ppermute | solution.py:223
  146.0 13.8 %collective-permute-start.35 = (bf16[2,192,256]{2,1,0:T(8,128)(2,1)S(1)}, bf16[2,192,256]{2,1,0:T(8,128)(2,1)S(1)}, u32[]{:S(2)}, u32[]{:S(2)}) collective-permute-start(bf16[2,192,256]{2,1,0:T(8,128)(2,1)S(1)} %get-tuple-element.44), channel_id=1, source_target_pairs={{0,16},{8,24},{16,32},{24,40},{32,48},{40,56},{48,0},{56,8},{64,80... | collective-permute-start | bytes 589832 | tf_op jit(solution)/shard_map/ppermute | solution.py:223
  150.4 9.5 %collective-permute-start.36 = (bf16[2,192,256]{2,1,0:T(8,128)(2,1)S(1)}, bf16[2,192,256]{2,1,0:T(8,128)(2,1)S(1)}, u32[]{:S(2)}, u32[]{:S(2)}) collective-permute-start(bf16[2,192,256]{2,1,0:T(8,128)(2,1)S(1)} %get-tuple-element.43), channel_id=1, source_target_pairs={{0,48},{8,56},{16,0},{24,8},{32,16},{40,24},{48,32},{56,40},{64,11... | collective-permute-start | bytes 589832 | tf_op jit(solution)/shard_map/ppermute | solution.py:223
  150.8 11.5 %copy-start.1 = (bf16[2,2,3,192,256]{4,3,2,1,0:T(8,128)(2,1)S(1)}, bf16[2,2,3,192,256]{4,3,2,1,0:T(8,128)(2,1)}, u32[]{:S(2)}) copy-start(bf16[2,2,3,192,256]{4,3,2,1,0:T(8,128)(2,1)} %copy-done) | copy-start | bytes 3538948
  150.8 12.8 %collective-permute-start.16 = (bf16[1,192,256]{2,1,0:T(8,128)(2,1)S(1)}, bf16[1,192,256]{2,1,0:T(8,128)(2,1)S(1)}, u32[]{:S(2)}, u32[]{:S(2)}) collective-permute-start(bf16[1,192,256]{2,1,0:T(8,128)(2,1)S(1)} %get-tuple-element.45), channel_id=1, source_target_pairs={{0,32},{8,40},{16,48},{24,56},{32,0},{40,8},{48,16},{56,24},{64,96... | collective-permute-start | bytes 294920 | tf_op jit(solution)/shard_map/ppermute | solution.py:223
  155.0 12.6 %collective-permute-start.17 = (bf16[1,192,256]{2,1,0:T(8,128)(2,1)S(1)}, bf16[1,192,256]{2,1,0:T(8,128)(2,1)S(1)}, u32[]{:S(2)}, u32[]{:S(2)}) collective-permute-start(bf16[1,192,256]{2,1,0:T(8,128)(2,1)S(1)} %get-tuple-element.47), channel_id=1, source_target_pairs={{0,16},{8,24},{16,32},{24,40},{32,48},{40,56},{48,0},{56,8},{64,80... | collective-permute-start | bytes 294920 | tf_op jit(solution)/shard_map/ppermute | solution.py:223
  159.8 10.4 %collective-permute-start.18 = (bf16[1,192,256]{2,1,0:T(8,128)(2,1)S(1)}, bf16[1,192,256]{2,1,0:T(8,128)(2,1)S(1)}, u32[]{:S(2)}, u32[]{:S(2)}) collective-permute-start(bf16[1,192,256]{2,1,0:T(8,128)(2,1)S(1)} %get-tuple-element.46), channel_id=1, source_target_pairs={{0,48},{8,56},{16,0},{24,8},{32,16},{40,24},{48,32},{56,40},{64,11... | collective-permute-start | bytes 294920 | tf_op jit(solution)/shard_map/ppermute | solution.py:223
  159.9 10.5 %collective-permute-start.28 = (bf16[2,192,256]{2,1,0:T(8,128)(2,1)S(1)}, bf16[2,192,256]{2,1,0:T(8,128)(2,1)S(1)}, u32[]{:S(2)}, u32[]{:S(2)}) collective-permute-start(bf16[2,192,256]{2,1,0:T(8,128)(2,1)S(1)} %fusion.8), channel_id=1, source_target_pairs={{0,128},{8,136},{16,144},{24,152},{32,160},{40,168},{48,176},{56,1... | collective-permute-start | bytes 589832 | tf_op jit(solution)/shard_map/ppermute | solution.py:233
  161.6 11.9 %collective-permute-start.29 = (bf16[2,192,256]{2,1,0:T(8,128)(2,1)S(1)}, bf16[2,192,256]{2,1,0:T(8,128)(2,1)S(1)}, u32[]{:S(2)}, u32[]{:S(2)}) collective-permute-start(bf16[2,192,256]{2,1,0:T(8,128)(2,1)S(1)} %fusion.8), channel_id=1, source_target_pairs={{64,128},{72,136},{80,144},{88,152},{96,160},{104,168},{112,176},{... | collective-permute-start | bytes 589832 | tf_op jit(solution)/shard_map/ppermute | solution.py:233
  163.7 11.2 %collective-permute-start.30 = (bf16[2,192,256]{2,1,0:T(8,128)(2,1)S(1)}, bf16[2,192,256]{2,1,0:T(8,128)(2,1)S(1)}, u32[]{:S(2)}, u32[]{:S(2)}) collective-permute-start(bf16[2,192,256]{2,1,0:T(8,128)(2,1)S(1)} %fusion.8), channel_id=1, source_target_pairs={{192,128},{200,136},{208,144},{216,152},{224,160},{232,168},{240,1... | collective-permute-start | bytes 589832 | tf_op jit(solution)/shard_map/ppermute | solution.py:233
  167.7 11.6 %collective-permute-start.3 = (bf16[3,192,256]{2,1,0:T(8,128)(2,1)S(1)}, bf16[3,192,256]{2,1,0:T(8,128)(2,1)S(1)}, u32[]{:S(2)}, u32[]{:S(2)}) collective-permute-start(bf16[3,192,256]{2,1,0:T(8,128)(2,1)S(1)} %get-tuple-element.36), channel_id=1, source_target_pairs={{0,32},{8,40},{16,48},{24,56},{32,0},{40,8},{48,16},{56,24},{64,96... | collective-permute-start | bytes 884744 | tf_op jit(solution)/shard_map/ppermute | solution.py:223
  170.2 12.6 %collective-permute-start.4 = (bf16[3,192,256]{2,1,0:T(8,128)(2,1)S(1)}, bf16[3,192,256]{2,1,0:T(8,128)(2,1)S(1)}, u32[]{:S(2)}, u32[]{:S(2)}) collective-permute-start(bf16[3,192,256]{2,1,0:T(8,128)(2,1)S(1)} %get-tuple-element.38), channel_id=1, source_target_pairs={{0,16},{8,24},{16,32},{24,40},{32,48},{40,56},{48,0},{56,8},{64,80... | collective-permute-start | bytes 884744 | tf_op jit(solution)/shard_map/ppermute | solution.py:223
  170.4 15.8 %collective-permute-start.5 = (bf16[3,192,256]{2,1,0:T(8,128)(2,1)S(1)}, bf16[3,192,256]{2,1,0:T(8,128)(2,1)S(1)}, u32[]{:S(2)}, u32[]{:S(2)}) collective-permute-start(bf16[3,192,256]{2,1,0:T(8,128)(2,1)S(1)} %get-tuple-element.37), channel_id=1, source_target_pairs={{0,48},{8,56},{16,0},{24,8},{32,16},{40,24},{48,32},{56,40},{64,11... | collective-permute-start | bytes 884744 | tf_op jit(solution)/shard_map/ppermute | solution.py:223
  173.6 14.6 %collective-permute-start.37 = (bf16[2,192,256]{2,1,0:T(8,128)(2,1)S(1)}, bf16[2,192,256]{2,1,0:T(8,128)(2,1)S(1)}, u32[]{:S(2)}, u32[]{:S(2)}) collective-permute-start(bf16[2,192,256]{2,1,0:T(8,128)(2,1)S(1)} %fusion.5), channel_id=1, source_target_pairs={{64,192},{72,200},{80,208},{88,216},{96,224},{104,232},{112,240},{... | collective-permute-start | bytes 589832 | tf_op jit(solution)/shard_map/ppermute | solution.py:233
  174.9 15.3 %collective-permute-start.38 = (bf16[2,192,256]{2,1,0:T(8,128)(2,1)S(1)}, bf16[2,192,256]{2,1,0:T(8,128)(2,1)S(1)}, u32[]{:S(2)}, u32[]{:S(2)}) collective-permute-start(bf16[2,192,256]{2,1,0:T(8,128)(2,1)S(1)} %fusion.5), channel_id=1, source_target_pairs={{128,192},{136,200},{144,208},{152,216},{160,224},{168,232},{176,2... | collective-permute-start | bytes 589832 | tf_op jit(solution)/shard_map/ppermute | solution.py:233
  179.2 13.5 %collective-permute-start.39 = (bf16[2,192,256]{2,1,0:T(8,128)(2,1)S(1)}, bf16[2,192,256]{2,1,0:T(8,128)(2,1)S(1)}, u32[]{:S(2)}, u32[]{:S(2)}) collective-permute-start(bf16[2,192,256]{2,1,0:T(8,128)(2,1)S(1)} %fusion.5), channel_id=1, source_target_pairs={{0,192},{8,200},{16,208},{24,216},{32,224},{40,232},{48,240},{56,2... | collective-permute-start | bytes 589832 | tf_op jit(solution)/shard_map/ppermute | solution.py:233
  182.8 16.7 %collective-permute-start.19 = (bf16[1,192,256]{2,1,0:T(8,128)(2,1)S(1)}, bf16[1,192,256]{2,1,0:T(8,128)(2,1)S(1)}, u32[]{:S(2)}, u32[]{:S(2)}) collective-permute-start(bf16[1,192,256]{2,1,0:T(8,128)(2,1)S(1)} %fusion.24), channel_id=1, source_target_pairs={{192,64},{200,72},{208,80},{216,88},{224,96},{232,104},{240,112},{... | collective-permute-start | bytes 294920 | tf_op jit(solution)/shard_map/ppermute | solution.py:233
  186.2 13.3 %collective-permute-start.20 = (bf16[1,192,256]{2,1,0:T(8,128)(2,1)S(1)}, bf16[1,192,256]{2,1,0:T(8,128)(2,1)S(1)}, u32[]{:S(2)}, u32[]{:S(2)}) collective-permute-start(bf16[1,192,256]{2,1,0:T(8,128)(2,1)S(1)} %fusion.24), channel_id=1, source_target_pairs={{0,64},{8,72},{16,80},{24,88},{32,96},{40,104},{48,112},{56,120},{... | collective-permute-start | bytes 294920 | tf_op jit(solution)/shard_map/ppermute | solution.py:233
  186.8 28.0 %copy-start.26 = (f32[4,128,128]{2,1,0:T(8,128)S(1)}, f32[4,128,128]{2,1,0:T(8,128)}, u32[]{:S(2)}) copy-start(f32[4,128,128]{2,1,0:T(8,128)} %copy-done.25) | copy-start | bytes 786436
  186.8 28.0 %copy-start.28 = (f32[4,128,128]{2,1,0:T(8,128)S(1)}, f32[4,128,128]{2,1,0:T(8,128)}, u32[]{:S(2)}) copy-start(f32[4,128,128]{2,1,0:T(8,128)} %copy-done.27) | copy-start | bytes 786436
  188.1 26.8 %copy-start.12 = (bf16[1024,512]{1,0:T(8,128)(2,1)S(1)}, bf16[1024,512]{1,0:T(8,128)(2,1)}, u32[]{:S(2)}) copy-start(bf16[1024,512]{1,0:T(8,128)(2,1)} %refs_7_.1) | copy-start | bytes 3145732
  188.1 5.8 %collective-permute-start.6 = (bf16[2,192,256]{2,1,0:T(8,128)(2,1)S(1)}, bf16[2,192,256]{2,1,0:T(8,128)(2,1)S(1)}, u32[]{:S(2)}, u32[]{:S(2)}) collective-permute-start(bf16[2,192,256]{2,1,0:T(8,128)(2,1)S(1)} %get-tuple-element.48), channel_id=1, source_target_pairs={{128,0},{136,8},{144,16},{152,24},{160,32},{168,40},{176,48},{184,... | collective-permute-start | bytes 589832 | tf_op jit(solution)/shard_map/ppermute | solution.py:233
  190.2 9.1 %collective-permute-start.7 = (bf16[2,192,256]{2,1,0:T(8,128)(2,1)S(1)}, bf16[2,192,256]{2,1,0:T(8,128)(2,1)S(1)}, u32[]{:S(2)}, u32[]{:S(2)}) collective-permute-start(bf16[2,192,256]{2,1,0:T(8,128)(2,1)S(1)} %get-tuple-element.49), channel_id=1, source_target_pairs={{192,0},{200,8},{208,16},{216,24},{224,32},{232,40},{240,48},{248,... | collective-permute-start | bytes 589832 | tf_op jit(solution)/shard_map/ppermute | solution.py:233
  192.7 6.6 %collective-permute-start.8 = (bf16[2,192,256]{2,1,0:T(8,128)(2,1)S(1)}, bf16[2,192,256]{2,1,0:T(8,128)(2,1)S(1)}, u32[]{:S(2)}, u32[]{:S(2)}) collective-permute-start(bf16[2,192,256]{2,1,0:T(8,128)(2,1)S(1)} %get-tuple-element.50), channel_id=1, source_target_pairs={{64,0},{72,8},{80,16},{88,24},{96,32},{104,40},{112,48},{120,56},{... | collective-permute-start | bytes 589832 | tf_op jit(solution)/shard_map/ppermute | solution.py:233
  193.4 21.5 %copy-start.9 = (bf16[1024,512]{1,0:T(8,128)(2,1)S(1)}, bf16[1024,512]{1,0:T(8,128)(2,1)}, u32[]{:S(2)}) copy-start(bf16[1024,512]{1,0:T(8,128)(2,1)} %v_ref.3) | copy-start | bytes 3145732
  193.5 21.4 %copy-start.4 = (bf16[1024,512]{1,0:T(8,128)(2,1)S(1)}, bf16[1024,512]{1,0:T(8,128)(2,1)}, u32[]{:S(2)}) copy-start(bf16[1024,512]{1,0:T(8,128)(2,1)} %refs_5_.1) | copy-start | bytes 3145732
  193.5 21.4 %copy-start.7 = (bf16[1024,512]{1,0:T(8,128)(2,1)S(1)}, bf16[1024,512]{1,0:T(8,128)(2,1)}, u32[]{:S(2)}) copy-start(bf16[1024,512]{1,0:T(8,128)(2,1)} %refs_6_.1) | copy-start | bytes 3145732
  193.5 21.4 %copy-start.16 = (bf16[1,32,16,128]{3,2,0,1:T(8,128)(2,1)S(1)}, bf16[1,32,16,128]{3,2,0,1:T(8,128)(2,1)}, u32[]{:S(2)}) copy-start(bf16[1,32,16,128]{3,2,0,1:T(8,128)(2,1)} %get-tuple-element.51) | copy-start | bytes 393220
  193.5 21.4 %copy-start.18 = (bf16[1,32,16,128]{3,2,0,1:T(8,128)(2,1)S(1)}, bf16[1,32,16,128]{3,2,0,1:T(8,128)(2,1)}, u32[]{:S(2)}) copy-start(bf16[1,32,16,128]{3,2,0,1:T(8,128)(2,1)} %copy-done.17) | copy-start | bytes 393220
  194.0 5.5 %collective-permute-start.21 = (bf16[1,192,256]{2,1,0:T(8,128)(2,1)S(1)}, bf16[1,192,256]{2,1,0:T(8,128)(2,1)S(1)}, u32[]{:S(2)}, u32[]{:S(2)}) collective-permute-start(bf16[1,192,256]{2,1,0:T(8,128)(2,1)S(1)} %fusion.24), channel_id=1, source_target_pairs={{128,64},{136,72},{144,80},{152,88},{160,96},{168,104},{176,112},{... | collective-permute-start | bytes 294920 | tf_op jit(solution)/shard_map/ppermute | solution.py:233
  199.7 21.7 %collective-permute-start.41 = (bf16[192,256]{1,0:T(8,128)(2,1)S(1)}, bf16[192,256]{1,0:T(8,128)(2,1)S(1)}, u32[]{:S(2)}, u32[]{:S(2)}) collective-permute-start(bf16[192,256]{1,0:T(8,128)(2,1)S(1)} %select_bitcast_fusion), channel_id=1, source_target_pairs={{0,0},{1,33},{2,66},{3,99},{4,132},{5,165},{6,198},{7,231},{8,8},{... | collective-permute-start | bytes 294920 | tf_op jit(solution)/shard_map/ppermute | solution.py:329
  212.8 13.3 %collective-permute-start.40 = (bf16[192,256]{1,0:T(8,128)(2,1)S(1)}, bf16[192,256]{1,0:T(8,128)(2,1)S(1)}, u32[]{:S(2)}, u32[]{:S(2)}) collective-permute-start(bf16[192,256]{1,0:T(8,128)(2,1)S(1)} %get-tuple-element.33), channel_id=1, source_target_pairs={{0,224},{1,1},{2,34},{3,67},{4,100},{5,133},{6,166},{7,199},{8,232... | collective-permute-start | bytes 294920 | tf_op jit(solution)/shard_map/ppermute | solution.py:330
  (10 other events, 9.6 us)

commit v2 on v1

v2 whole, which is shorter than its diff:
```python
import functools
import math

import jax
import jax.numpy as jnp
from jax import lax
from jax.experimental import pallas as pl
from jax.experimental.pallas import tpu as pltpu
from jax.sharding import PartitionSpec as P

DH = 128
BLOCK = 512
HALF = BLOCK // 2
NX, NY, NC = 4, 4, 2
BF16 = jnp.bfloat16
F32 = jnp.float32

NN = (((1,), (0,)), ((), ()))
NT = (((1,), (1,)), ((), ()))
TN = (((0,), (0,)), ((), ()))


def dot(a, b, dims):
    return lax.dot_general(a, b, dims, preferred_element_type=F32)


QUICK = pl.CostEstimate(flops=1, bytes_accessed=1, transcendentals=0)


def params():
    return pltpu.CompilerParams(vmem_limit_bytes=58 * 1024 * 1024)


def tie(*arrays):
    return lax.optimization_barrier(arrays)


def states_kernel(_, q_ref, k_ref, v_ref, o_ref, kv_ref, g_ref, tot_ref, pack_ref):
    kv = []
    g = []
    for b in range(2):
        rows = pl.ds(b * BLOCK, BLOCK)
        kv.append(dot(k_ref[rows, :], v_ref[rows, :], TN))
        g.append(dot(q_ref[rows, :], o_ref[rows, :], TN))
    kv_ref[0] = kv[0]
    g_ref[0] = g[1]
    cut = tot_ref.shape[3]
    for p in range(DH // cut):
        rows = slice(p * cut, (p + 1) * cut)
        tot_ref[0, p, 0] = (g[0] + g[1])[rows].astype(BF16)
        tot_ref[0, p, 1] = (kv[0] + kv[1])[rows].astype(BF16)

    @pl.when(pl.program_id(0) < 2)
    def _():
        for p, ref in enumerate((q_ref, k_ref, o_ref)):
            pack_ref[p] = ref[...]


def local_states(core, q, k, v, o, n_seq):
    rows, features = q.shape
    heads = features // DH
    parts = n_seq // heads

    def head(h, c):
        return lax.rem(2 * (1 - c[0]) + h, heads)

    by_head = pl.BlockSpec((rows, DH), lambda h, c: (0, head(h, c)))
    state = pl.BlockSpec((1, DH, DH), lambda h, c: (head(h, c), 0, 0))
    cuts = (parts, 2, DH // parts, DH)
    return pl.pallas_call(
        states_kernel,
        grid_spec=pltpu.PrefetchScalarGridSpec(
            num_scalar_prefetch=1,
            grid=(heads,),
            in_specs=[by_head] * 4,
            out_specs=[
                state,
                state,
                pl.BlockSpec((1, *cuts), lambda h, c: (head(h, c), 0, 0, 0, 0)),
                pl.BlockSpec((3, rows, DH), lambda h, c: (0, 0, jnp.minimum(h, 1))),
            ],
        ),
        out_shape=[
            jax.ShapeDtypeStruct((heads, DH, DH), F32),
            jax.ShapeDtypeStruct((heads, DH, DH), F32),
            jax.ShapeDtypeStruct((heads, *cuts), BF16),
            jax.ShapeDtypeStruct((3, rows, 2 * DH), BF16),
        ],
        compiler_params=params(),
        cost_estimate=QUICK,
        name="states",
    )(core, q, k, v, o)


def sums_kernel(in_ref, out_ref):
    n = in_ref.shape[0]
    for which, order in ((0, range(n - 1, -1, -1)), (1, range(n))):
        acc = jnp.zeros(in_ref.shape[2:], F32)
        for at in order:
            part = acc.astype(BF16)
            out_ref[at, which] = part
            if which == 0:
                out_ref[at ^ 1, 2] = part
            acc = acc + in_ref[at, which].astype(F32)


def running_sums(parts):
    return pl.pallas_call(
        sums_kernel,
        out_shape=jax.ShapeDtypeStruct((parts.shape[0], 3, *parts.shape[2:]), BF16),
        compiler_params=params(),
        cost_estimate=QUICK,
        name="running_sums",
    )(parts)


def keep(s0, t0, rows, cols, upper):
    s = lax.broadcasted_iota(jnp.int32, (rows, cols), 0) + s0
    t = lax.broadcasted_iota(jnp.int32, (rows, cols), 1) + t0
    return t >= s if upper else t <= s


def upper_product(a, b, c):
    top = dot(a[:HALF], b, NT)
    top = jnp.where(keep(0, 0, HALF, BLOCK, True), top, 0.0).astype(BF16)
    low = dot(a[HALF:], b[HALF:], NT)
    low = jnp.where(keep(0, 0, HALF, HALF, True), low, 0.0).astype(BF16)
    return jnp.concatenate([dot(top, c, NN), dot(low, c[HALF:], NN)], 0)


def lower_product(a, b, c):
    top = dot(a[:HALF], b[:HALF], NT)
    top = jnp.where(keep(0, 0, HALF, HALF, False), top, 0.0).astype(BF16)
    low = dot(a[HALF:], b, NT)
    low = jnp.where(keep(HALF, 0, HALF, BLOCK, False), low, 0.0).astype(BF16)
    return jnp.concatenate([dot(top, c[:HALF], NN), dot(low, c, NN)], 0)


def value_kernel(scaling, _, *refs):
    own, other = refs[:3], refs[3:6]
    own_later, other_later, out_ref = refs[6:]

    def load(members, b):
        rows = pl.ds(b * BLOCK, BLOCK)
        return [ref[rows, :] if len(ref.shape) == 2 else ref[0, rows, :] for ref in members]

    for at, (members, later) in enumerate(((own, own_later), (other, other_later))):
        after = later[0, :, 0].reshape(DH, DH).astype(F32)
        for b in (1, 0):
            q, k, o = load(members, b)
            grad = upper_product(k, q, o) + dot(k, after.astype(BF16), NN)
            out_ref[at, pl.ds(b * BLOCK, BLOCK), :] = (grad * scaling).astype(BF16)
            if b == 1:
                after = after + dot(q, o, TN)


def value_gradient(core, q, k, o, packed, sums, scaling):
    rows = q.shape[0]
    parts, cut = sums.shape[1], sums.shape[3]
    own = pl.BlockSpec((rows, DH), lambda h, c: (0, 2 * c[0] + h))
    other = [pl.BlockSpec((1, rows, DH), lambda h, c, p=p: (p, 0, h)) for p in range(3)]
    later = [
        pl.BlockSpec((1, parts, 1, cut, DH), lambda h, c, k=k: (2 * c[0] + h, 0, k, 0, 0)) for k in (0, 2)
    ]
    out = pl.BlockSpec((2, rows, DH), lambda h, c: (0, 0, h))
    return pl.pallas_call(
        functools.partial(value_kernel, scaling),
        grid_spec=pltpu.PrefetchScalarGridSpec(
            num_scalar_prefetch=1,
            grid=(2,),
            in_specs=[own] * 3 + other + later,
            out_specs=out,
        ),
        out_shape=jax.ShapeDtypeStruct((2, rows, 2 * DH), BF16),
        compiler_params=params(),
        cost_estimate=QUICK,
        name="value_gradient",
    )(core, q, k, o, packed, packed, packed, sums, sums)


def query_key_kernel(scaling, q_ref, k_ref, v_ref, o_ref, later_ref, before_ref, g_ref, kv_ref, dq_ref, dk_ref):
    later = later_ref[0, :, 0].reshape(DH, DH).astype(F32)
    earlier = before_ref[0, :, 0].reshape(DH, DH).astype(F32)
    for b in range(2):
        rows = pl.ds(b * BLOCK, BLOCK)
        q, k, v, o = q_ref[rows, :], k_ref[rows, :], v_ref[rows, :], o_ref[rows, :]
        after = (later + g_ref[0]) if b == 0 else later
        before = earlier if b == 0 else (earlier + kv_ref[0])
        dq = lower_product(o, v, k) + dot(o, before.astype(BF16), NT)
        dk = upper_product(v, o, q) + dot(v, after.astype(BF16), NT)
        dq_ref[rows, :] = (dq * scaling).astype(BF16)
        dk_ref[rows, :] = (dk * scaling).astype(BF16)


def query_key_gradients(q, k, v, o, sums, g, kv, scaling):
    rows = q.shape[0]
    heads = q.shape[1] // DH
    parts, cut = sums.shape[1], sums.shape[3]
    by_head = pl.BlockSpec((rows, DH), lambda h: (0, h))
    state = pl.BlockSpec((1, DH, DH), lambda h: (h, 0, 0))
    later = pl.BlockSpec((1, parts, 1, cut, DH), lambda h: (h, 0, 0, 0, 0))
    earlier = pl.BlockSpec((1, parts, 1, cut, DH), lambda h: (h, 0, 1, 0, 0))
    return pl.pallas_call(
        functools.partial(query_key_kernel, scaling),
        grid=(heads,),
        in_specs=[by_head] * 4 + [later, earlier, state, state],
        out_specs=[by_head, by_head],
        out_shape=[jax.ShapeDtypeStruct(q.shape, BF16)] * 2,
        compiler_params=params(),
        cost_estimate=QUICK,
        name="query_key_gradients",
    )(q, k, v, o, sums, sums, g, kv)


def x_spec(tokens, rows, at):
    return pl.BlockSpec((tokens, rows // 2), at)


def terms_kernel(scale, blocks, n_x, n_v, *refs):
    xs, vs, out_ref = refs[:n_x], refs[n_x : n_x + n_v], refs[n_x + n_v]
    piece = out_ref.shape[2]
    for n, (x, v) in enumerate(blocks):
        term = dot(xs[2 * x][...], vs[v][0], TN) + dot(xs[2 * x + 1][...], vs[v][1], TN)
        for low in range(2):
            out_ref[low, n] = (term[low * piece : (low + 1) * piece] * scale).astype(BF16)


def weight_terms(xs, vs, blocks, scale):
    tokens, rows = xs[0].shape
    cols = vs[0].shape[2]
    tail = (len(blocks), rows // 4, cols)
    return pl.pallas_call(
        functools.partial(terms_kernel, scale, blocks, len(xs), len(vs)),
        grid=(2,),
        in_specs=[x_spec(tokens, rows, lambda r: (0, r))] * len(xs)
        + [pl.BlockSpec((2, tokens, cols), lambda r: (0, 0, 0))] * len(vs),
        out_specs=pl.BlockSpec((2, *tail), lambda r: (r, 0, 0, 0)),
        out_shape=jax.ShapeDtypeStruct((4, *tail), BF16),
        compiler_params=params(),
        cost_estimate=QUICK,
        name="weight_terms",
    )(*xs, *vs)


def last_kernel(scale, at_ref, *refs):
    xs, v_ref, outs = refs[:4], refs[4], refs[5:]
    piece = outs[0].shape[0]
    for core, pair in enumerate((xs[2:], xs[:2])):

        @pl.when(at_ref[1] == core)
        def _(pair=pair):
            term = dot(pair[0][...], v_ref[0], TN) + dot(pair[1][...], v_ref[1], TN)
            for low in range(2):
                place = lax.rem(2 * pl.program_id(0) + low + 4 - at_ref[0], 4)
                rounded = (term[low * piece : (low + 1) * piece] * scale).astype(BF16)
                for d in range(4):

                    @pl.when(place == d)
                    def _(d=d, rounded=rounded):
                        outs[d][...] = rounded


def last_terms(at, xs, v, scale):
    tokens, rows = xs[0].shape
    cols = v.shape[2]
    shape = (rows // 4, cols)

    def used_by(core):
        return lambda r, s: (0, jnp.where(s[1] == core, r, 0))

    return pl.pallas_call(
        functools.partial(last_kernel, scale),
        grid_spec=pltpu.PrefetchScalarGridSpec(
            num_scalar_prefetch=1,
            grid=(2,),
            in_specs=[x_spec(tokens, rows, used_by(1))] * 2
            + [x_spec(tokens, rows, used_by(0))] * 2
            + [pl.BlockSpec((2, tokens, cols), lambda r, s: (0, 0, 0))],
            out_specs=[pl.BlockSpec(shape, lambda r, s: (0, 0))] * 4,
        ),
        out_shape=[jax.ShapeDtypeStruct(shape, BF16)] * 4,
        compiler_params=params(),
        cost_estimate=QUICK,
        name="last_terms",
    )(at, *xs, v)


def seq_index(x, y, c):
    return ((x % NX) * NY + (y % NY)) * NC + c


CHIPS = [(x, y, c) for x in range(NX) for y in range(NY) for c in range(NC)]
SWAP = [(seq_index(x, y, c), seq_index(x, y, 1 - c)) for x, y, c in CHIPS]


def shift(axis, d):
    dx, dy = (d, 0) if axis == "x" else (0, d)
    return [(seq_index(x, y, c), seq_index(x + dx, y + dy, c)) for x, y, c in CHIPS]


def shift_to(axis, targets, d):
    at = {seq_index(x, y, c): (x if axis == "x" else y) for x, y, c in CHIPS}
    return [(a, b) for a, b in shift(axis, d) if at[b] in targets]


def total(parts):
    acc = parts[0].astype(F32)
    for part in parts[1:]:
        acc = acc + part.astype(F32)
    return acc.astype(BF16)


def send_all(axis, sums):
    return [lax.ppermute(sums[d], "seq", shift(axis, d)) for d in (2, 1, 3)]


def choose(pieces, targets, at):
    chosen = []
    for d in range(4):
        piece = pieces[0]
        for t, other in zip(targets[1:], pieces[1:]):
            piece = jnp.where(at == (t - d) % 4, other, piece)
        chosen.append(piece)
    return chosen


def send_to(axis, chosen, targets):
    return [lax.ppermute(chosen[d], "seq", shift_to(axis, targets, d)) for d in (2, 1, 3)]


HELD_AT_X = {0: ((-1, 1),) * 2, 1: ((1, -1),) * 2, 2: ((-1, 2),) * 2, 3: ((1, -2),) * 2}
HELD_AT_Y = {0: ((0, 0),) * 2, 1: ((-1, 0),) * 2, 2: ((1, 0),) * 2, 3: ((1, -3), (-1, 3))}
LAST = 3


def owners(turn, nz):
    pairs = ([], [])
    for x, y, c in CHIPS:
        by_x = c == turn
        r = y if by_x else x
        di, dj = HELD_AT_X[x][c] if by_x else HELD_AT_Y[y][c]
        for m in range(nz):
            i, j = (m + di) % nz, (m + dj) % nz
            pairs[not by_x and y == LAST].append((seq_index(x, y, c) * nz + m, (4 * i + r) * nz + j))
    return pairs


def per_device(layer_input, queries, keys, values, out_grad):
    tok_rows, features = queries.shape
    half = features // 2
    n_seq, n_z = lax.axis_size("seq"), lax.axis_size("head")
    scaling = 1.0 / math.sqrt(DH * tok_rows * n_seq)
    weight_scale = 1.0 / math.sqrt(tok_rows * n_seq)
    s = lax.axis_index("seq").astype(jnp.int32)
    z = lax.axis_index("head").astype(jnp.int32)
    x, y, c = s // (NY * NC), lax.rem(s // NC, NY), lax.rem(s, NC)
    core, at_x = c.reshape(1), jnp.stack([x, c])
    up = [(i, (i + 1) % n_z) for i in range(n_z)]
    down = [(i, (i - 1) % n_z) for i in range(n_z)]
    both = ("seq", "head")
    apart = [
        (seq_index(a, b, e) * n_z + m, seq_index(a, b, e) * n_z + (m + 1 - 2 * e) % n_z)
        for a, b, e in CHIPS
        for m in range(n_z)
    ]

    def go(array, way):
        return lax.ppermute(array, "head", way)

    def swap(array):
        return lax.ppermute(array, "seq", SWAP)

    def terms(xs, vs, blocks):
        return weight_terms(xs, vs, blocks, weight_scale)

    groups = {
        "x": [[seq_index(a, b, e) for a in range(NX)] for b in range(NY) for e in range(NC)],
        "y": [[seq_index(a, b, e) for b in range(NY)] for a in range(NX) for e in range(NC)],
    }

    def exchange(axis, pieces):
        return lax.all_to_all(pieces, "seq", 0, 0, axis_index_groups=groups[axis])

    prev0, next0 = go(layer_input, up), go(layer_input, down)
    kv0, g1, totals, packed = local_states(core, queries, keys, values, out_grad, n_seq)
    spread = lax.all_to_all(totals.reshape(n_seq, *totals.shape[2:]), "seq", 0, 0)
    sums = lax.all_to_all(running_sums(spread), "seq", 0, 0)
    sums = sums.reshape(*totals.shape[:2], *sums.shape[1:])
    packed = swap(packed)
    v0 = value_gradient(core, queries, keys, out_grad, packed, sums, scaling)

    u1, d1 = go(v0, up), go(v0, down)
    prev0, next0, kv0, x_own, _ = tie(prev0, next0, kv0, layer_input, v0)
    prev1, next1, own1 = swap(prev0), swap(next0), swap(x_own)
    query_grad, key_grad = query_key_gradients(queries, keys, values, out_grad, sums, g1, kv0, scaling)
    prev1, next1, query_grad, key_grad = tie(prev1, next1, query_grad, key_grad)
    near = [prev0, prev1, next0, next1]
    t0 = terms([x_own, own1, *near], [v0], [(0, 0), (1, 0), (2, 0)])

    p0 = exchange("x", t0)

    u1, d1 = tie(u1, d1, t0)[:2]
    u2, d2 = go(u1, up), go(d1, down)
    t1 = terms(near, [d1, u1], [(0, 0), (1, 1)])
    p0 = total(list(p0))
    p1 = exchange("y", t1)
    c0 = choose([p0[0], p0[1], p0[2]], [0, 1, 2], y)
    y0 = send_to("y", c0, [0, 1, 2])

    u2, d2 = tie(u2, d2, t1, *c0)[:2]
    v3 = lax.ppermute(jnp.where(c == 0, u2, d2), both, apart)
    t2 = terms(near, [d2, u2], [(0, 0), (1, 1)])
    p1 = total(list(p1))
    p2 = exchange("y", t2)

    v3 = tie(v3, t2, p1)[0]
    q3 = last_terms(at_x, near, v3, weight_scale)
    x3 = send_all("x", q3)
    *y0, p2, _ = tie(*y0, p2, q3[0])
    held = jnp.concatenate([p1, total(list(p2))], 0)
    x2 = exchange("x", held)
    r0 = total([c0[0]] + y0)
    p3 = total([q3[0]] + x3)

    p3 = tie(p3, held)[0]
    y3 = send_to("y", [p3] * 4, [LAST])
    held_x = total(list(x2))
    first = jnp.where(c == 0, held_x, r0)
    second = jnp.where(c == 0, r0, held_x)
    early0, late0 = owners(0, n_z)
    early1, late1 = owners(1, n_z)
    early_first = lax.ppermute(first, both, early0)
    early_second = lax.ppermute(second, both, early1)
    r3 = total([p3] + y3)
    r3 = tie(r3, first, second)[0]
    late_first = lax.ppermute(r3, both, late0)
    late_second = lax.ppermute(r3, both, late1)

    away = lax.rem(z - s // 4 + n_z, n_z)
    first = jnp.where(away == 4, late_first, early_first)
    second = jnp.where(away == 4, late_second, early_second)
    by_x = (away == 2) | (away == 3) | (away == 5) | (away == 6)
    left = jnp.where(by_x, first, second)
    right = jnp.where(by_x, second, first)
    weight_grad = jnp.concatenate([left, right], 1).astype(F32)
    return (query_grad, key_grad, weight_grad)


def solution(mesh):
    return jax.shard_map(
        per_device,
        mesh=mesh,
        in_specs=(P("seq", "head"),) * 5,
        out_specs=(P("seq", "head"),) * 3,
        check_vma=False,
    )
```

time: 228 us -> 182 us (0.80)
  the two profiles are of different devices: /device:TPU:70 before, /device:TPU:18 now
where the time goes in v2:
time: 182 us; the launch traced here: 181 us
  starting transfers between devices  68.2 us (37%)
  Pallas kernels  42.1 us (23%)
  waiting for transfers between devices  33.8 us (19%)
  blocking collectives  28.4 us (16%)
  other arithmetic  4.21 us (2%)
  local copies, waits for them, and re-layouts  3.57 us (2%)
    all_to_all x4, starting transfers between devices, exchange(): return lax.all_to_all(pieces, 'seq', 0, 0, axis_index_groups=groups[axis])  22 us
    pallas_call x3, Pallas kernels, weight_terms(): pl.pallas_call(functools.partial(terms_kernel, scale, blocks, len(xs), le...  18 us
    all_to_all x1, blocking collectives, per_device(): sums = lax.all_to_all(running_sums(spread), 'seq', 0, 0)  14.9 us
    ppermute x6, starting transfers between devices, send_to(): lax.ppermute(chosen[d], 'seq', shift_to(axis, targets, d))  13.7 us
    all_to_all x1, blocking collectives, per_device(): lax.all_to_all(totals.reshape(n_seq, *totals.shape[2:]), 'seq', 0, 0)  13.5 us
    ppermute x6, starting transfers between devices, go(): return lax.ppermute(array, 'head', way)  12.5 us
    ppermute x6, waiting for transfers between devices, go(): return lax.ppermute(array, 'head', way)  11.8 us
    ppermute x1, starting transfers between devices, per_device(): early_first = lax.ppermute(first, both, early0)  10.7 us
  transfers between devices with their start and end apart: 28, of which 9 were waited for; matrix products, arithmetic and copies ran while one was open for 2% of the time, Pallas kernels for 20%

profile of v2, /device:TPU:18, one launch (start us, length us, event | category | flops | bytes accessed | tf_op | source)
XLA Modules:
  0.0 181.3 jit_solution(7355900711901143828)
XLA Ops:
  0.6 5.3 %states.1 = (f32[4,128,128]{2,1,0:T(8,128)}, f32[4,128,128]{2,1,0:T(8,128)}, bf16[4,8,2,16,128]{4,3,2,1,0:T(8,128)(2,1)}, bf16[3,1024,256]{2,1,0:T(8,128)(2,1)}) custom-call(s32[1]{0:T(128)} %bitcast._, bf16[1024,512]{1,0:T(8,128)(2,1)} %q_ref.3, bf16[1024,512]{1,0:T(8,128)(2,1)} %k_ref.3, bf16[1024,512]{1,0:T(8,128)(2,1)} %v_ref.3, bf16[1024,512]{1,0:T(8,128)(2,1)} %o_ref.3), custom_call_target="tpu_custom_call" | custom-call | flops 1 | bytes 1 | tf_op jit(solution)/shard_map/states/pallas_call | solution.py:70
  5.9 0.0 collective-permute-start.2
  5.9 2.0 %collective-permute-start = (bf16[1024,768]{1,0:T(8,128)(2,1)}, bf16[1024,768]{1,0:T(8,128)(2,1)S(1)}, u32[]{:S(2)}, u32[]{:S(2)}) collective-permute-start(bf16[1024,768]{1,0:T(8,128)(2,1)} %refs_0_.2), channel_id=1, source_target_pairs={{0,1},{1,2},{2,3},{3,4},{4,5},{5,6},{6,7},{7,0},{8,9},{9,10},{10,1... | collective-permute-start | bytes 4718600 | tf_op jit(solution)/shard_map/ppermute | solution.py:368
  7.9 4.0 %collective-permute-start.1 = (bf16[1024,768]{1,0:T(8,128)(2,1)}, bf16[1024,768]{1,0:T(8,128)(2,1)S(1)}, u32[]{:S(2)}, u32[]{:S(2)}) collective-permute-start(bf16[1024,768]{1,0:T(8,128)(2,1)} %refs_0_.2), channel_id=1, source_target_pairs={{0,7},{1,0},{2,1},{3,2},{4,3},{5,4},{6,5},{7,6},{8,15},{9,8},{10,9... | collective-permute-start | bytes 4718600 | tf_op jit(solution)/shard_map/ppermute | solution.py:368
  12.0 13.5 %all_to_all.30.in_ref = bf16[32,2,16,128]{3,2,1,0:T(8,128)(2,1)} all-to-all(bf16[32,2,16,128]{3,2,1,0:T(8,128)(2,1)} %bitcast.23), channel_id=1, replica_groups=mesh['seq'=32,'head'=8] {'seq'}, dimensions={0} | all-to-all | bytes 524288 | tf_op jit(solution)/shard_map/all_to_all | solution.py:386
  25.5 1.7 running_sums.1
  27.2 14.9 %all_to_all.31 = bf16[32,3,16,128]{3,2,1,0:T(8,128)(2,1)} all-to-all(bf16[32,3,16,128]{3,2,1,0:T(8,128)(2,1)} %running_sums.1), channel_id=1, replica_groups=mesh['seq'=32,'head'=8] {'seq'}, dimensions={0} | all-to-all | bytes 786432 | tf_op jit(solution)/shard_map/all_to_all | solution.py:387
  42.2 0.0 collective-permute-done.2.refs_3_.refs_4_.refs_5_
  42.2 1.2 copy-done.3
  43.3 4.9 %value_gradient.1.refs_6_ = bf16[2,1024,256]{2,1,0:T(8,128)(2,1)} custom-call(s32[1]{0:T(128)} %bitcast._, bf16[1024,512]{1,0:T(8,128)(2,1)} %q_ref.3, bf16[1024,512]{1,0:T(8,128)(2,1)} %k_ref.3, bf16[1024,512]{1,0:T(8,128)(2,1)} %o_ref.3, bf16[3,1024,256]{2,1,0:T(8,128)(2,1)} %copy-done.3, bf16[3,1024,256]{2,1,0:T(8,128)(2,1)} %copy-done.3, ...), custom_call_target="tpu_custom_call" | custom-call | flops 1 | bytes 1 | tf_op jit(solution)/shard_map/value_gradient/pallas_call | solution.py:166
  48.2 0.0 collective-permute-done.refs_2_.refs_0_
  48.3 0.0 collective-permute-done.1.refs_4_.refs_2_
  48.3 0.1 collective-permute-start.3
  48.4 0.5 collective-permute-start.4
  48.9 0.1 collective-permute-start.7
  49.0 3.2 %collective-permute-start.6 = (bf16[2,1024,256]{2,1,0:T(8,128)(2,1)}, bf16[2,1024,256]{2,1,0:T(8,128)(2,1)}, u32[]{:S(2)}, u32[]{:S(2)}) collective-permute-start(bf16[2,1024,256]{2,1,0:T(8,128)(2,1)} %value_gradient.1.refs_6_), channel_id=1, source_target_pairs={{0,7},{1,0},{2,1},{3,2},{4,3},{5,4},{6,5},{7,6},{8,15},{9,8},{10,9... | collective-permute-start | bytes 3145736 | tf_op jit(solution)/shard_map/ppermute | solution.py:368
  52.2 7.0 %query_key_gradients.1 = (bf16[1024,512]{1,0:T(8,128)(2,1)}, bf16[1024,512]{1,0:T(8,128)(2,1)}) custom-call(bf16[1024,512]{1,0:T(8,128)(2,1)} %q_ref.3, bf16[1024,512]{1,0:T(8,128)(2,1)} %k_ref.3, bf16[1024,512]{1,0:T(8,128)(2,1)} %v_ref.3, bf16[1024,512]{1,0:T(8,128)(2,1)} %o_ref.3, bf16[4,8,3,16,128]{4,3,2,1,0:T(8,128)(2,1)} %bitcast.21, ...), custom_call_target="tpu_custom_call" | custom-call | flops 1 | bytes 1 | tf_op jit(solution)/shard_map/query_key_gradients/pallas_call | solution.py:203
  59.3 0.0 collective-permute-done.4.refs_5_.refs_3_
  59.3 1.2 copy-done.2
  60.5 6.9 %weight_terms.3 = bf16[4,3,192,256]{3,2,1,0:T(8,128)(2,1)} custom-call(bf16[1024,768]{1,0:T(8,128)(2,1)} %refs_0_.2, bf16[1024,768]{1,0:T(8,128)(2,1)} %collective-permute-done.7.refs_1_, bf16[1024,768]{1,0:T(8,128)(2,1)} %copy-done, bf16[1024,768]{1,0:T(8,128)(2,1)} %copy-done.2, bf16[1024,768]{1,0:T(8,128)(2,1)} %copy-done.1, ...), custom_call_target="tpu_custom_call" | custom-call | flops 1 | bytes 1 | tf_op jit(solution)/shard_map/weight_terms/pallas_call | solution.py:232
  67.3 4.9 %all-to-all-start.2 = ((bf16[4,3,192,256]{3,2,1,0:T(8,128)(2,1)}), bf16[4,3,192,256]{3,2,1,0:T(8,128)(2,1)S(1)}, u32[]{:S(2)}, u32[]{:S(2)}) async-start(bf16[4,3,192,256]{3,2,1,0:T(8,128)(2,1)} %weight_terms.3), calls=%async_computation.2 | async-start | bytes 2359296 | tf_op jit(solution)/shard_map/all_to_all | solution.py:382
  72.2 3.7 %collective-permute-done.5.refs_5_ = bf16[2,1024,256]{2,1,0:T(8,128)(2,1)} collective-permute-done((bf16[2,1024,256]{2,1,0:T(8,128)(2,1)}, bf16[2,1024,256]{2,1,0:T(8,128)(2,1)}, u32[]{:S(2)}, u32[]{:S(2)}) %collective-permute-start.5) | collective-permute-done | bytes 1048608 | tf_op jit(solution)/shard_map/ppermute | solution.py:368
  76.0 1.2 collective-permute-start.8
  77.2 2.0 %collective-permute-start.9 = (bf16[2,1024,256]{2,1,0:T(8,128)(2,1)}, bf16[2,1024,256]{2,1,0:T(8,128)(2,1)S(1)}, u32[]{:S(2)}, u32[]{:S(2)}) collective-permute-start(bf16[2,1024,256]{2,1,0:T(8,128)(2,1)} %collective-permute-done.6.refs_4_), channel_id=1, source_target_pairs={{0,7},{1,0},{2,1},{3,2},{4,3},{5,4},{6,5},{7,6},{8,15},{9,8},{10,9... | collective-permute-start | bytes 3145736 | tf_op jit(solution)/shard_map/ppermute | solution.py:368
  79.2 5.6 %weight_terms.4 = bf16[4,2,192,256]{3,2,1,0:T(8,128)(2,1)} custom-call(bf16[1024,768]{1,0:T(8,128)(2,1)} %copy-done, bf16[1024,768]{1,0:T(8,128)(2,1)} %copy-done.2, bf16[1024,768]{1,0:T(8,128)(2,1)} %copy-done.1, bf16[1024,768]{1,0:T(8,128)(2,1)} %collective-permute-done.4.refs_5_.refs_3_, bf16[2,1024,256]{2,1,0:T(8,128)(2,1)} %collective-permute-done.6.refs_4_, ...), custom_call_target="tpu_custom_call" | custom-call | flops 1 | bytes 1 | tf_op jit(solution)/shard_map/weight_terms/pallas_call | solution.py:232
  84.8 2.8 %all-to-all-done.2 = bf16[4,3,192,256]{3,2,1,0:T(8,128)(2,1)S(1)} async-done(((bf16[4,3,192,256]{3,2,1,0:T(8,128)(2,1)}), bf16[4,3,192,256]{3,2,1,0:T(8,128)(2,1)S(1)}, u32[]{:S(2)}, u32[]{:S(2)}) %all-to-all-start.2) | async-done | bytes 1179680 | tf_op jit(solution)/shard_map/all_to_all | solution.py:382
  87.6 6.3 %all-to-all-start.3 = ((bf16[4,2,192,256]{3,2,1,0:T(8,128)(2,1)}), bf16[4,2,192,256]{3,2,1,0:T(8,128)(2,1)}, u32[]{:S(2)}, u32[]{:S(2)}) async-start(bf16[4,2,192,256]{3,2,1,0:T(8,128)(2,1)} %weight_terms.4), calls=%async_computation.3 | async-start | bytes 1572864 | tf_op jit(solution)/shard_map/all_to_all | solution.py:382
  93.9 0.1 add_convert_fusion
  94.1 8.0 %collective-permute-done.8.refs_5_ = bf16[2,1024,256]{2,1,0:T(8,128)(2,1)S(1)} collective-permute-done((bf16[2,1024,256]{2,1,0:T(8,128)(2,1)}, bf16[2,1024,256]{2,1,0:T(8,128)(2,1)S(1)}, u32[]{:S(2)}, u32[]{:S(2)}) %collective-permute-start.8) | collective-permute-done | bytes 1048608 | tf_op jit(solution)/shard_map/ppermute | solution.py:368
  102.1 0.1 broadcast_select_fusion
  102.2 0.9 copy-done.4
  103.1 0.4 copy-done.5
  103.5 2.0 %collective-permute-start.10 = (bf16[2,1024,256]{2,1,0:T(8,128)(2,1)S(1)}, bf16[2,1024,256]{2,1,0:T(8,128)(2,1)}, u32[]{:S(2)}, u32[]{:S(2)}) collective-permute-start(bf16[2,1024,256]{2,1,0:T(8,128)(2,1)S(1)} %broadcast_select_fusion), channel_id=1, source_target_pairs={{0,1},{1,2},{2,3},{3,4},{4,5},{5,6},{6,7},{7,0},{8,15},{9,8},{10,9... | collective-permute-start | bytes 3145736 | tf_op jit(solution)/shard_map/ppermute | solution.py:411
  105.5 5.6 %weight_terms.5 = bf16[4,2,192,256]{3,2,1,0:T(8,128)(2,1)} custom-call(bf16[1024,768]{1,0:T(8,128)(2,1)} %copy-done, bf16[1024,768]{1,0:T(8,128)(2,1)} %copy-done.2, bf16[1024,768]{1,0:T(8,128)(2,1)} %copy-done.1, bf16[1024,768]{1,0:T(8,128)(2,1)} %collective-permute-done.4.refs_5_.refs_3_, bf16[2,1024,256]{2,1,0:T(8,128)(2,1)} %copy-done.5, ...), custom_call_target="tpu_custom_call" | custom-call | flops 1 | bytes 1 | tf_op jit(solution)/shard_map/weight_terms/pallas_call | solution.py:232
  111.0 5.1 %all-to-all-start.4 = ((bf16[4,2,192,256]{3,2,1,0:T(8,128)(2,1)}), bf16[4,2,192,256]{3,2,1,0:T(8,128)(2,1)S(1)}, u32[]{:S(2)}, u32[]{:S(2)}) async-start(bf16[4,2,192,256]{3,2,1,0:T(8,128)(2,1)} %weight_terms.5), calls=%async_computation.4 | async-start | bytes 1572864 | tf_op jit(solution)/shard_map/all_to_all | solution.py:382
  116.1 0.7 pad_add_fusion.at_ref
  116.8 1.9 %collective-permute-start.14 = (bf16[192,256]{1,0:T(8,128)(2,1)S(1)}, bf16[192,256]{1,0:T(8,128)(2,1)S(1)}, u32[]{:S(2)}, u32[]{:S(2)}) collective-permute-start(bf16[192,256]{1,0:T(8,128)(2,1)S(1)} %get-tuple-element.68), channel_id=1, source_target_pairs={{0,32},{8,40},{32,0},{40,8},{48,16},{56,24},{64,96},{72,104},{96,6... | collective-permute-start | bytes 294920 | tf_op jit(solution)/shard_map/ppermute | solution.py:328
  118.7 1.3 collective-permute-start.15
  120.0 4.6 %collective-permute-start.16 = (bf16[192,256]{1,0:T(8,128)(2,1)S(1)}, bf16[192,256]{1,0:T(8,128)(2,1)S(1)}, u32[]{:S(2)}, u32[]{:S(2)}) collective-permute-start(bf16[192,256]{1,0:T(8,128)(2,1)S(1)} %get-tuple-element.66), channel_id=1, source_target_pairs={{16,0},{24,8},{32,16},{40,24},{48,32},{56,40},{80,64},{88,72},{96,... | collective-permute-start | bytes 294920 | tf_op jit(solution)/shard_map/ppermute | solution.py:328
  124.6 1.3 fusion
  125.9 5.1 %last_terms.1 = (bf16[192,256]{1,0:T(8,128)(2,1)}, bf16[192,256]{1,0:T(8,128)(2,1)}, bf16[192,256]{1,0:T(8,128)(2,1)}, bf16[192,256]{1,0:T(8,128)(2,1)}) custom-call(s32[2]{0:T(128)} %pad_add_fusion.at_ref, bf16[1024,768]{1,0:T(8,128)(2,1)} %copy-done, bf16[1024,768]{1,0:T(8,128)(2,1)} %copy-done.2, bf16[1024,768]{1,0:T(8,128)(2,1)} %copy-done.1, ...), custom_call_target="tpu_custom_call" | custom-call | flops 1 | bytes 1 | tf_op jit(solution)/shard_map/last_terms/pallas_call | solution.py:271
  131.1 0.1 fusion.1
  131.2 1.4 collective-permute-start.11
  132.6 1.6 collective-permute-start.12
  134.3 0.4 collective-permute-start.13
  134.7 0.8 pad_maximum_fusion
  135.4 2.2 %collective-permute-done.11 = bf16[192,256]{1,0:T(8,128)(2,1)S(1)} collective-permute-done((bf16[192,256]{1,0:T(8,128)(2,1)}, bf16[192,256]{1,0:T(8,128)(2,1)S(1)}, u32[]{:S(2)}, u32[]{:S(2)}) %collective-permute-start.11) | collective-permute-done | bytes 98336 | tf_op jit(solution)/shard_map/ppermute | solution.py:314
  137.6 0.5 collective-permute-done.12
  138.1 1.0 collective-permute-done.13
  139.1 0.1 add_convert_fusion.6
  139.2 0.7 collective-permute-start.17
  139.8 4.5 %collective-permute-start.18 = (bf16[192,256]{1,0:T(8,128)(2,1)S(1)}, bf16[192,256]{1,0:T(8,128)(2,1)S(1)}, u32[]{:S(2)}, u32[]{:S(2)}) collective-permute-start(bf16[192,256]{1,0:T(8,128)(2,1)S(1)} %add_convert_fusion.6), channel_id=1, source_target_pairs={{32,48},{40,56},{96,112},{104,120},{160,176},{168,184},{224,240},{... | collective-permute-start | bytes 294920 | tf_op jit(solution)/shard_map/ppermute | solution.py:328
  144.4 0.7 collective-permute-start.19
  145.1 5.7 %all-to-all-start.5 = ((bf16[4,192,256]{2,1,0:T(8,128)(2,1)}), bf16[4,192,256]{2,1,0:T(8,128)(2,1)S(1)}, u32[]{:S(2)}, u32[]{:S(2)}) async-start(bf16[4,192,256]{2,1,0:T(8,128)(2,1)} %pad_maximum_fusion), calls=%async_computation.5 | async-start | bytes 786432 | tf_op jit(solution)/shard_map/all_to_all | solution.py:382
  150.8 0.1 add_convert_fusion.5
  150.8 5.9 %all-to-all-done.5 = bf16[4,192,256]{2,1,0:T(8,128)(2,1)S(1)} async-done(((bf16[4,192,256]{2,1,0:T(8,128)(2,1)}), bf16[4,192,256]{2,1,0:T(8,128)(2,1)S(1)}, u32[]{:S(2)}, u32[]{:S(2)}) %all-to-all-start.5) | async-done | bytes 393248 | tf_op jit(solution)/shard_map/all_to_all | solution.py:382
  156.7 0.1 broadcast_select_fusion.1
  156.8 0.7 collective-permute-start.20
  157.5 0.7 collective-permute-start.22
  158.2 10.7 %collective-permute-start.21 = (bf16[192,256]{1,0:T(8,128)(2,1)S(1)}, bf16[192,256]{1,0:T(8,128)(2,1)S(1)}, u32[]{:S(2)}, u32[]{:S(2)}) collective-permute-start(bf16[192,256]{1,0:T(8,128)(2,1)S(1)} %broadcast_select_fusion.2), channel_id=1, source_target_pairs={{0,225},{1,2},{2,35},{3,68},{4,101},{5,134},{6,167},{7,192},{8,0},... | collective-permute-start | bytes 294920 | tf_op jit(solution)/shard_map/ppermute | solution.py:432
  168.8 1.9 %collective-permute-start.23 = (bf16[192,256]{1,0:T(8,128)(2,1)S(1)}, bf16[192,256]{1,0:T(8,128)(2,1)S(1)}, u32[]{:S(2)}, u32[]{:S(2)}) collective-permute-start(bf16[192,256]{1,0:T(8,128)(2,1)S(1)} %get-tuple-element.61), channel_id=1, source_target_pairs={{0,0},{1,33},{2,66},{3,99},{4,132},{5,165},{6,198},{7,231},{8,225}... | collective-permute-start | bytes 294920 | tf_op jit(solution)/shard_map/ppermute | solution.py:433
  170.8 0.2 collective-permute-done.21
  171.0 9.4 %collective-permute-done.23 = bf16[192,256]{1,0:T(8,128)(2,1)S(1)} collective-permute-done((bf16[192,256]{1,0:T(8,128)(2,1)S(1)}, bf16[192,256]{1,0:T(8,128)(2,1)S(1)}, u32[]{:S(2)}, u32[]{:S(2)}) %collective-permute-start.23) | collective-permute-done | bytes 98336 | tf_op jit(solution)/shard_map/ppermute | solution.py:433
  180.5 0.8 maximum_convert_fusion
  (29 shorter events, 0.1 us)
Async XLA Ops:
  5.9 36.2 %collective-permute-start.2 = (bf16[3,1024,256]{2,1,0:T(8,128)(2,1)}, bf16[3,1024,256]{2,1,0:T(8,128)(2,1)S(1)}, u32[]{:S(2)}, u32[]{:S(2)}) collective-permute-start(bf16[3,1024,256]{2,1,0:T(8,128)(2,1)} %get-tuple-element.33), channel_id=1, source_target_pairs={{0,8},{8,0},{16,24},{24,16},{32,40},{40,32},{48,56},{56,48},{64,72... | collective-permute-start | bytes 4718600 | tf_op jit(solution)/shard_map/ppermute | solution.py:371
  5.9 42.3 %collective-permute-start = (bf16[1024,768]{1,0:T(8,128)(2,1)}, bf16[1024,768]{1,0:T(8,128)(2,1)S(1)}, u32[]{:S(2)}, u32[]{:S(2)}) collective-permute-start(bf16[1024,768]{1,0:T(8,128)(2,1)} %refs_0_.2), channel_id=1, source_target_pairs={{0,1},{1,2},{2,3},{3,4},{4,5},{5,6},{6,7},{7,0},{8,9},{9,10},{10,1... | collective-permute-start | bytes 4718600 | tf_op jit(solution)/shard_map/ppermute | solution.py:368
  7.9 40.3 %collective-permute-start.1 = (bf16[1024,768]{1,0:T(8,128)(2,1)}, bf16[1024,768]{1,0:T(8,128)(2,1)S(1)}, u32[]{:S(2)}, u32[]{:S(2)}) collective-permute-start(bf16[1024,768]{1,0:T(8,128)(2,1)} %refs_0_.2), channel_id=1, source_target_pairs={{0,7},{1,0},{2,1},{3,2},{4,3},{5,4},{6,5},{7,6},{8,15},{9,8},{10,9... | collective-permute-start | bytes 4718600 | tf_op jit(solution)/shard_map/ppermute | solution.py:368
  42.2 1.2 copy-start.3
  48.2 11.0 %copy-start = (bf16[1024,768]{1,0:T(8,128)(2,1)}, bf16[1024,768]{1,0:T(8,128)(2,1)S(1)}, u32[]{:S(2)}) copy-start(bf16[1024,768]{1,0:T(8,128)(2,1)S(1)} %collective-permute-done.refs_2_.refs_0_) | copy-start | bytes 4718596
  48.3 11.0 %copy-start.1 = (bf16[1024,768]{1,0:T(8,128)(2,1)}, bf16[1024,768]{1,0:T(8,128)(2,1)S(1)}, u32[]{:S(2)}) copy-start(bf16[1024,768]{1,0:T(8,128)(2,1)S(1)} %collective-permute-done.1.refs_4_.refs_2_) | copy-start | bytes 4718596
  48.3 11.0 %collective-permute-start.3 = (bf16[1024,768]{1,0:T(8,128)(2,1)S(1)}, bf16[1024,768]{1,0:T(8,128)(2,1)S(1)}, u32[]{:S(2)}, u32[]{:S(2)}) collective-permute-start(bf16[1024,768]{1,0:T(8,128)(2,1)S(1)} %collective-permute-done.refs_2_.refs_0_), channel_id=1, source_target_pairs={{0,8},{8,0},{16,24},{24,16},{32,40},{40,32},{48,56},{56,48},{64,72... | collective-permute-start | bytes 4718600 | tf_op jit(solution)/shard_map/ppermute | solution.py:371
  48.4 10.9 %collective-permute-start.4 = (bf16[1024,768]{1,0:T(8,128)(2,1)S(1)}, bf16[1024,768]{1,0:T(8,128)(2,1)}, u32[]{:S(2)}, u32[]{:S(2)}) collective-permute-start(bf16[1024,768]{1,0:T(8,128)(2,1)S(1)} %collective-permute-done.1.refs_4_.refs_2_), channel_id=1, source_target_pairs={{0,8},{8,0},{16,24},{24,16},{32,40},{40,32},{48,56},{56,48},{64,72... | collective-permute-start | bytes 4718600 | tf_op jit(solution)/shard_map/ppermute | solution.py:371
  48.9 10.4 %collective-permute-start.7 = (bf16[1024,768]{1,0:T(8,128)(2,1)}, bf16[1024,768]{1,0:T(8,128)(2,1)}, u32[]{:S(2)}, u32[]{:S(2)}) collective-permute-start(bf16[1024,768]{1,0:T(8,128)(2,1)} %refs_0_.2), channel_id=1, source_target_pairs={{0,8},{8,0},{16,24},{24,16},{32,40},{40,32},{48,56},{56,48},{64,72... | collective-permute-start | bytes 4718600 | tf_op jit(solution)/shard_map/ppermute | solution.py:371
  49.0 27.0 %collective-permute-start.5 = (bf16[2,1024,256]{2,1,0:T(8,128)(2,1)}, bf16[2,1024,256]{2,1,0:T(8,128)(2,1)}, u32[]{:S(2)}, u32[]{:S(2)}) collective-permute-start(bf16[2,1024,256]{2,1,0:T(8,128)(2,1)} %value_gradient.1.refs_6_), channel_id=1, source_target_pairs={{0,1},{1,2},{2,3},{3,4},{4,5},{5,6},{6,7},{7,0},{8,9},{9,10},{10,1... | collective-permute-start | bytes 3145736 | tf_op jit(solution)/shard_map/ppermute | solution.py:368
  49.0 27.0 %collective-permute-start.6 = (bf16[2,1024,256]{2,1,0:T(8,128)(2,1)}, bf16[2,1024,256]{2,1,0:T(8,128)(2,1)}, u32[]{:S(2)}, u32[]{:S(2)}) collective-permute-start(bf16[2,1024,256]{2,1,0:T(8,128)(2,1)} %value_gradient.1.refs_6_), channel_id=1, source_target_pairs={{0,7},{1,0},{2,1},{3,2},{4,3},{5,4},{6,5},{7,6},{8,15},{9,8},{10,9... | collective-permute-start | bytes 3145736 | tf_op jit(solution)/shard_map/ppermute | solution.py:368
  59.3 1.2 copy-start.2
  67.3 20.3 %all-to-all-start.2 = ((bf16[4,3,192,256]{3,2,1,0:T(8,128)(2,1)}), bf16[4,3,192,256]{3,2,1,0:T(8,128)(2,1)S(1)}, u32[]{:S(2)}, u32[]{:S(2)}) async-start(bf16[4,3,192,256]{3,2,1,0:T(8,128)(2,1)} %weight_terms.3), calls=%async_computation.2 | async-start | bytes 2359296 | tf_op jit(solution)/shard_map/all_to_all | solution.py:382
  76.0 26.1 %collective-permute-start.8 = (bf16[2,1024,256]{2,1,0:T(8,128)(2,1)}, bf16[2,1024,256]{2,1,0:T(8,128)(2,1)S(1)}, u32[]{:S(2)}, u32[]{:S(2)}) collective-permute-start(bf16[2,1024,256]{2,1,0:T(8,128)(2,1)} %collective-permute-done.5.refs_5_), channel_id=1, source_target_pairs={{0,1},{1,2},{2,3},{3,4},{4,5},{5,6},{6,7},{7,0},{8,9},{9,10},{10,1... | collective-permute-start | bytes 3145736 | tf_op jit(solution)/shard_map/ppermute | solution.py:368
  77.2 24.9 %collective-permute-start.9 = (bf16[2,1024,256]{2,1,0:T(8,128)(2,1)}, bf16[2,1024,256]{2,1,0:T(8,128)(2,1)S(1)}, u32[]{:S(2)}, u32[]{:S(2)}) collective-permute-start(bf16[2,1024,256]{2,1,0:T(8,128)(2,1)} %collective-permute-done.6.refs_4_), channel_id=1, source_target_pairs={{0,7},{1,0},{2,1},{3,2},{4,3},{5,4},{6,5},{7,6},{8,15},{9,8},{10,9... | collective-permute-start | bytes 3145736 | tf_op jit(solution)/shard_map/ppermute | solution.py:368
  87.6 23.4 %all-to-all-start.3 = ((bf16[4,2,192,256]{3,2,1,0:T(8,128)(2,1)}), bf16[4,2,192,256]{3,2,1,0:T(8,128)(2,1)}, u32[]{:S(2)}, u32[]{:S(2)}) async-start(bf16[4,2,192,256]{3,2,1,0:T(8,128)(2,1)} %weight_terms.4), calls=%async_computation.3 | async-start | bytes 1572864 | tf_op jit(solution)/shard_map/all_to_all | solution.py:382
  102.1 1.0 copy-start.4
  102.1 1.3 copy-start.5
  103.5 22.5 %collective-permute-start.10 = (bf16[2,1024,256]{2,1,0:T(8,128)(2,1)S(1)}, bf16[2,1024,256]{2,1,0:T(8,128)(2,1)}, u32[]{:S(2)}, u32[]{:S(2)}) collective-permute-start(bf16[2,1024,256]{2,1,0:T(8,128)(2,1)S(1)} %broadcast_select_fusion), channel_id=1, source_target_pairs={{0,1},{1,2},{2,3},{3,4},{4,5},{5,6},{6,7},{7,0},{8,15},{9,8},{10,9... | collective-permute-start | bytes 3145736 | tf_op jit(solution)/shard_map/ppermute | solution.py:411
  111.0 20.0 %all-to-all-start.4 = ((bf16[4,2,192,256]{3,2,1,0:T(8,128)(2,1)}), bf16[4,2,192,256]{3,2,1,0:T(8,128)(2,1)S(1)}, u32[]{:S(2)}, u32[]{:S(2)}) async-start(bf16[4,2,192,256]{3,2,1,0:T(8,128)(2,1)} %weight_terms.5), calls=%async_computation.4 | async-start | bytes 1572864 | tf_op jit(solution)/shard_map/all_to_all | solution.py:382
  116.8 14.3 %collective-permute-start.14 = (bf16[192,256]{1,0:T(8,128)(2,1)S(1)}, bf16[192,256]{1,0:T(8,128)(2,1)S(1)}, u32[]{:S(2)}, u32[]{:S(2)}) collective-permute-start(bf16[192,256]{1,0:T(8,128)(2,1)S(1)} %get-tuple-element.68), channel_id=1, source_target_pairs={{0,32},{8,40},{32,0},{40,8},{48,16},{56,24},{64,96},{72,104},{96,6... | collective-permute-start | bytes 294920 | tf_op jit(solution)/shard_map/ppermute | solution.py:328
  118.7 12.3 %collective-permute-start.15 = (bf16[192,256]{1,0:T(8,128)(2,1)S(1)}, bf16[192,256]{1,0:T(8,128)(2,1)S(1)}, u32[]{:S(2)}, u32[]{:S(2)}) collective-permute-start(bf16[192,256]{1,0:T(8,128)(2,1)S(1)} %get-tuple-element.67), channel_id=1, source_target_pairs={{0,16},{8,24},{16,32},{24,40},{48,0},{56,8},{64,80},{72,88},{80,96... | collective-permute-start | bytes 294920 | tf_op jit(solution)/shard_map/ppermute | solution.py:328
  120.0 11.0 %collective-permute-start.16 = (bf16[192,256]{1,0:T(8,128)(2,1)S(1)}, bf16[192,256]{1,0:T(8,128)(2,1)S(1)}, u32[]{:S(2)}, u32[]{:S(2)}) collective-permute-start(bf16[192,256]{1,0:T(8,128)(2,1)S(1)} %get-tuple-element.66), channel_id=1, source_target_pairs={{16,0},{24,8},{32,16},{40,24},{48,32},{56,40},{80,64},{88,72},{96,... | collective-permute-start | bytes 294920 | tf_op jit(solution)/shard_map/ppermute | solution.py:328
  131.1 8.1 %copy-start.6 = (bf16[192,256]{1,0:T(8,128)(2,1)S(1)}, bf16[192,256]{1,0:T(8,128)(2,1)}, u32[]{:S(2)}) copy-start(bf16[192,256]{1,0:T(8,128)(2,1)} %get-tuple-element.51) | copy-start | bytes 294916
  131.2 6.4 %collective-permute-start.11 = (bf16[192,256]{1,0:T(8,128)(2,1)}, bf16[192,256]{1,0:T(8,128)(2,1)S(1)}, u32[]{:S(2)}, u32[]{:S(2)}) collective-permute-start(bf16[192,256]{1,0:T(8,128)(2,1)} %get-tuple-element.52), channel_id=1, source_target_pairs={{0,128},{8,136},{16,144},{24,152},{32,160},{40,168},{48,176},{56,1... | collective-permute-start | bytes 294920 | tf_op jit(solution)/shard_map/ppermute | solution.py:314
  132.6 5.5 %collective-permute-start.12 = (bf16[192,256]{1,0:T(8,128)(2,1)}, bf16[192,256]{1,0:T(8,128)(2,1)S(1)}, u32[]{:S(2)}, u32[]{:S(2)}) collective-permute-start(bf16[192,256]{1,0:T(8,128)(2,1)} %get-tuple-element.53), channel_id=1, source_target_pairs={{0,64},{8,72},{16,80},{24,88},{32,96},{40,104},{48,112},{56,120},{... | collective-permute-start | bytes 294920 | tf_op jit(solution)/shard_map/ppermute | solution.py:314
  134.3 4.8 %collective-permute-start.13 = (bf16[192,256]{1,0:T(8,128)(2,1)}, bf16[192,256]{1,0:T(8,128)(2,1)S(1)}, u32[]{:S(2)}, u32[]{:S(2)}) collective-permute-start(bf16[192,256]{1,0:T(8,128)(2,1)} %get-tuple-element.54), channel_id=1, source_target_pairs={{0,192},{8,200},{16,208},{24,216},{32,224},{40,232},{48,240},{56,2... | collective-permute-start | bytes 294920 | tf_op jit(solution)/shard_map/ppermute | solution.py:314
  139.2 11.6 %collective-permute-start.17 = (bf16[192,256]{1,0:T(8,128)(2,1)S(1)}, bf16[192,256]{1,0:T(8,128)(2,1)S(1)}, u32[]{:S(2)}, u32[]{:S(2)}) collective-permute-start(bf16[192,256]{1,0:T(8,128)(2,1)S(1)} %add_convert_fusion.6), channel_id=1, source_target_pairs={{16,48},{24,56},{80,112},{88,120},{144,176},{152,184},{208,240},{2... | collective-permute-start | bytes 294920 | tf_op jit(solution)/shard_map/ppermute | solution.py:328
  139.8 10.9 %collective-permute-start.18 = (bf16[192,256]{1,0:T(8,128)(2,1)S(1)}, bf16[192,256]{1,0:T(8,128)(2,1)S(1)}, u32[]{:S(2)}, u32[]{:S(2)}) collective-permute-start(bf16[192,256]{1,0:T(8,128)(2,1)S(1)} %add_convert_fusion.6), channel_id=1, source_target_pairs={{32,48},{40,56},{96,112},{104,120},{160,176},{168,184},{224,240},{... | collective-permute-start | bytes 294920 | tf_op jit(solution)/shard_map/ppermute | solution.py:328
  144.4 6.4 %collective-permute-start.19 = (bf16[192,256]{1,0:T(8,128)(2,1)S(1)}, bf16[192,256]{1,0:T(8,128)(2,1)S(1)}, u32[]{:S(2)}, u32[]{:S(2)}) collective-permute-start(bf16[192,256]{1,0:T(8,128)(2,1)S(1)} %add_convert_fusion.6), channel_id=1, source_target_pairs={{0,48},{8,56},{64,112},{72,120},{128,176},{136,184},{192,240},{200... | collective-permute-start | bytes 294920 | tf_op jit(solution)/shard_map/ppermute | solution.py:328
  145.1 11.6 %all-to-all-start.5 = ((bf16[4,192,256]{2,1,0:T(8,128)(2,1)}), bf16[4,192,256]{2,1,0:T(8,128)(2,1)S(1)}, u32[]{:S(2)}, u32[]{:S(2)}) async-start(bf16[4,192,256]{2,1,0:T(8,128)(2,1)} %pad_maximum_fusion), calls=%async_computation.5 | async-start | bytes 786432 | tf_op jit(solution)/shard_map/all_to_all | solution.py:382
  156.8 14.0 %collective-permute-start.20 = (bf16[192,256]{1,0:T(8,128)(2,1)S(1)}, bf16[192,256]{1,0:T(8,128)(2,1)S(1)}, u32[]{:S(2)}, u32[]{:S(2)}) collective-permute-start(bf16[192,256]{1,0:T(8,128)(2,1)S(1)} %add_convert_fusion.5), channel_id=1, source_target_pairs={{56,227},{57,4},{58,37},{59,70},{60,103},{61,128},{62,161},{63,194... | collective-permute-start | bytes 294920 | tf_op jit(solution)/shard_map/ppermute | solution.py:436
  157.5 13.3 %collective-permute-start.22 = (bf16[192,256]{1,0:T(8,128)(2,1)S(1)}, bf16[192,256]{1,0:T(8,128)(2,1)S(1)}, u32[]{:S(2)}, u32[]{:S(2)}) collective-permute-start(bf16[192,256]{1,0:T(8,128)(2,1)S(1)} %add_convert_fusion.5), channel_id=1, source_target_pairs={{48,37},{49,70},{50,103},{51,128},{52,161},{53,194},{54,227},{55,4... | collective-permute-start | bytes 294920 | tf_op jit(solution)/shard_map/ppermute | solution.py:437
  158.2 12.9 %collective-permute-start.21 = (bf16[192,256]{1,0:T(8,128)(2,1)S(1)}, bf16[192,256]{1,0:T(8,128)(2,1)S(1)}, u32[]{:S(2)}, u32[]{:S(2)}) collective-permute-start(bf16[192,256]{1,0:T(8,128)(2,1)S(1)} %broadcast_select_fusion.2), channel_id=1, source_target_pairs={{0,225},{1,2},{2,35},{3,68},{4,101},{5,134},{6,167},{7,192},{8,0},... | collective-permute-start | bytes 294920 | tf_op jit(solution)/shard_map/ppermute | solution.py:432
  168.8 11.6 %collective-permute-start.23 = (bf16[192,256]{1,0:T(8,128)(2,1)S(1)}, bf16[192,256]{1,0:T(8,128)(2,1)S(1)}, u32[]{:S(2)}, u32[]{:S(2)}) collective-permute-start(bf16[192,256]{1,0:T(8,128)(2,1)S(1)} %get-tuple-element.61), channel_id=1, source_target_pairs={{0,0},{1,33},{2,66},{3,99},{4,132},{5,165},{6,198},{7,231},{8,225}... | collective-permute-start | bytes 294920 | tf_op jit(solution)/shard_map/ppermute | solution.py:433

commit v3 on v2

--- a/solution.py
+++ b/solution.py
@@ -328,20 +328,37 @@
     return [lax.ppermute(chosen[d], "seq", shift_to(axis, targets, d)) for d in (2, 1, 3)]
 
 
-HELD_AT_X = {0: ((-1, 1),) * 2, 1: ((1, -1),) * 2, 2: ((-1, 2),) * 2, 3: ((1, -2),) * 2}
-HELD_AT_Y = {0: ((0, 0),) * 2, 1: ((-1, 0),) * 2, 2: ((1, 0),) * 2, 3: ((1, -3), (-1, 3))}
+HELD_AT_X = ((2, 1), (-2, -1), (3, 2), (-3, -2))
+HELD_AT_Y = ((0, 0), (1, 0), (-1, 0), (4, None))
 LAST = 3
+LAST_STEP = (-3, 3)
+
+
+def to_x(d, nz):
+    return [
+        (seq_index(x, y, c) * nz + m, seq_index(x + d, y, c) * nz + (m + HELD_AT_X[(x + d) % NX][1]) % nz)
+        for x, y, c in CHIPS
+        for m in range(nz)
+    ]
+
+
+def to_last(d, nz):
+    return [
+        (seq_index(x, y, c) * nz + m, seq_index(x, LAST, c) * nz + (m + LAST_STEP[c]) % nz)
+        for x, y, c in CHIPS
+        for m in range(nz)
+        if (y + d) % NY == LAST
+    ]
 
 
 def owners(turn, nz):
-    pairs = ([], [])
+    pairs = []
     for x, y, c in CHIPS:
         by_x = c == turn
         r = y if by_x else x
-        di, dj = HELD_AT_X[x][c] if by_x else HELD_AT_Y[y][c]
-        for m in range(nz):
-            i, j = (m + di) % nz, (m + dj) % nz
-            pairs[not by_x and y == LAST].append((seq_index(x, y, c) * nz + m, (4 * i + r) * nz + j))
+        d = HELD_AT_X[x][0] if by_x else HELD_AT_Y[y][0]
+        for j in range(nz):
+            pairs.append((seq_index(x, y, c) * nz + j, (4 * ((j - d) % nz) + r) * nz + j))
     return pairs
 
 
@@ -402,43 +419,38 @@
     u1, d1 = tie(u1, d1, t0)[:2]
     u2, d2 = go(u1, up), go(d1, down)
     t1 = terms(near, [d1, u1], [(0, 0), (1, 1)])
-    p0 = total(list(p0))
+    p0 = total(list(tie(p0, t1)[0]))
     p1 = exchange("y", t1)
     c0 = choose([p0[0], p0[1], p0[2]], [0, 1, 2], y)
     y0 = send_to("y", c0, [0, 1, 2])
 
-    u2, d2 = tie(u2, d2, t1, *c0)[:2]
+    u2, d2, *y0 = tie(u2, d2, *y0, t1)[:5]
     v3 = lax.ppermute(jnp.where(c == 0, u2, d2), both, apart)
     t2 = terms(near, [d2, u2], [(0, 0), (1, 1)])
     p1 = total(list(p1))
     p2 = exchange("y", t2)
 
-    v3 = tie(v3, t2, p1)[0]
+    v3, p1, r0 = tie(v3, p1, total([c0[0]] + y0), t2)[:3]
     q3 = last_terms(at_x, near, v3, weight_scale)
     x3 = send_all("x", q3)
-    *y0, p2, _ = tie(*y0, p2, q3[0])
-    held = jnp.concatenate([p1, total(list(p2))], 0)
-    x2 = exchange("x", held)
-    r0 = total([c0[0]] + y0)
+    p2 = total(list(tie(p2, q3[0])[0]))
+    held = choose([p1[0], p1[1], p2[0], p2[1]], [0, 1, 2, 3], x)
+    x2 = [lax.ppermute(held[d], both, to_x(d, n_z)) for d in (0, 2, 1, 3)]
     p3 = total([q3[0]] + x3)
 
-    p3 = tie(p3, held)[0]
-    y3 = send_to("y", [p3] * 4, [LAST])
-    held_x = total(list(x2))
+    p3 = tie(p3, *held)[0]
+    y3 = [lax.ppermute(p3, both, to_last(d, n_z)) for d in (0, 2, 1, 3)]
+    held_x = total(x2)
     first = jnp.where(c == 0, held_x, r0)
     second = jnp.where(c == 0, r0, held_x)
-    early0, late0 = owners(0, n_z)
-    early1, late1 = owners(1, n_z)
-    early_first = lax.ppermute(first, both, early0)
-    early_second = lax.ppermute(second, both, early1)
-    r3 = total([p3] + y3)
-    r3 = tie(r3, first, second)[0]
-    late_first = lax.ppermute(r3, both, late0)
-    late_second = lax.ppermute(r3, both, late1)
+    r3 = total(y3)
+    last = y == LAST
+    first = jnp.where((c == 1) & last, r3, first)
+    second = jnp.where((c == 0) & last, r3, second)
+    first = lax.ppermute(first, both, owners(0, n_z))
+    second = lax.ppermute(second, both, owners(1, n_z))
 
     away = lax.rem(z - s // 4 + n_z, n_z)
-    first = jnp.where(away == 4, late_first, early_first)
-    second = jnp.where(away == 4, late_second, early_second)
     by_x = (away == 2) | (away == 3) | (away == 5) | (away == 6)
     left = jnp.where(by_x, first, second)
     right = jnp.where(by_x, second, first)

time: 182 us -> 174 us (0.956)
  the two profiles are of different devices: /device:TPU:18 before, /device:TPU:20 now
where the time goes in v3:
time: 174 us; the launch traced here: 173 us
  starting transfers between devices  79.8 us (46%)
  Pallas kernels  42.1 us (24%)
  blocking collectives  27.4 us (16%)
  waiting for transfers between devices  16.7 us (10%)
  other arithmetic  3.34 us (2%)
  local copies, waits for them, and re-layouts  3.22 us (2%)
    pallas_call x3, Pallas kernels, weight_terms(): pl.pallas_call(functools.partial(terms_kernel, scale, blocks, len(xs), le...  18 us
    all_to_all x3, starting transfers between devices, exchange(): return lax.all_to_all(pieces, 'seq', 0, 0, axis_index_groups=groups[axis])  16.4 us
    all_to_all x1, blocking collectives, per_device(): sums = lax.all_to_all(running_sums(spread), 'seq', 0, 0)  14.8 us
    ppermute x1, starting transfers between devices, per_device(): second = lax.ppermute(second, both, owners(1, n_z))  12.7 us
    all_to_all x1, blocking collectives, per_device(): lax.all_to_all(totals.reshape(n_seq, *totals.shape[2:]), 'seq', 0, 0)  12.6 us
    ppermute x6, starting transfers between devices, go(): return lax.ppermute(array, 'head', way)  12.5 us
    ppermute x4, starting transfers between devices, per_device(): x2 = [lax.ppermute(held[d], both, to_x(d, n_z)) for d in (0, 2, 1, 3)]  10.5 us
    ppermute x3, starting transfers between devices, send_to(): lax.ppermute(chosen[d], 'seq', shift_to(axis, targets, d))  9.86 us
  transfers between devices with their start and end apart: 30, of which 7 were waited for; matrix products, arithmetic and copies ran while one was open for 1% of the time, Pallas kernels for 21%

profile of v3, /device:TPU:20, one launch (start us, length us, event | category | flops | bytes accessed | tf_op | source)
XLA Modules:
  0.0 173.5 jit_solution(12101060782913468490)
XLA Ops:
  0.6 5.3 %states.1 = (f32[4,128,128]{2,1,0:T(8,128)}, f32[4,128,128]{2,1,0:T(8,128)}, bf16[4,8,2,16,128]{4,3,2,1,0:T(8,128)(2,1)}, bf16[3,1024,256]{2,1,0:T(8,128)(2,1)}) custom-call(s32[1]{0:T(128)} %bitcast._, bf16[1024,512]{1,0:T(8,128)(2,1)} %q_ref.3, bf16[1024,512]{1,0:T(8,128)(2,1)} %k_ref.3, bf16[1024,512]{1,0:T(8,128)(2,1)} %v_ref.3, bf16[1024,512]{1,0:T(8,128)(2,1)} %o_ref.3), custom_call_target="tpu_custom_call" | custom-call | flops 1 | bytes 1 | tf_op jit(solution)/shard_map/states/pallas_call | solution.py:70
  5.9 0.0 collective-permute-start.2
  5.9 2.0 %collective-permute-start = (bf16[1024,768]{1,0:T(8,128)(2,1)}, bf16[1024,768]{1,0:T(8,128)(2,1)S(1)}, u32[]{:S(2)}, u32[]{:S(2)}) collective-permute-start(bf16[1024,768]{1,0:T(8,128)(2,1)} %refs_0_.2), channel_id=1, source_target_pairs={{0,1},{1,2},{2,3},{3,4},{4,5},{5,6},{6,7},{7,0},{8,9},{9,10},{10,1... | collective-permute-start | bytes 4718600 | tf_op jit(solution)/shard_map/ppermute | solution.py:385
  7.9 4.0 %collective-permute-start.1 = (bf16[1024,768]{1,0:T(8,128)(2,1)}, bf16[1024,768]{1,0:T(8,128)(2,1)S(1)}, u32[]{:S(2)}, u32[]{:S(2)}) collective-permute-start(bf16[1024,768]{1,0:T(8,128)(2,1)} %refs_0_.2), channel_id=1, source_target_pairs={{0,7},{1,0},{2,1},{3,2},{4,3},{5,4},{6,5},{7,6},{8,15},{9,8},{10,9... | collective-permute-start | bytes 4718600 | tf_op jit(solution)/shard_map/ppermute | solution.py:385
  11.9 12.6 %all_to_all.25.in_ref = bf16[32,2,16,128]{3,2,1,0:T(8,128)(2,1)} all-to-all(bf16[32,2,16,128]{3,2,1,0:T(8,128)(2,1)} %bitcast.47), channel_id=1, replica_groups=mesh['seq'=32,'head'=8] {'seq'}, dimensions={0} | all-to-all | bytes 524288 | tf_op jit(solution)/shard_map/all_to_all | solution.py:403
  24.5 1.7 %running_sums.1 = bf16[32,3,16,128]{3,2,1,0:T(8,128)(2,1)} custom-call(bf16[32,2,16,128]{3,2,1,0:T(8,128)(2,1)} %all_to_all.25.in_ref), custom_call_target="tpu_custom_call" | custom-call | flops 1 | bytes 1 | tf_op jit(solution)/shard_map/running_sums/pallas_call | solution.py:108
  26.3 14.8 %all_to_all.26 = bf16[32,3,16,128]{3,2,1,0:T(8,128)(2,1)} all-to-all(bf16[32,3,16,128]{3,2,1,0:T(8,128)(2,1)} %running_sums.1), channel_id=1, replica_groups=mesh['seq'=32,'head'=8] {'seq'}, dimensions={0} | all-to-all | bytes 786432 | tf_op jit(solution)/shard_map/all_to_all | solution.py:404
  41.1 0.0 collective-permute-done.2.refs_3_.refs_4_.refs_5_
  41.1 1.2 copy-done.3
  42.3 4.9 %value_gradient.1.refs_6_ = bf16[2,1024,256]{2,1,0:T(8,128)(2,1)} custom-call(s32[1]{0:T(128)} %bitcast._, bf16[1024,512]{1,0:T(8,128)(2,1)} %q_ref.3, bf16[1024,512]{1,0:T(8,128)(2,1)} %k_ref.3, bf16[1024,512]{1,0:T(8,128)(2,1)} %o_ref.3, bf16[3,1024,256]{2,1,0:T(8,128)(2,1)} %copy-done.3, bf16[3,1024,256]{2,1,0:T(8,128)(2,1)} %copy-done.3, ...), custom_call_target="tpu_custom_call" | custom-call | flops 1 | bytes 1 | tf_op jit(solution)/shard_map/value_gradient/pallas_call | solution.py:166
  47.2 0.0 collective-permute-done.1.refs_4_.refs_2_
  47.2 0.3 collective-permute-start.3
  47.5 0.3 collective-permute-start.4
  47.8 0.2 collective-permute-start.7
  48.0 0.0 collective-permute-start.5
  48.0 3.2 %collective-permute-start.6 = (bf16[2,1024,256]{2,1,0:T(8,128)(2,1)}, bf16[2,1024,256]{2,1,0:T(8,128)(2,1)}, u32[]{:S(2)}, u32[]{:S(2)}) collective-permute-start(bf16[2,1024,256]{2,1,0:T(8,128)(2,1)} %value_gradient.1.refs_6_), channel_id=1, source_target_pairs={{0,7},{1,0},{2,1},{3,2},{4,3},{5,4},{6,5},{7,6},{8,15},{9,8},{10,9... | collective-permute-start | bytes 3145736 | tf_op jit(solution)/shard_map/ppermute | solution.py:385
  51.2 7.0 %query_key_gradients.1 = (bf16[1024,512]{1,0:T(8,128)(2,1)}, bf16[1024,512]{1,0:T(8,128)(2,1)}) custom-call(bf16[1024,512]{1,0:T(8,128)(2,1)} %q_ref.3, bf16[1024,512]{1,0:T(8,128)(2,1)} %k_ref.3, bf16[1024,512]{1,0:T(8,128)(2,1)} %v_ref.3, bf16[1024,512]{1,0:T(8,128)(2,1)} %o_ref.3, bf16[4,8,3,16,128]{4,3,2,1,0:T(8,128)(2,1)} %bitcast.45, ...), custom_call_target="tpu_custom_call" | custom-call | flops 1 | bytes 1 | tf_op jit(solution)/shard_map/query_key_gradients/pallas_call | solution.py:203
  58.3 0.0 collective-permute-done.4.refs_5_.refs_3_
  58.3 1.1 copy-done.2
  59.4 6.9 %weight_terms.3 = bf16[4,3,192,256]{3,2,1,0:T(8,128)(2,1)} custom-call(bf16[1024,768]{1,0:T(8,128)(2,1)} %refs_0_.2, bf16[1024,768]{1,0:T(8,128)(2,1)} %collective-permute-done.7.refs_1_, bf16[1024,768]{1,0:T(8,128)(2,1)} %copy-done, bf16[1024,768]{1,0:T(8,128)(2,1)} %copy-done.2, bf16[1024,768]{1,0:T(8,128)(2,1)} %copy-done.1, ...), custom_call_target="tpu_custom_call" | custom-call | flops 1 | bytes 1 | tf_op jit(solution)/shard_map/weight_terms/pallas_call | solution.py:232
  66.3 5.8 %all-to-all-start.2 = ((bf16[4,3,192,256]{3,2,1,0:T(8,128)(2,1)}), bf16[4,3,192,256]{3,2,1,0:T(8,128)(2,1)S(1)}, u32[]{:S(2)}, u32[]{:S(2)}) async-start(bf16[4,3,192,256]{3,2,1,0:T(8,128)(2,1)} %weight_terms.3), calls=%async_computation.2 | async-start | bytes 2359296 | tf_op jit(solution)/shard_map/all_to_all | solution.py:399
  72.1 2.8 %collective-permute-done.5.refs_5_ = bf16[2,1024,256]{2,1,0:T(8,128)(2,1)} collective-permute-done((bf16[2,1024,256]{2,1,0:T(8,128)(2,1)}, bf16[2,1024,256]{2,1,0:T(8,128)(2,1)}, u32[]{:S(2)}, u32[]{:S(2)}) %collective-permute-start.5) | collective-permute-done | bytes 1048608 | tf_op jit(solution)/shard_map/ppermute | solution.py:385
  74.9 2.3 %collective-permute-start.8 = (bf16[2,1024,256]{2,1,0:T(8,128)(2,1)}, bf16[2,1024,256]{2,1,0:T(8,128)(2,1)S(1)}, u32[]{:S(2)}, u32[]{:S(2)}) collective-permute-start(bf16[2,1024,256]{2,1,0:T(8,128)(2,1)} %collective-permute-done.5.refs_5_), channel_id=1, source_target_pairs={{0,1},{1,2},{2,3},{3,4},{4,5},{5,6},{6,7},{7,0},{8,9},{9,10},{10,1... | collective-permute-start | bytes 3145736 | tf_op jit(solution)/shard_map/ppermute | solution.py:385
  77.2 1.0 collective-permute-start.9
  78.2 5.6 %weight_terms.4 = bf16[4,2,192,256]{3,2,1,0:T(8,128)(2,1)} custom-call(bf16[1024,768]{1,0:T(8,128)(2,1)} %copy-done, bf16[1024,768]{1,0:T(8,128)(2,1)} %copy-done.2, bf16[1024,768]{1,0:T(8,128)(2,1)} %copy-done.1, bf16[1024,768]{1,0:T(8,128)(2,1)} %collective-permute-done.4.refs_5_.refs_3_, bf16[2,1024,256]{2,1,0:T(8,128)(2,1)} %collective-permute-done.6.refs_4_, ...), custom_call_target="tpu_custom_call" | custom-call | flops 1 | bytes 1 | tf_op jit(solution)/shard_map/weight_terms/pallas_call | solution.py:232
  83.8 2.2 %all-to-all-done.2 = bf16[4,3,192,256]{3,2,1,0:T(8,128)(2,1)S(1)} async-done(((bf16[4,3,192,256]{3,2,1,0:T(8,128)(2,1)}), bf16[4,3,192,256]{3,2,1,0:T(8,128)(2,1)S(1)}, u32[]{:S(2)}, u32[]{:S(2)}) %all-to-all-start.2) | async-done | bytes 1179680 | tf_op jit(solution)/shard_map/all_to_all | solution.py:399
  86.0 0.1 add_convert_fusion
  86.1 0.0 copy-start.6
  86.1 0.7 copy-done.6
  86.9 4.0 %collective-permute-start.10 = (bf16[192,256]{1,0:T(8,128)(2,1)S(1)}, bf16[192,256]{1,0:T(8,128)(2,1)S(1)}, u32[]{:S(2)}, u32[]{:S(2)}) collective-permute-start(bf16[192,256]{1,0:T(8,128)(2,1)S(1)} %get-tuple-element.73), channel_id=1, source_target_pairs={{0,32},{8,40},{32,0},{40,8},{48,16},{56,24},{64,96},{72,104},{96,6... | collective-permute-start | bytes 294920 | tf_op jit(solution)/shard_map/ppermute | solution.py:328
  90.9 1.3 collective-permute-start.11
  92.2 4.6 %collective-permute-start.12 = (bf16[192,256]{1,0:T(8,128)(2,1)S(1)}, bf16[192,256]{1,0:T(8,128)(2,1)S(1)}, u32[]{:S(2)}, u32[]{:S(2)}) collective-permute-start(bf16[192,256]{1,0:T(8,128)(2,1)S(1)} %get-tuple-element.71), channel_id=1, source_target_pairs={{16,0},{24,8},{32,16},{40,24},{48,32},{56,40},{80,64},{88,72},{96,... | collective-permute-start | bytes 294920 | tf_op jit(solution)/shard_map/ppermute | solution.py:328
  96.8 4.8 %all-to-all-start.3 = ((bf16[4,2,192,256]{3,2,1,0:T(8,128)(2,1)}), bf16[4,2,192,256]{3,2,1,0:T(8,128)(2,1)S(1)}, u32[]{:S(2)}, u32[]{:S(2)}) async-start(bf16[4,2,192,256]{3,2,1,0:T(8,128)(2,1)} %weight_terms.4), calls=%async_computation.3 | async-start | bytes 1572864 | tf_op jit(solution)/shard_map/all_to_all | solution.py:399
  101.6 0.3 collective-permute-done.9.refs_4_
  101.9 1.2 broadcast_select_fusion
  103.1 0.2 copy-done.5
  103.3 1.4 collective-permute-start.13
  104.7 5.6 %weight_terms.5 = bf16[4,2,192,256]{3,2,1,0:T(8,128)(2,1)} custom-call(bf16[1024,768]{1,0:T(8,128)(2,1)} %copy-done, bf16[1024,768]{1,0:T(8,128)(2,1)} %copy-done.2, bf16[1024,768]{1,0:T(8,128)(2,1)} %copy-done.1, bf16[1024,768]{1,0:T(8,128)(2,1)} %collective-permute-done.4.refs_5_.refs_3_, bf16[2,1024,256]{2,1,0:T(8,128)(2,1)} %copy-done.5, ...), custom_call_target="tpu_custom_call" | custom-call | flops 1 | bytes 1 | tf_op jit(solution)/shard_map/weight_terms/pallas_call | solution.py:232
  110.2 5.8 %all-to-all-start.4 = ((bf16[4,2,192,256]{3,2,1,0:T(8,128)(2,1)}), bf16[4,2,192,256]{3,2,1,0:T(8,128)(2,1)S(1)}, u32[]{:S(2)}, u32[]{:S(2)}) async-start(bf16[4,2,192,256]{3,2,1,0:T(8,128)(2,1)} %weight_terms.5), calls=%async_computation.4 | async-start | bytes 1572864 | tf_op jit(solution)/shard_map/all_to_all | solution.py:399
  116.0 0.6 pad_add_fusion.at_ref
  116.6 0.1 fusion
  116.7 0.1 fusion.3
  116.8 2.8 %collective-permute-done.13.refs_4_ = bf16[2,1024,256]{2,1,0:T(8,128)(2,1)} collective-permute-done((bf16[2,1024,256]{2,1,0:T(8,128)(2,1)}, bf16[2,1024,256]{2,1,0:T(8,128)(2,1)}, u32[]{:S(2)}, u32[]{:S(2)}) %collective-permute-start.13) | collective-permute-done | bytes 1048608 | tf_op jit(solution)/shard_map/ppermute | solution.py:428
  119.6 5.1 %last_terms.1 = (bf16[192,256]{1,0:T(8,128)(2,1)}, bf16[192,256]{1,0:T(8,128)(2,1)}, bf16[192,256]{1,0:T(8,128)(2,1)}, bf16[192,256]{1,0:T(8,128)(2,1)}) custom-call(s32[2]{0:T(128)} %pad_add_fusion.at_ref, bf16[1024,768]{1,0:T(8,128)(2,1)} %copy-done, bf16[1024,768]{1,0:T(8,128)(2,1)} %copy-done.2, bf16[1024,768]{1,0:T(8,128)(2,1)} %copy-done.1, ...), custom_call_target="tpu_custom_call" | custom-call | flops 1 | bytes 1 | tf_op jit(solution)/shard_map/last_terms/pallas_call | solution.py:271
  124.7 3.0 %collective-permute-start.14 = (bf16[192,256]{1,0:T(8,128)(2,1)}, bf16[192,256]{1,0:T(8,128)(2,1)S(1)}, u32[]{:S(2)}, u32[]{:S(2)}) collective-permute-start(bf16[192,256]{1,0:T(8,128)(2,1)} %get-tuple-element.58), channel_id=1, source_target_pairs={{0,128},{8,136},{16,144},{24,152},{32,160},{40,168},{48,176},{56,1... | collective-permute-start | bytes 294920 | tf_op jit(solution)/shard_map/ppermute | solution.py:314
  127.7 1.2 collective-permute-start.15
  128.9 0.8 collective-permute-start.16
  129.8 0.1 add_convert_fusion.1
  129.9 1.5 collective-permute-start.22
  131.4 3.0 %collective-permute-start.21 = (bf16[192,256]{1,0:T(8,128)(2,1)S(1)}, bf16[192,256]{1,0:T(8,128)(2,1)S(1)}, u32[]{:S(2)}, u32[]{:S(2)}) collective-permute-start(bf16[192,256]{1,0:T(8,128)(2,1)S(1)} %get-tuple-element.68), channel_id=1, source_target_pairs={{0,1},{1,2},{2,3},{3,4},{4,5},{5,6},{6,7},{7,0},{8,9},{9,10},{10,1... | collective-permute-start | bytes 294920 | tf_op jit(solution)/shard_map/ppermute | solution.py:438
  134.4 2.5 %collective-permute-start.23 = (bf16[192,256]{1,0:T(8,128)(2,1)S(1)}, bf16[192,256]{1,0:T(8,128)(2,1)S(1)}, u32[]{:S(2)}, u32[]{:S(2)}) collective-permute-start(bf16[192,256]{1,0:T(8,128)(2,1)S(1)} %get-tuple-element.70), channel_id=1, source_target_pairs={{0,71},{1,64},{2,65},{3,66},{4,67},{5,68},{6,69},{7,70},{8,79},{9,... | collective-permute-start | bytes 294920 | tf_op jit(solution)/shard_map/ppermute | solution.py:438
  136.9 3.5 %collective-permute-start.24 = (bf16[192,256]{1,0:T(8,128)(2,1)S(1)}, bf16[192,256]{1,0:T(8,128)(2,1)S(1)}, u32[]{:S(2)}, u32[]{:S(2)}) collective-permute-start(bf16[192,256]{1,0:T(8,128)(2,1)S(1)} %get-tuple-element.69), channel_id=1, source_target_pairs={{0,198},{1,199},{2,192},{3,193},{4,194},{5,195},{6,196},{7,197},{8... | collective-permute-start | bytes 294920 | tf_op jit(solution)/shard_map/ppermute | solution.py:438
  140.4 0.1 add_convert_fusion.5
  140.5 0.7 collective-permute-start.17
  141.2 0.7 collective-permute-start.18
  141.9 6.8 %collective-permute-start.19 = (bf16[192,256]{1,0:T(8,128)(2,1)S(1)}, bf16[192,256]{1,0:T(8,128)(2,1)S(1)}, u32[]{:S(2)}, u32[]{:S(2)}) collective-permute-start(bf16[192,256]{1,0:T(8,128)(2,1)S(1)} %add_convert_fusion.5), channel_id=1, source_target_pairs={{32,53},{33,54},{34,55},{35,48},{36,49},{37,50},{38,51},{39,52},{4... | collective-permute-start | bytes 294920 | tf_op jit(solution)/shard_map/ppermute | solution.py:442
  148.6 0.7 collective-permute-start.20
  149.3 2.4 %collective-permute-done.19 = bf16[192,256]{1,0:T(8,128)(2,1)S(1)} collective-permute-done((bf16[192,256]{1,0:T(8,128)(2,1)S(1)}, bf16[192,256]{1,0:T(8,128)(2,1)S(1)}, u32[]{:S(2)}, u32[]{:S(2)}) %collective-permute-start.19) | collective-permute-done | bytes 98336 | tf_op jit(solution)/shard_map/ppermute | solution.py:442
  151.8 0.1 select_select_fusion.1
  151.9 12.7 %collective-permute-start.26 = (bf16[192,256]{1,0:T(8,128)(2,1)S(1)}, bf16[192,256]{1,0:T(8,128)(2,1)S(1)}, u32[]{:S(2)}, u32[]{:S(2)}) collective-permute-start(bf16[192,256]{1,0:T(8,128)(2,1)S(1)} %select_select_fusion), channel_id=1, source_target_pairs={{0,0},{1,33},{2,66},{3,99},{4,132},{5,165},{6,198},{7,231},{8,192}... | collective-permute-start | bytes 294920 | tf_op jit(solution)/shard_map/ppermute | solution.py:451
  164.7 1.9 %collective-permute-start.25 = (bf16[192,256]{1,0:T(8,128)(2,1)S(1)}, bf16[192,256]{1,0:T(8,128)(2,1)S(1)}, u32[]{:S(2)}, u32[]{:S(2)}) collective-permute-start(bf16[192,256]{1,0:T(8,128)(2,1)S(1)} %get-tuple-element.65), channel_id=1, source_target_pairs={{0,192},{1,225},{2,2},{3,35},{4,68},{5,101},{6,134},{7,167},{8,0},... | collective-permute-start | bytes 294920 | tf_op jit(solution)/shard_map/ppermute | solution.py:450
  166.6 0.2 collective-permute-done.26
  166.8 5.8 %collective-permute-done.25 = bf16[192,256]{1,0:T(8,128)(2,1)S(1)} collective-permute-done((bf16[192,256]{1,0:T(8,128)(2,1)S(1)}, bf16[192,256]{1,0:T(8,128)(2,1)S(1)}, u32[]{:S(2)}, u32[]{:S(2)}) %collective-permute-start.25) | collective-permute-done | bytes 98336 | tf_op jit(solution)/shard_map/ppermute | solution.py:450
  172.7 0.8 maximum_convert_fusion
  (38 shorter events, 0.2 us)
Async XLA Ops:
  5.9 35.2 %collective-permute-start.2 = (bf16[3,1024,256]{2,1,0:T(8,128)(2,1)}, bf16[3,1024,256]{2,1,0:T(8,128)(2,1)S(1)}, u32[]{:S(2)}, u32[]{:S(2)}) collective-permute-start(bf16[3,1024,256]{2,1,0:T(8,128)(2,1)} %get-tuple-element.35), channel_id=1, source_target_pairs={{0,8},{8,0},{16,24},{24,16},{32,40},{40,32},{48,56},{56,48},{64,72... | collective-permute-start | bytes 4718600 | tf_op jit(solution)/shard_map/ppermute | solution.py:388
  5.9 41.3 %collective-permute-start = (bf16[1024,768]{1,0:T(8,128)(2,1)}, bf16[1024,768]{1,0:T(8,128)(2,1)S(1)}, u32[]{:S(2)}, u32[]{:S(2)}) collective-permute-start(bf16[1024,768]{1,0:T(8,128)(2,1)} %refs_0_.2), channel_id=1, source_target_pairs={{0,1},{1,2},{2,3},{3,4},{4,5},{5,6},{6,7},{7,0},{8,9},{9,10},{10,1... | collective-permute-start | bytes 4718600 | tf_op jit(solution)/shard_map/ppermute | solution.py:385
  7.9 39.3 %collective-permute-start.1 = (bf16[1024,768]{1,0:T(8,128)(2,1)}, bf16[1024,768]{1,0:T(8,128)(2,1)S(1)}, u32[]{:S(2)}, u32[]{:S(2)}) collective-permute-start(bf16[1024,768]{1,0:T(8,128)(2,1)} %refs_0_.2), channel_id=1, source_target_pairs={{0,7},{1,0},{2,1},{3,2},{4,3},{5,4},{6,5},{7,6},{8,15},{9,8},{10,9... | collective-permute-start | bytes 4718600 | tf_op jit(solution)/shard_map/ppermute | solution.py:385
  41.1 1.2 copy-start.3
  47.2 11.1 %copy-start = (bf16[1024,768]{1,0:T(8,128)(2,1)}, bf16[1024,768]{1,0:T(8,128)(2,1)S(1)}, u32[]{:S(2)}) copy-start(bf16[1024,768]{1,0:T(8,128)(2,1)S(1)} %collective-permute-done.refs_2_.refs_0_) | copy-start | bytes 4718596
  47.2 11.0 %copy-start.1 = (bf16[1024,768]{1,0:T(8,128)(2,1)}, bf16[1024,768]{1,0:T(8,128)(2,1)S(1)}, u32[]{:S(2)}) copy-start(bf16[1024,768]{1,0:T(8,128)(2,1)S(1)} %collective-permute-done.1.refs_4_.refs_2_) | copy-start | bytes 4718596
  47.2 11.0 %collective-permute-start.3 = (bf16[1024,768]{1,0:T(8,128)(2,1)S(1)}, bf16[1024,768]{1,0:T(8,128)(2,1)S(1)}, u32[]{:S(2)}, u32[]{:S(2)}) collective-permute-start(bf16[1024,768]{1,0:T(8,128)(2,1)S(1)} %collective-permute-done.refs_2_.refs_0_), channel_id=1, source_target_pairs={{0,8},{8,0},{16,24},{24,16},{32,40},{40,32},{48,56},{56,48},{64,72... | collective-permute-start | bytes 4718600 | tf_op jit(solution)/shard_map/ppermute | solution.py:388
  47.5 10.8 %collective-permute-start.4 = (bf16[1024,768]{1,0:T(8,128)(2,1)S(1)}, bf16[1024,768]{1,0:T(8,128)(2,1)}, u32[]{:S(2)}, u32[]{:S(2)}) collective-permute-start(bf16[1024,768]{1,0:T(8,128)(2,1)S(1)} %collective-permute-done.1.refs_4_.refs_2_), channel_id=1, source_target_pairs={{0,8},{8,0},{16,24},{24,16},{32,40},{40,32},{48,56},{56,48},{64,72... | collective-permute-start | bytes 4718600 | tf_op jit(solution)/shard_map/ppermute | solution.py:388
  47.8 10.5 %collective-permute-start.7 = (bf16[1024,768]{1,0:T(8,128)(2,1)}, bf16[1024,768]{1,0:T(8,128)(2,1)}, u32[]{:S(2)}, u32[]{:S(2)}) collective-permute-start(bf16[1024,768]{1,0:T(8,128)(2,1)} %refs_0_.2), channel_id=1, source_target_pairs={{0,8},{8,0},{16,24},{24,16},{32,40},{40,32},{48,56},{56,48},{64,72... | collective-permute-start | bytes 4718600 | tf_op jit(solution)/shard_map/ppermute | solution.py:388
  48.0 26.9 %collective-permute-start.5 = (bf16[2,1024,256]{2,1,0:T(8,128)(2,1)}, bf16[2,1024,256]{2,1,0:T(8,128)(2,1)}, u32[]{:S(2)}, u32[]{:S(2)}) collective-permute-start(bf16[2,1024,256]{2,1,0:T(8,128)(2,1)} %value_gradient.1.refs_6_), channel_id=1, source_target_pairs={{0,1},{1,2},{2,3},{3,4},{4,5},{5,6},{6,7},{7,0},{8,9},{9,10},{10,1... | collective-permute-start | bytes 3145736 | tf_op jit(solution)/shard_map/ppermute | solution.py:385
  48.0 26.9 %collective-permute-start.6 = (bf16[2,1024,256]{2,1,0:T(8,128)(2,1)}, bf16[2,1024,256]{2,1,0:T(8,128)(2,1)}, u32[]{:S(2)}, u32[]{:S(2)}) collective-permute-start(bf16[2,1024,256]{2,1,0:T(8,128)(2,1)} %value_gradient.1.refs_6_), channel_id=1, source_target_pairs={{0,7},{1,0},{2,1},{3,2},{4,3},{5,4},{6,5},{7,6},{8,15},{9,8},{10,9... | collective-permute-start | bytes 3145736 | tf_op jit(solution)/shard_map/ppermute | solution.py:385
  58.3 1.2 copy-start.2
  66.3 19.7 %all-to-all-start.2 = ((bf16[4,3,192,256]{3,2,1,0:T(8,128)(2,1)}), bf16[4,3,192,256]{3,2,1,0:T(8,128)(2,1)S(1)}, u32[]{:S(2)}, u32[]{:S(2)}) async-start(bf16[4,3,192,256]{3,2,1,0:T(8,128)(2,1)} %weight_terms.3), calls=%async_computation.2 | async-start | bytes 2359296 | tf_op jit(solution)/shard_map/all_to_all | solution.py:399
  74.9 26.7 %collective-permute-start.8 = (bf16[2,1024,256]{2,1,0:T(8,128)(2,1)}, bf16[2,1024,256]{2,1,0:T(8,128)(2,1)S(1)}, u32[]{:S(2)}, u32[]{:S(2)}) collective-permute-start(bf16[2,1024,256]{2,1,0:T(8,128)(2,1)} %collective-permute-done.5.refs_5_), channel_id=1, source_target_pairs={{0,1},{1,2},{2,3},{3,4},{4,5},{5,6},{6,7},{7,0},{8,9},{9,10},{10,1... | collective-permute-start | bytes 3145736 | tf_op jit(solution)/shard_map/ppermute | solution.py:385
  77.2 24.7 %collective-permute-start.9 = (bf16[2,1024,256]{2,1,0:T(8,128)(2,1)}, bf16[2,1024,256]{2,1,0:T(8,128)(2,1)S(1)}, u32[]{:S(2)}, u32[]{:S(2)}) collective-permute-start(bf16[2,1024,256]{2,1,0:T(8,128)(2,1)} %collective-permute-done.6.refs_4_), channel_id=1, source_target_pairs={{0,7},{1,0},{2,1},{3,2},{4,3},{5,4},{6,5},{7,6},{8,15},{9,8},{10,9... | collective-permute-start | bytes 3145736 | tf_op jit(solution)/shard_map/ppermute | solution.py:385
  86.1 0.7 copy-start.6
  86.9 14.7 %collective-permute-start.10 = (bf16[192,256]{1,0:T(8,128)(2,1)S(1)}, bf16[192,256]{1,0:T(8,128)(2,1)S(1)}, u32[]{:S(2)}, u32[]{:S(2)}) collective-permute-start(bf16[192,256]{1,0:T(8,128)(2,1)S(1)} %get-tuple-element.73), channel_id=1, source_target_pairs={{0,32},{8,40},{32,0},{40,8},{48,16},{56,24},{64,96},{72,104},{96,6... | collective-permute-start | bytes 294920 | tf_op jit(solution)/shard_map/ppermute | solution.py:328
  90.9 10.7 %collective-permute-start.11 = (bf16[192,256]{1,0:T(8,128)(2,1)S(1)}, bf16[192,256]{1,0:T(8,128)(2,1)S(1)}, u32[]{:S(2)}, u32[]{:S(2)}) collective-permute-start(bf16[192,256]{1,0:T(8,128)(2,1)S(1)} %get-tuple-element.72), channel_id=1, source_target_pairs={{0,16},{8,24},{16,32},{24,40},{48,0},{56,8},{64,80},{72,88},{80,96... | collective-permute-start | bytes 294920 | tf_op jit(solution)/shard_map/ppermute | solution.py:328
  92.2 9.4 %collective-permute-start.12 = (bf16[192,256]{1,0:T(8,128)(2,1)S(1)}, bf16[192,256]{1,0:T(8,128)(2,1)S(1)}, u32[]{:S(2)}, u32[]{:S(2)}) collective-permute-start(bf16[192,256]{1,0:T(8,128)(2,1)S(1)} %get-tuple-element.71), channel_id=1, source_target_pairs={{16,0},{24,8},{32,16},{40,24},{48,32},{56,40},{80,64},{88,72},{96,... | collective-permute-start | bytes 294920 | tf_op jit(solution)/shard_map/ppermute | solution.py:328
  96.8 13.5 %all-to-all-start.3 = ((bf16[4,2,192,256]{3,2,1,0:T(8,128)(2,1)}), bf16[4,2,192,256]{3,2,1,0:T(8,128)(2,1)S(1)}, u32[]{:S(2)}, u32[]{:S(2)}) async-start(bf16[4,2,192,256]{3,2,1,0:T(8,128)(2,1)} %weight_terms.4), calls=%async_computation.3 | async-start | bytes 1572864 | tf_op jit(solution)/shard_map/all_to_all | solution.py:399
  101.6 1.5 copy-start.4
  101.9 1.4 copy-start.5
  103.3 16.3 %collective-permute-start.13 = (bf16[2,1024,256]{2,1,0:T(8,128)(2,1)}, bf16[2,1024,256]{2,1,0:T(8,128)(2,1)}, u32[]{:S(2)}, u32[]{:S(2)}) collective-permute-start(bf16[2,1024,256]{2,1,0:T(8,128)(2,1)} %broadcast_select_fusion), channel_id=1, source_target_pairs={{0,1},{1,2},{2,3},{3,4},{4,5},{5,6},{6,7},{7,0},{8,15},{9,8},{10,9... | collective-permute-start | bytes 3145736 | tf_op jit(solution)/shard_map/ppermute | solution.py:428
  110.2 6.5 %copy-start.7 = (bf16[1,3,192,256]{3,2,1,0:T(8,128)(2,1)S(1)}, bf16[1,3,192,256]{3,2,1,0:T(8,128)(2,1)}, u32[]{:S(2)}) copy-start(bf16[1,3,192,256]{3,2,1,0:T(8,128)(2,1)} %copy-done.6) | copy-start | bytes 884740
  110.2 19.5 %all-to-all-start.4 = ((bf16[4,2,192,256]{3,2,1,0:T(8,128)(2,1)}), bf16[4,2,192,256]{3,2,1,0:T(8,128)(2,1)S(1)}, u32[]{:S(2)}, u32[]{:S(2)}) async-start(bf16[4,2,192,256]{3,2,1,0:T(8,128)(2,1)} %weight_terms.5), calls=%async_computation.4 | async-start | bytes 1572864 | tf_op jit(solution)/shard_map/all_to_all | solution.py:399
  124.7 15.7 %copy-start.8 = (bf16[192,256]{1,0:T(8,128)(2,1)S(1)}, bf16[192,256]{1,0:T(8,128)(2,1)}, u32[]{:S(2)}) copy-start(bf16[192,256]{1,0:T(8,128)(2,1)} %get-tuple-element.57) | copy-start | bytes 294916
  124.7 9.7 %collective-permute-start.14 = (bf16[192,256]{1,0:T(8,128)(2,1)}, bf16[192,256]{1,0:T(8,128)(2,1)S(1)}, u32[]{:S(2)}, u32[]{:S(2)}) collective-permute-start(bf16[192,256]{1,0:T(8,128)(2,1)} %get-tuple-element.58), channel_id=1, source_target_pairs={{0,128},{8,136},{16,144},{24,152},{32,160},{40,168},{48,176},{56,1... | collective-permute-start | bytes 294920 | tf_op jit(solution)/shard_map/ppermute | solution.py:314
  127.7 9.2 %collective-permute-start.15 = (bf16[192,256]{1,0:T(8,128)(2,1)}, bf16[192,256]{1,0:T(8,128)(2,1)S(1)}, u32[]{:S(2)}, u32[]{:S(2)}) collective-permute-start(bf16[192,256]{1,0:T(8,128)(2,1)} %get-tuple-element.59), channel_id=1, source_target_pairs={{0,64},{8,72},{16,80},{24,88},{32,96},{40,104},{48,112},{56,120},{... | collective-permute-start | bytes 294920 | tf_op jit(solution)/shard_map/ppermute | solution.py:314
  128.9 11.5 %collective-permute-start.16 = (bf16[192,256]{1,0:T(8,128)(2,1)}, bf16[192,256]{1,0:T(8,128)(2,1)S(1)}, u32[]{:S(2)}, u32[]{:S(2)}) collective-permute-start(bf16[192,256]{1,0:T(8,128)(2,1)} %get-tuple-element.60), channel_id=1, source_target_pairs={{0,192},{8,200},{16,208},{24,216},{32,224},{40,232},{48,240},{56,2... | collective-permute-start | bytes 294920 | tf_op jit(solution)/shard_map/ppermute | solution.py:314
  129.9 11.2 %collective-permute-start.22 = (bf16[192,256]{1,0:T(8,128)(2,1)S(1)}, bf16[192,256]{1,0:T(8,128)(2,1)S(1)}, u32[]{:S(2)}, u32[]{:S(2)}) collective-permute-start(bf16[192,256]{1,0:T(8,128)(2,1)S(1)} %select_bitcast_fusion.4), channel_id=1, source_target_pairs={{0,130},{1,131},{2,132},{3,133},{4,134},{5,135},{6,128},{7,129},{8... | collective-permute-start | bytes 294920 | tf_op jit(solution)/shard_map/ppermute | solution.py:438
  131.4 10.4 %collective-permute-start.21 = (bf16[192,256]{1,0:T(8,128)(2,1)S(1)}, bf16[192,256]{1,0:T(8,128)(2,1)S(1)}, u32[]{:S(2)}, u32[]{:S(2)}) collective-permute-start(bf16[192,256]{1,0:T(8,128)(2,1)S(1)} %get-tuple-element.68), channel_id=1, source_target_pairs={{0,1},{1,2},{2,3},{3,4},{4,5},{5,6},{6,7},{7,0},{8,9},{9,10},{10,1... | collective-permute-start | bytes 294920 | tf_op jit(solution)/shard_map/ppermute | solution.py:438
  134.4 14.2 %collective-permute-start.23 = (bf16[192,256]{1,0:T(8,128)(2,1)S(1)}, bf16[192,256]{1,0:T(8,128)(2,1)S(1)}, u32[]{:S(2)}, u32[]{:S(2)}) collective-permute-start(bf16[192,256]{1,0:T(8,128)(2,1)S(1)} %get-tuple-element.70), channel_id=1, source_target_pairs={{0,71},{1,64},{2,65},{3,66},{4,67},{5,68},{6,69},{7,70},{8,79},{9,... | collective-permute-start | bytes 294920 | tf_op jit(solution)/shard_map/ppermute | solution.py:438
  136.9 12.4 %collective-permute-start.24 = (bf16[192,256]{1,0:T(8,128)(2,1)S(1)}, bf16[192,256]{1,0:T(8,128)(2,1)S(1)}, u32[]{:S(2)}, u32[]{:S(2)}) collective-permute-start(bf16[192,256]{1,0:T(8,128)(2,1)S(1)} %get-tuple-element.69), channel_id=1, source_target_pairs={{0,198},{1,199},{2,192},{3,193},{4,194},{5,195},{6,196},{7,197},{8... | collective-permute-start | bytes 294920 | tf_op jit(solution)/shard_map/ppermute | solution.py:438
  140.5 8.8 %collective-permute-start.17 = (bf16[192,256]{1,0:T(8,128)(2,1)S(1)}, bf16[192,256]{1,0:T(8,128)(2,1)S(1)}, u32[]{:S(2)}, u32[]{:S(2)}) collective-permute-start(bf16[192,256]{1,0:T(8,128)(2,1)S(1)} %add_convert_fusion.5), channel_id=1, source_target_pairs={{48,53},{49,54},{50,55},{51,48},{52,49},{53,50},{54,51},{55,52},{5... | collective-permute-start | bytes 294920 | tf_op jit(solution)/shard_map/ppermute | solution.py:442
  141.2 8.2 %collective-permute-start.18 = (bf16[192,256]{1,0:T(8,128)(2,1)S(1)}, bf16[192,256]{1,0:T(8,128)(2,1)S(1)}, u32[]{:S(2)}, u32[]{:S(2)}) collective-permute-start(bf16[192,256]{1,0:T(8,128)(2,1)S(1)} %add_convert_fusion.5), channel_id=1, source_target_pairs={{16,53},{17,54},{18,55},{19,48},{20,49},{21,50},{22,51},{23,52},{2... | collective-permute-start | bytes 294920 | tf_op jit(solution)/shard_map/ppermute | solution.py:442
  141.9 9.9 %collective-permute-start.19 = (bf16[192,256]{1,0:T(8,128)(2,1)S(1)}, bf16[192,256]{1,0:T(8,128)(2,1)S(1)}, u32[]{:S(2)}, u32[]{:S(2)}) collective-permute-start(bf16[192,256]{1,0:T(8,128)(2,1)S(1)} %add_convert_fusion.5), channel_id=1, source_target_pairs={{32,53},{33,54},{34,55},{35,48},{36,49},{37,50},{38,51},{39,52},{4... | collective-permute-start | bytes 294920 | tf_op jit(solution)/shard_map/ppermute | solution.py:442
  148.6 3.2 %collective-permute-start.20 = (bf16[192,256]{1,0:T(8,128)(2,1)S(1)}, bf16[192,256]{1,0:T(8,128)(2,1)S(1)}, u32[]{:S(2)}, u32[]{:S(2)}) collective-permute-start(bf16[192,256]{1,0:T(8,128)(2,1)S(1)} %add_convert_fusion.5), channel_id=1, source_target_pairs={{0,53},{1,54},{2,55},{3,48},{4,49},{5,50},{6,51},{7,52},{8,59},{9,... | collective-permute-start | bytes 294920 | tf_op jit(solution)/shard_map/ppermute | solution.py:442
  151.9 14.9 %collective-permute-start.26 = (bf16[192,256]{1,0:T(8,128)(2,1)S(1)}, bf16[192,256]{1,0:T(8,128)(2,1)S(1)}, u32[]{:S(2)}, u32[]{:S(2)}) collective-permute-start(bf16[192,256]{1,0:T(8,128)(2,1)S(1)} %select_select_fusion), channel_id=1, source_target_pairs={{0,0},{1,33},{2,66},{3,99},{4,132},{5,165},{6,198},{7,231},{8,192}... | collective-permute-start | bytes 294920 | tf_op jit(solution)/shard_map/ppermute | solution.py:451
  164.7 8.0 %collective-permute-start.25 = (bf16[192,256]{1,0:T(8,128)(2,1)S(1)}, bf16[192,256]{1,0:T(8,128)(2,1)S(1)}, u32[]{:S(2)}, u32[]{:S(2)}) collective-permute-start(bf16[192,256]{1,0:T(8,128)(2,1)S(1)} %get-tuple-element.65), channel_id=1, source_target_pairs={{0,192},{1,225},{2,2},{3,35},{4,68},{5,101},{6,134},{7,167},{8,0},... | collective-permute-start | bytes 294920 | tf_op jit(solution)/shard_map/ppermute | solution.py:450

commit v4 on v3

--- a/solution.py
+++ b/solution.py
@@ -27,8 +27,8 @@
 QUICK = pl.CostEstimate(flops=1, bytes_accessed=1, transcendentals=0)
 
 
-def params():
-    return pltpu.CompilerParams(vmem_limit_bytes=58 * 1024 * 1024)
+def params(mib=58):
+    return pltpu.CompilerParams(vmem_limit_bytes=mib * 1024 * 1024)
 
 
 def tie(*arrays):
@@ -172,7 +172,7 @@
             out_specs=out,
         ),
         out_shape=jax.ShapeDtypeStruct((2, rows, 2 * DH), BF16),
-        compiler_params=params(),
+        compiler_params=params(52),
         cost_estimate=QUICK,
         name="value_gradient",
     )(core, q, k, o, packed, packed, packed, sums, sums)
@@ -409,14 +409,14 @@
     u1, d1 = go(v0, up), go(v0, down)
     prev0, next0, kv0, x_own, _ = tie(prev0, next0, kv0, layer_input, v0)
     prev1, next1, own1 = swap(prev0), swap(next0), swap(x_own)
-    query_grad, key_grad = query_key_gradients(queries, keys, values, out_grad, sums, g1, kv0, scaling)
-    prev1, next1, query_grad, key_grad = tie(prev1, next1, query_grad, key_grad)
     near = [prev0, prev1, next0, next1]
     t0 = terms([x_own, own1, *near], [v0], [(0, 0), (1, 0), (2, 0)])
 
     p0 = exchange("x", t0)
-
-    u1, d1 = tie(u1, d1, t0)[:2]
+    kv0 = tie(kv0, t0)[0]
+    query_grad, key_grad = query_key_gradients(queries, keys, values, out_grad, sums, g1, kv0, scaling)
+
+    u1, d1, query_grad, key_grad = tie(u1, d1, query_grad, key_grad)
     u2, d2 = go(u1, up), go(d1, down)
     t1 = terms(near, [d1, u1], [(0, 0), (1, 1)])
     p0 = total(list(tie(p0, t1)[0]))

time: 174 us -> 170 us (0.977)
  the two profiles are of different devices: /device:TPU:20 before, /device:TPU:35 now
where the time goes in v4:
time: 170 us
  starting transfers between devices  74.3 us (44%)
  Pallas kernels  41.9 us (25%)
  blocking collectives  29.8 us (18%)
  waiting for transfers between devices  17.2 us (10%)
  other arithmetic  3.38 us (2%)
  local copies, waits for them, and re-layouts  2.04 us (1%)
    pallas_call x3, Pallas kernels, weight_terms(): pl.pallas_call(functools.partial(terms_kernel, scale, blocks, len(xs), le...  18.1 us
    all_to_all x1, blocking collectives, per_device(): lax.all_to_all(totals.reshape(n_seq, *totals.shape[2:]), 'seq', 0, 0)  15.7 us
    ppermute x4, starting transfers between devices, per_device(): x2 = [lax.ppermute(held[d], both, to_x(d, n_z)) for d in (0, 2, 1, 3)]  15.3 us
    ppermute x1, starting transfers between devices, per_device(): second = lax.ppermute(second, both, owners(1, n_z))  15.1 us
    all_to_all x1, blocking collectives, per_device(): sums = lax.all_to_all(running_sums(spread), 'seq', 0, 0)  14.1 us
    all_to_all x3, starting transfers between devices, exchange(): return lax.all_to_all(pieces, 'seq', 0, 0, axis_index_groups=groups[axis])  13 us
    ppermute x3, starting transfers between devices, send_to(): lax.ppermute(chosen[d], 'seq', shift_to(axis, targets, d))  8.33 us
    ppermute x6, starting transfers between devices, go(): return lax.ppermute(array, 'head', way)  7.16 us
  transfers between devices with their start and end apart: 30, of which 9 were waited for; matrix products, arithmetic and copies ran while one was open for 1% of the time, Pallas kernels for 22%

profile of v4, /device:TPU:35, one launch (start us, length us, event | category | flops | bytes accessed | tf_op | source)
XLA Modules:
  0.0 169.5 jit_solution(15320412862379019015)
XLA Ops:
  0.6 0.0 copy-start.9
  0.6 5.4 %states.1 = (f32[4,128,128]{2,1,0:T(8,128)}, f32[4,128,128]{2,1,0:T(8,128)}, bf16[4,8,2,16,128]{4,3,2,1,0:T(8,128)(2,1)}, bf16[3,1024,256]{2,1,0:T(8,128)(2,1)}) custom-call(s32[1]{0:T(128)} %bitcast._, bf16[1024,512]{1,0:T(8,128)(2,1)} %q_ref.3, bf16[1024,512]{1,0:T(8,128)(2,1)} %k_ref.3, bf16[1024,512]{1,0:T(8,128)(2,1)} %v_ref.3, bf16[1024,512]{1,0:T(8,128)(2,1)} %o_ref.3), custom_call_target="tpu_custom_call" | custom-call | flops 1 | bytes 1 | tf_op jit(solution)/shard_map/states/pallas_call | solution.py:70
  6.0 0.7 collective-permute-start
  6.7 1.7 collective-permute-start.3
  8.4 15.7 %all_to_all.25.in_ref = bf16[32,2,16,128]{3,2,1,0:T(8,128)(2,1)} all-to-all(bf16[32,2,16,128]{3,2,1,0:T(8,128)(2,1)} %bitcast.47), channel_id=1, replica_groups=mesh['seq'=32,'head'=8] {'seq'}, dimensions={0} | all-to-all | bytes 524288 | tf_op jit(solution)/shard_map/all_to_all | solution.py:403
  24.0 1.7 %running_sums.1 = bf16[32,3,16,128]{3,2,1,0:T(8,128)(2,1)} custom-call(bf16[32,2,16,128]{3,2,1,0:T(8,128)(2,1)} %all_to_all.25.in_ref), custom_call_target="tpu_custom_call" | custom-call | flops 1 | bytes 1 | tf_op jit(solution)/shard_map/running_sums/pallas_call | solution.py:108
  25.8 14.1 %all_to_all.26 = bf16[32,3,16,128]{3,2,1,0:T(8,128)(2,1)S(1)} all-to-all(bf16[32,3,16,128]{3,2,1,0:T(8,128)(2,1)} %running_sums.1), channel_id=1, replica_groups=mesh['seq'=32,'head'=8] {'seq'}, dimensions={0} | all-to-all | bytes 786432 | tf_op jit(solution)/shard_map/all_to_all | solution.py:404
  39.9 4.4 %value_gradient.1.refs_6_ = bf16[2,1024,256]{2,1,0:T(8,128)(2,1)S(1)} custom-call(s32[1]{0:T(128)} %bitcast._, bf16[1024,512]{1,0:T(8,128)(2,1)} %q_ref.3, bf16[1024,512]{1,0:T(8,128)(2,1)} %k_ref.3, bf16[1024,512]{1,0:T(8,128)(2,1)} %o_ref.3, bf16[3,1024,256]{2,1,0:T(8,128)(2,1)} %collective-permute-done.refs_3_.refs_4_.refs_5_, ...), custom_call_target="tpu_custom_call" | custom-call | flops 1 | bytes 1 | tf_op jit(solution)/shard_map/value_gradient/pallas_call | solution.py:166
  44.3 0.0 copy-start.1
  44.3 0.0 collective-permute-done.3.refs_2_.refs_0_
  44.3 0.1 collective-permute-done.4.refs_4_.refs_2_
  44.4 1.0 collective-permute-start.5
  45.3 0.0 collective-permute-start.6
  45.3 0.5 collective-permute-start.7
  45.9 2.9 %collective-permute-start.2 = (bf16[2,1024,256]{2,1,0:T(8,128)(2,1)S(1)}, bf16[2,1024,256]{2,1,0:T(8,128)(2,1)}, u32[]{:S(2)}, u32[]{:S(2)}) collective-permute-start(bf16[2,1024,256]{2,1,0:T(8,128)(2,1)S(1)} %value_gradient.1.refs_6_), channel_id=1, source_target_pairs={{0,7},{1,0},{2,1},{3,2},{4,3},{5,4},{6,5},{7,6},{8,15},{9,8},{10,9... | collective-permute-start | bytes 3145736 | tf_op jit(solution)/shard_map/ppermute | solution.py:385
  48.8 0.0 collective-permute-start.1
  48.8 0.0 collective-permute-done.5.refs_1_
  48.8 4.1 %collective-permute-done.6.refs_3_.refs_1_ = bf16[1024,768]{1,0:T(8,128)(2,1)S(1)} collective-permute-done((bf16[1024,768]{1,0:T(8,128)(2,1)S(1)}, bf16[1024,768]{1,0:T(8,128)(2,1)S(1)}, u32[]{:S(2)}, u32[]{:S(2)}) %collective-permute-start.6) | collective-permute-done | bytes 1572896 | tf_op jit(solution)/shard_map/ppermute | solution.py:388
  52.9 1.2 copy-done.4
  54.1 6.9 %weight_terms.3 = bf16[4,3,192,256]{3,2,1,0:T(8,128)(2,1)} custom-call(bf16[1024,768]{1,0:T(8,128)(2,1)} %refs_0_.2, bf16[1024,768]{1,0:T(8,128)(2,1)} %copy-done.10, bf16[1024,768]{1,0:T(8,128)(2,1)} %copy-done.2, bf16[1024,768]{1,0:T(8,128)(2,1)} %copy-done.4, bf16[1024,768]{1,0:T(8,128)(2,1)} %copy-done.3, ...), custom_call_target="tpu_custom_call" | custom-call | flops 1 | bytes 1 | tf_op jit(solution)/shard_map/weight_terms/pallas_call | solution.py:232
  60.9 4.3 %all-to-all-start.2 = ((bf16[4,3,192,256]{3,2,1,0:T(8,128)(2,1)}), bf16[4,3,192,256]{3,2,1,0:T(8,128)(2,1)S(1)}, u32[]{:S(2)}, u32[]{:S(2)}) async-start(bf16[4,3,192,256]{3,2,1,0:T(8,128)(2,1)} %weight_terms.3), calls=%async_computation.2 | async-start | bytes 2359296 | tf_op jit(solution)/shard_map/all_to_all | solution.py:399
  65.2 7.0 %query_key_gradients.1 = (bf16[1024,512]{1,0:T(8,128)(2,1)}, bf16[1024,512]{1,0:T(8,128)(2,1)}) custom-call(bf16[1024,512]{1,0:T(8,128)(2,1)} %q_ref.3, bf16[1024,512]{1,0:T(8,128)(2,1)} %k_ref.3, bf16[1024,512]{1,0:T(8,128)(2,1)} %v_ref.3, bf16[1024,512]{1,0:T(8,128)(2,1)} %o_ref.3, bf16[4,8,3,16,128]{4,3,2,1,0:T(8,128)(2,1)} %bitcast.45, ...), custom_call_target="tpu_custom_call" | custom-call | flops 1 | bytes 1 | tf_op jit(solution)/shard_map/query_key_gradients/pallas_call | solution.py:203
  72.2 0.1 collective-permute-done.2.refs_4_
  72.3 1.4 collective-permute-done.1.refs_5_
  73.7 1.4 collective-permute-start.8
  75.2 1.1 collective-permute-start.9
  76.3 5.6 %weight_terms.4 = bf16[4,2,192,256]{3,2,1,0:T(8,128)(2,1)} custom-call(bf16[1024,768]{1,0:T(8,128)(2,1)} %copy-done.2, bf16[1024,768]{1,0:T(8,128)(2,1)} %copy-done.4, bf16[1024,768]{1,0:T(8,128)(2,1)} %copy-done.3, bf16[1024,768]{1,0:T(8,128)(2,1)} %collective-permute-done.7.refs_5_.refs_3_, bf16[2,1024,256]{2,1,0:T(8,128)(2,1)} %collective-permute-done.2.refs_4_, ...), custom_call_target="tpu_custom_call" | custom-call | flops 1 | bytes 1 | tf_op jit(solution)/shard_map/weight_terms/pallas_call | solution.py:232
  81.9 0.1 add_convert_fusion
  82.1 0.0 copy-start.7
  82.1 0.7 copy-done.7
  82.8 1.3 collective-permute-start.12
  84.1 4.0 %collective-permute-start.11 = (bf16[192,256]{1,0:T(8,128)(2,1)S(1)}, bf16[192,256]{1,0:T(8,128)(2,1)S(1)}, u32[]{:S(2)}, u32[]{:S(2)}) collective-permute-start(bf16[192,256]{1,0:T(8,128)(2,1)S(1)} %get-tuple-element.70), channel_id=1, source_target_pairs={{0,16},{8,24},{16,32},{24,40},{48,0},{56,8},{64,80},{72,88},{80,96... | collective-permute-start | bytes 294920 | tf_op jit(solution)/shard_map/ppermute | solution.py:328
  88.1 3.0 %collective-permute-start.10 = (bf16[192,256]{1,0:T(8,128)(2,1)S(1)}, bf16[192,256]{1,0:T(8,128)(2,1)S(1)}, u32[]{:S(2)}, u32[]{:S(2)}) collective-permute-start(bf16[192,256]{1,0:T(8,128)(2,1)S(1)} %get-tuple-element.71), channel_id=1, source_target_pairs={{0,32},{8,40},{32,0},{40,8},{48,16},{56,24},{64,96},{72,104},{96,6... | collective-permute-start | bytes 294920 | tf_op jit(solution)/shard_map/ppermute | solution.py:328
  91.2 4.0 %all-to-all-start.3 = ((bf16[4,2,192,256]{3,2,1,0:T(8,128)(2,1)}), bf16[4,2,192,256]{3,2,1,0:T(8,128)(2,1)S(1)}, u32[]{:S(2)}, u32[]{:S(2)}) async-start(bf16[4,2,192,256]{3,2,1,0:T(8,128)(2,1)} %weight_terms.4), calls=%async_computation.3 | async-start | bytes 1572864 | tf_op jit(solution)/shard_map/all_to_all | solution.py:399
  95.2 3.4 %collective-permute-done.8.refs_5_ = bf16[2,1024,256]{2,1,0:T(8,128)(2,1)S(1)} collective-permute-done((bf16[2,1024,256]{2,1,0:T(8,128)(2,1)}, bf16[2,1024,256]{2,1,0:T(8,128)(2,1)S(1)}, u32[]{:S(2)}, u32[]{:S(2)}) %collective-permute-start.8) | collective-permute-done | bytes 1048608 | tf_op jit(solution)/shard_map/ppermute | solution.py:385
  98.6 1.8 %collective-permute-done.9.refs_4_ = bf16[2,1024,256]{2,1,0:T(8,128)(2,1)S(1)} collective-permute-done((bf16[2,1024,256]{2,1,0:T(8,128)(2,1)}, bf16[2,1024,256]{2,1,0:T(8,128)(2,1)S(1)}, u32[]{:S(2)}, u32[]{:S(2)}) %collective-permute-start.9) | collective-permute-done | bytes 1048608 | tf_op jit(solution)/shard_map/ppermute | solution.py:385
  100.3 1.2 broadcast_select_fusion
  101.6 0.1 copy-done.6
  101.7 0.9 collective-permute-start.13
  102.7 5.6 %weight_terms.5 = bf16[4,2,192,256]{3,2,1,0:T(8,128)(2,1)} custom-call(bf16[1024,768]{1,0:T(8,128)(2,1)} %copy-done.2, bf16[1024,768]{1,0:T(8,128)(2,1)} %copy-done.4, bf16[1024,768]{1,0:T(8,128)(2,1)} %copy-done.3, bf16[1024,768]{1,0:T(8,128)(2,1)} %collective-permute-done.7.refs_5_.refs_3_, bf16[2,1024,256]{2,1,0:T(8,128)(2,1)} %copy-done.6, ...), custom_call_target="tpu_custom_call" | custom-call | flops 1 | bytes 1 | tf_op jit(solution)/shard_map/weight_terms/pallas_call | solution.py:232
  108.2 4.8 %all-to-all-start.4 = ((bf16[4,2,192,256]{3,2,1,0:T(8,128)(2,1)}), bf16[4,2,192,256]{3,2,1,0:T(8,128)(2,1)S(1)}, u32[]{:S(2)}, u32[]{:S(2)}) async-start(bf16[4,2,192,256]{3,2,1,0:T(8,128)(2,1)} %weight_terms.5), calls=%async_computation.4 | async-start | bytes 1572864 | tf_op jit(solution)/shard_map/all_to_all | solution.py:399
  113.0 0.6 pad_add_fusion.at_ref
  113.6 0.1 fusion
  113.7 0.1 fusion.3
  113.8 2.5 %collective-permute-done.13.refs_4_ = bf16[2,1024,256]{2,1,0:T(8,128)(2,1)} collective-permute-done((bf16[2,1024,256]{2,1,0:T(8,128)(2,1)}, bf16[2,1024,256]{2,1,0:T(8,128)(2,1)}, u32[]{:S(2)}, u32[]{:S(2)}) %collective-permute-start.13) | collective-permute-done | bytes 1048608 | tf_op jit(solution)/shard_map/ppermute | solution.py:428
  116.3 5.3 %last_terms.1 = (bf16[192,256]{1,0:T(8,128)(2,1)}, bf16[192,256]{1,0:T(8,128)(2,1)}, bf16[192,256]{1,0:T(8,128)(2,1)}, bf16[192,256]{1,0:T(8,128)(2,1)}) custom-call(s32[2]{0:T(128)} %pad_add_fusion.at_ref, bf16[1024,768]{1,0:T(8,128)(2,1)} %copy-done.2, bf16[1024,768]{1,0:T(8,128)(2,1)} %copy-done.4, bf16[1024,768]{1,0:T(8,128)(2,1)} %copy-done.3, ...), custom_call_target="tpu_custom_call" | custom-call | flops 1 | bytes 1 | tf_op jit(solution)/shard_map/last_terms/pallas_call | solution.py:271
  121.6 0.4 all-to-all-done.4
  122.0 0.1 add_convert_fusion.1
  122.1 1.9 %collective-permute-start.14 = (bf16[192,256]{1,0:T(8,128)(2,1)}, bf16[192,256]{1,0:T(8,128)(2,1)S(1)}, u32[]{:S(2)}, u32[]{:S(2)}) collective-permute-start(bf16[192,256]{1,0:T(8,128)(2,1)} %get-tuple-element.56), channel_id=1, source_target_pairs={{0,128},{8,136},{16,144},{24,152},{32,160},{40,168},{48,176},{56,1... | collective-permute-start | bytes 294920 | tf_op jit(solution)/shard_map/ppermute | solution.py:314
  124.1 1.5 collective-permute-start.16
  125.6 5.2 %collective-permute-start.21 = (bf16[192,256]{1,0:T(8,128)(2,1)S(1)}, bf16[192,256]{1,0:T(8,128)(2,1)S(1)}, u32[]{:S(2)}, u32[]{:S(2)}) collective-permute-start(bf16[192,256]{1,0:T(8,128)(2,1)S(1)} %get-tuple-element.66), channel_id=1, source_target_pairs={{0,1},{1,2},{2,3},{3,4},{4,5},{5,6},{6,7},{7,0},{8,9},{9,10},{10,1... | collective-permute-start | bytes 294920 | tf_op jit(solution)/shard_map/ppermute | solution.py:438
  130.8 1.3 collective-permute-start.24
  132.1 0.7 collective-permute-start.23
  132.8 8.2 %collective-permute-start.22 = (bf16[192,256]{1,0:T(8,128)(2,1)S(1)}, bf16[192,256]{1,0:T(8,128)(2,1)S(1)}, u32[]{:S(2)}, u32[]{:S(2)}) collective-permute-start(bf16[192,256]{1,0:T(8,128)(2,1)S(1)} %select_bitcast_fusion.4), channel_id=1, source_target_pairs={{0,130},{1,131},{2,132},{3,133},{4,134},{5,135},{6,128},{7,129},{8... | collective-permute-start | bytes 294920 | tf_op jit(solution)/shard_map/ppermute | solution.py:438
  141.0 0.1 add_convert_fusion.5
  141.0 2.8 %collective-permute-start.20 = (bf16[192,256]{1,0:T(8,128)(2,1)S(1)}, bf16[192,256]{1,0:T(8,128)(2,1)S(1)}, u32[]{:S(2)}, u32[]{:S(2)}) collective-permute-start(bf16[192,256]{1,0:T(8,128)(2,1)S(1)} %add_convert_fusion.5), channel_id=1, source_target_pairs={{0,53},{1,54},{2,55},{3,48},{4,49},{5,50},{6,51},{7,52},{8,59},{9,... | collective-permute-start | bytes 294920 | tf_op jit(solution)/shard_map/ppermute | solution.py:442
  143.8 0.7 collective-permute-start.19
  144.5 0.7 collective-permute-start.18
  145.2 0.7 collective-permute-start.17
  145.9 0.1 select_select_fusion.1
  146.1 4.0 %collective-permute-start.25 = (bf16[192,256]{1,0:T(8,128)(2,1)S(1)}, bf16[192,256]{1,0:T(8,128)(2,1)S(1)}, u32[]{:S(2)}, u32[]{:S(2)}) collective-permute-start(bf16[192,256]{1,0:T(8,128)(2,1)S(1)} %get-tuple-element.63), channel_id=1, source_target_pairs={{0,192},{1,225},{2,2},{3,35},{4,68},{5,101},{6,134},{7,167},{8,0},... | collective-permute-start | bytes 294920 | tf_op jit(solution)/shard_map/ppermute | solution.py:450
  150.1 15.1 %collective-permute-start.26 = (bf16[192,256]{1,0:T(8,128)(2,1)S(1)}, bf16[192,256]{1,0:T(8,128)(2,1)S(1)}, u32[]{:S(2)}, u32[]{:S(2)}) collective-permute-start(bf16[192,256]{1,0:T(8,128)(2,1)S(1)} %select_select_fusion), channel_id=1, source_target_pairs={{0,0},{1,33},{2,66},{3,99},{4,132},{5,165},{6,198},{7,231},{8,192}... | collective-permute-start | bytes 294920 | tf_op jit(solution)/shard_map/ppermute | solution.py:451
  165.3 3.4 %collective-permute-done.26 = bf16[192,256]{1,0:T(8,128)(2,1)S(1)} collective-permute-done((bf16[192,256]{1,0:T(8,128)(2,1)S(1)}, bf16[192,256]{1,0:T(8,128)(2,1)S(1)}, u32[]{:S(2)}, u32[]{:S(2)}) %collective-permute-start.26) | collective-permute-done | bytes 98336 | tf_op jit(solution)/shard_map/ppermute | solution.py:451
  168.8 0.8 maximum_convert_fusion
  (44 shorter events, 0.2 us)
Async XLA Ops:
  0.6 6.1 %copy-start.9 = (bf16[1024,768]{1,0:T(8,128)(2,1)S(1)}, bf16[1024,768]{1,0:T(8,128)(2,1)}, u32[]{:S(2)}) copy-start(bf16[1024,768]{1,0:T(8,128)(2,1)} %refs_0_.2) | copy-start | bytes 4718596
  6.0 33.8 %collective-permute-start = (bf16[3,1024,256]{2,1,0:T(8,128)(2,1)}, bf16[3,1024,256]{2,1,0:T(8,128)(2,1)}, u32[]{:S(2)}, u32[]{:S(2)}) collective-permute-start(bf16[3,1024,256]{2,1,0:T(8,128)(2,1)} %get-tuple-element.33), channel_id=1, source_target_pairs={{0,8},{8,0},{16,24},{24,16},{32,40},{40,32},{48,56},{56,48},{64,72... | collective-permute-start | bytes 4718600 | tf_op jit(solution)/shard_map/ppermute | solution.py:388
  6.7 37.6 %collective-permute-start.3 = (bf16[1024,768]{1,0:T(8,128)(2,1)S(1)}, bf16[1024,768]{1,0:T(8,128)(2,1)S(1)}, u32[]{:S(2)}, u32[]{:S(2)}) collective-permute-start(bf16[1024,768]{1,0:T(8,128)(2,1)S(1)} %copy-done.9), channel_id=1, source_target_pairs={{0,1},{1,2},{2,3},{3,4},{4,5},{5,6},{6,7},{7,0},{8,9},{9,10},{10,1... | collective-permute-start | bytes 4718600 | tf_op jit(solution)/shard_map/ppermute | solution.py:385
  8.4 36.0 %collective-permute-start.4 = (bf16[1024,768]{1,0:T(8,128)(2,1)S(1)}, bf16[1024,768]{1,0:T(8,128)(2,1)S(1)}, u32[]{:S(2)}, u32[]{:S(2)}) collective-permute-start(bf16[1024,768]{1,0:T(8,128)(2,1)S(1)} %copy-done.9), channel_id=1, source_target_pairs={{0,7},{1,0},{2,1},{3,2},{4,3},{5,4},{6,5},{7,6},{8,15},{9,8},{10,9... | collective-permute-start | bytes 4718600 | tf_op jit(solution)/shard_map/ppermute | solution.py:385
  39.9 4.4 %copy-start = (bf16[32,3,16,128]{3,2,1,0:T(8,128)(2,1)}, bf16[32,3,16,128]{3,2,1,0:T(8,128)(2,1)S(1)}, u32[]{:S(2)}) copy-start(bf16[32,3,16,128]{3,2,1,0:T(8,128)(2,1)S(1)} %all_to_all.26) | copy-start | bytes 1179652
  44.3 9.8 %copy-start.1 = (bf16[2,1024,256]{2,1,0:T(8,128)(2,1)}, bf16[2,1024,256]{2,1,0:T(8,128)(2,1)S(1)}, u32[]{:S(2)}) copy-start(bf16[2,1024,256]{2,1,0:T(8,128)(2,1)S(1)} %value_gradient.1.refs_6_) | copy-start | bytes 3145732
  44.3 9.8 %copy-start.2 = (bf16[1024,768]{1,0:T(8,128)(2,1)}, bf16[1024,768]{1,0:T(8,128)(2,1)S(1)}, u32[]{:S(2)}) copy-start(bf16[1024,768]{1,0:T(8,128)(2,1)S(1)} %collective-permute-done.3.refs_2_.refs_0_) | copy-start | bytes 4718596
  44.4 9.7 %copy-start.3 = (bf16[1024,768]{1,0:T(8,128)(2,1)}, bf16[1024,768]{1,0:T(8,128)(2,1)S(1)}, u32[]{:S(2)}) copy-start(bf16[1024,768]{1,0:T(8,128)(2,1)S(1)} %collective-permute-done.4.refs_4_.refs_2_) | copy-start | bytes 4718596
  44.4 4.4 %collective-permute-start.5 = (bf16[1024,768]{1,0:T(8,128)(2,1)S(1)}, bf16[1024,768]{1,0:T(8,128)(2,1)S(1)}, u32[]{:S(2)}, u32[]{:S(2)}) collective-permute-start(bf16[1024,768]{1,0:T(8,128)(2,1)S(1)} %copy-done.9), channel_id=1, source_target_pairs={{0,8},{8,0},{16,24},{24,16},{32,40},{40,32},{48,56},{56,48},{64,72... | collective-permute-start | bytes 4718600 | tf_op jit(solution)/shard_map/ppermute | solution.py:388
  45.3 7.5 %collective-permute-start.6 = (bf16[1024,768]{1,0:T(8,128)(2,1)S(1)}, bf16[1024,768]{1,0:T(8,128)(2,1)S(1)}, u32[]{:S(2)}, u32[]{:S(2)}) collective-permute-start(bf16[1024,768]{1,0:T(8,128)(2,1)S(1)} %collective-permute-done.3.refs_2_.refs_0_), channel_id=1, source_target_pairs={{0,8},{8,0},{16,24},{24,16},{32,40},{40,32},{48,56},{56,48},{64,72... | collective-permute-start | bytes 4718600 | tf_op jit(solution)/shard_map/ppermute | solution.py:388
  45.3 8.7 %collective-permute-start.7 = (bf16[1024,768]{1,0:T(8,128)(2,1)S(1)}, bf16[1024,768]{1,0:T(8,128)(2,1)}, u32[]{:S(2)}, u32[]{:S(2)}) collective-permute-start(bf16[1024,768]{1,0:T(8,128)(2,1)S(1)} %collective-permute-done.4.refs_4_.refs_2_), channel_id=1, source_target_pairs={{0,8},{8,0},{16,24},{24,16},{32,40},{40,32},{48,56},{56,48},{64,72... | collective-permute-start | bytes 4718600 | tf_op jit(solution)/shard_map/ppermute | solution.py:388
  45.9 26.5 %collective-permute-start.2 = (bf16[2,1024,256]{2,1,0:T(8,128)(2,1)S(1)}, bf16[2,1024,256]{2,1,0:T(8,128)(2,1)}, u32[]{:S(2)}, u32[]{:S(2)}) collective-permute-start(bf16[2,1024,256]{2,1,0:T(8,128)(2,1)S(1)} %value_gradient.1.refs_6_), channel_id=1, source_target_pairs={{0,7},{1,0},{2,1},{3,2},{4,3},{5,4},{6,5},{7,6},{8,15},{9,8},{10,9... | collective-permute-start | bytes 3145736 | tf_op jit(solution)/shard_map/ppermute | solution.py:385
  48.8 24.9 %collective-permute-start.1 = (bf16[2,1024,256]{2,1,0:T(8,128)(2,1)S(1)}, bf16[2,1024,256]{2,1,0:T(8,128)(2,1)}, u32[]{:S(2)}, u32[]{:S(2)}) collective-permute-start(bf16[2,1024,256]{2,1,0:T(8,128)(2,1)S(1)} %value_gradient.1.refs_6_), channel_id=1, source_target_pairs={{0,1},{1,2},{2,3},{3,4},{4,5},{5,6},{6,7},{7,0},{8,9},{9,10},{10,1... | collective-permute-start | bytes 3145736 | tf_op jit(solution)/shard_map/ppermute | solution.py:385
  48.8 4.1 %copy-start.10 = (bf16[1024,768]{1,0:T(8,128)(2,1)}, bf16[1024,768]{1,0:T(8,128)(2,1)S(1)}, u32[]{:S(2)}) copy-start(bf16[1024,768]{1,0:T(8,128)(2,1)S(1)} %collective-permute-done.5.refs_1_) | copy-start | bytes 4718596
  52.9 1.2 copy-start.4
  60.9 21.0 %all-to-all-start.2 = ((bf16[4,3,192,256]{3,2,1,0:T(8,128)(2,1)}), bf16[4,3,192,256]{3,2,1,0:T(8,128)(2,1)S(1)}, u32[]{:S(2)}, u32[]{:S(2)}) async-start(bf16[4,3,192,256]{3,2,1,0:T(8,128)(2,1)} %weight_terms.3), calls=%async_computation.2 | async-start | bytes 2359296 | tf_op jit(solution)/shard_map/all_to_all | solution.py:399
  73.7 24.8 %collective-permute-start.8 = (bf16[2,1024,256]{2,1,0:T(8,128)(2,1)}, bf16[2,1024,256]{2,1,0:T(8,128)(2,1)S(1)}, u32[]{:S(2)}, u32[]{:S(2)}) collective-permute-start(bf16[2,1024,256]{2,1,0:T(8,128)(2,1)} %collective-permute-done.1.refs_5_), channel_id=1, source_target_pairs={{0,1},{1,2},{2,3},{3,4},{4,5},{5,6},{6,7},{7,0},{8,9},{9,10},{10,1... | collective-permute-start | bytes 3145736 | tf_op jit(solution)/shard_map/ppermute | solution.py:385
  75.2 25.2 %collective-permute-start.9 = (bf16[2,1024,256]{2,1,0:T(8,128)(2,1)}, bf16[2,1024,256]{2,1,0:T(8,128)(2,1)S(1)}, u32[]{:S(2)}, u32[]{:S(2)}) collective-permute-start(bf16[2,1024,256]{2,1,0:T(8,128)(2,1)} %collective-permute-done.2.refs_4_), channel_id=1, source_target_pairs={{0,7},{1,0},{2,1},{3,2},{4,3},{5,4},{6,5},{7,6},{8,15},{9,8},{10,9... | collective-permute-start | bytes 3145736 | tf_op jit(solution)/shard_map/ppermute | solution.py:385
  82.1 0.7 copy-start.7
  82.8 12.3 %collective-permute-start.12 = (bf16[192,256]{1,0:T(8,128)(2,1)S(1)}, bf16[192,256]{1,0:T(8,128)(2,1)S(1)}, u32[]{:S(2)}, u32[]{:S(2)}) collective-permute-start(bf16[192,256]{1,0:T(8,128)(2,1)S(1)} %get-tuple-element.69), channel_id=1, source_target_pairs={{16,0},{24,8},{32,16},{40,24},{48,32},{56,40},{80,64},{88,72},{96,... | collective-permute-start | bytes 294920 | tf_op jit(solution)/shard_map/ppermute | solution.py:328
  84.1 11.0 %collective-permute-start.11 = (bf16[192,256]{1,0:T(8,128)(2,1)S(1)}, bf16[192,256]{1,0:T(8,128)(2,1)S(1)}, u32[]{:S(2)}, u32[]{:S(2)}) collective-permute-start(bf16[192,256]{1,0:T(8,128)(2,1)S(1)} %get-tuple-element.70), channel_id=1, source_target_pairs={{0,16},{8,24},{16,32},{24,40},{48,0},{56,8},{64,80},{72,88},{80,96... | collective-permute-start | bytes 294920 | tf_op jit(solution)/shard_map/ppermute | solution.py:328
  88.1 7.0 %collective-permute-start.10 = (bf16[192,256]{1,0:T(8,128)(2,1)S(1)}, bf16[192,256]{1,0:T(8,128)(2,1)S(1)}, u32[]{:S(2)}, u32[]{:S(2)}) collective-permute-start(bf16[192,256]{1,0:T(8,128)(2,1)S(1)} %get-tuple-element.71), channel_id=1, source_target_pairs={{0,32},{8,40},{32,0},{40,8},{48,16},{56,24},{64,96},{72,104},{96,6... | collective-permute-start | bytes 294920 | tf_op jit(solution)/shard_map/ppermute | solution.py:328
  91.2 17.1 %all-to-all-start.3 = ((bf16[4,2,192,256]{3,2,1,0:T(8,128)(2,1)}), bf16[4,2,192,256]{3,2,1,0:T(8,128)(2,1)S(1)}, u32[]{:S(2)}, u32[]{:S(2)}) async-start(bf16[4,2,192,256]{3,2,1,0:T(8,128)(2,1)} %weight_terms.4), calls=%async_computation.3 | async-start | bytes 1572864 | tf_op jit(solution)/shard_map/all_to_all | solution.py:399
  98.6 3.0 %copy-start.5 = (bf16[2,1024,256]{2,1,0:T(8,128)(2,1)}, bf16[2,1024,256]{2,1,0:T(8,128)(2,1)S(1)}, u32[]{:S(2)}) copy-start(bf16[2,1024,256]{2,1,0:T(8,128)(2,1)S(1)} %collective-permute-done.8.refs_5_) | copy-start | bytes 3145732
  100.3 1.4 copy-start.6
  101.7 14.6 %collective-permute-start.13 = (bf16[2,1024,256]{2,1,0:T(8,128)(2,1)}, bf16[2,1024,256]{2,1,0:T(8,128)(2,1)}, u32[]{:S(2)}, u32[]{:S(2)}) collective-permute-start(bf16[2,1024,256]{2,1,0:T(8,128)(2,1)} %broadcast_select_fusion), channel_id=1, source_target_pairs={{0,1},{1,2},{2,3},{3,4},{4,5},{5,6},{6,7},{7,0},{8,15},{9,8},{10,9... | collective-permute-start | bytes 3145736 | tf_op jit(solution)/shard_map/ppermute | solution.py:428
  108.2 5.5 %copy-start.8 = (bf16[1,3,192,256]{3,2,1,0:T(8,128)(2,1)S(1)}, bf16[1,3,192,256]{3,2,1,0:T(8,128)(2,1)}, u32[]{:S(2)}) copy-start(bf16[1,3,192,256]{3,2,1,0:T(8,128)(2,1)} %copy-done.7) | copy-start | bytes 884740
  108.2 13.8 %all-to-all-start.4 = ((bf16[4,2,192,256]{3,2,1,0:T(8,128)(2,1)}), bf16[4,2,192,256]{3,2,1,0:T(8,128)(2,1)S(1)}, u32[]{:S(2)}, u32[]{:S(2)}) async-start(bf16[4,2,192,256]{3,2,1,0:T(8,128)(2,1)} %weight_terms.5), calls=%async_computation.4 | async-start | bytes 1572864 | tf_op jit(solution)/shard_map/all_to_all | solution.py:399
  121.6 19.4 %copy-start.11 = (bf16[192,256]{1,0:T(8,128)(2,1)S(1)}, bf16[192,256]{1,0:T(8,128)(2,1)}, u32[]{:S(2)}) copy-start(bf16[192,256]{1,0:T(8,128)(2,1)} %get-tuple-element.55) | copy-start | bytes 294916
  122.1 10.0 %collective-permute-start.14 = (bf16[192,256]{1,0:T(8,128)(2,1)}, bf16[192,256]{1,0:T(8,128)(2,1)S(1)}, u32[]{:S(2)}, u32[]{:S(2)}) collective-permute-start(bf16[192,256]{1,0:T(8,128)(2,1)} %get-tuple-element.56), channel_id=1, source_target_pairs={{0,128},{8,136},{16,144},{24,152},{32,160},{40,168},{48,176},{56,1... | collective-permute-start | bytes 294920 | tf_op jit(solution)/shard_map/ppermute | solution.py:314
  124.1 8.7 %collective-permute-start.15 = (bf16[192,256]{1,0:T(8,128)(2,1)}, bf16[192,256]{1,0:T(8,128)(2,1)S(1)}, u32[]{:S(2)}, u32[]{:S(2)}) collective-permute-start(bf16[192,256]{1,0:T(8,128)(2,1)} %get-tuple-element.57), channel_id=1, source_target_pairs={{0,64},{8,72},{16,80},{24,88},{32,96},{40,104},{48,112},{56,120},{... | collective-permute-start | bytes 294920 | tf_op jit(solution)/shard_map/ppermute | solution.py:314
  124.1 16.9 %collective-permute-start.16 = (bf16[192,256]{1,0:T(8,128)(2,1)}, bf16[192,256]{1,0:T(8,128)(2,1)S(1)}, u32[]{:S(2)}, u32[]{:S(2)}) collective-permute-start(bf16[192,256]{1,0:T(8,128)(2,1)} %get-tuple-element.58), channel_id=1, source_target_pairs={{0,192},{8,200},{16,208},{24,216},{32,224},{40,232},{48,240},{56,2... | collective-permute-start | bytes 294920 | tf_op jit(solution)/shard_map/ppermute | solution.py:314
  125.6 18.2 %collective-permute-start.21 = (bf16[192,256]{1,0:T(8,128)(2,1)S(1)}, bf16[192,256]{1,0:T(8,128)(2,1)S(1)}, u32[]{:S(2)}, u32[]{:S(2)}) collective-permute-start(bf16[192,256]{1,0:T(8,128)(2,1)S(1)} %get-tuple-element.66), channel_id=1, source_target_pairs={{0,1},{1,2},{2,3},{3,4},{4,5},{5,6},{6,7},{7,0},{8,9},{9,10},{10,1... | collective-permute-start | bytes 294920 | tf_op jit(solution)/shard_map/ppermute | solution.py:438
  130.8 13.7 %collective-permute-start.24 = (bf16[192,256]{1,0:T(8,128)(2,1)S(1)}, bf16[192,256]{1,0:T(8,128)(2,1)S(1)}, u32[]{:S(2)}, u32[]{:S(2)}) collective-permute-start(bf16[192,256]{1,0:T(8,128)(2,1)S(1)} %get-tuple-element.67), channel_id=1, source_target_pairs={{0,198},{1,199},{2,192},{3,193},{4,194},{5,195},{6,196},{7,197},{8... | collective-permute-start | bytes 294920 | tf_op jit(solution)/shard_map/ppermute | solution.py:438
  132.1 13.1 %collective-permute-start.23 = (bf16[192,256]{1,0:T(8,128)(2,1)S(1)}, bf16[192,256]{1,0:T(8,128)(2,1)S(1)}, u32[]{:S(2)}, u32[]{:S(2)}) collective-permute-start(bf16[192,256]{1,0:T(8,128)(2,1)S(1)} %get-tuple-element.68), channel_id=1, source_target_pairs={{0,71},{1,64},{2,65},{3,66},{4,67},{5,68},{6,69},{7,70},{8,79},{9,... | collective-permute-start | bytes 294920 | tf_op jit(solution)/shard_map/ppermute | solution.py:438
  132.8 13.1 %collective-permute-start.22 = (bf16[192,256]{1,0:T(8,128)(2,1)S(1)}, bf16[192,256]{1,0:T(8,128)(2,1)S(1)}, u32[]{:S(2)}, u32[]{:S(2)}) collective-permute-start(bf16[192,256]{1,0:T(8,128)(2,1)S(1)} %select_bitcast_fusion.4), channel_id=1, source_target_pairs={{0,130},{1,131},{2,132},{3,133},{4,134},{5,135},{6,128},{7,129},{8... | collective-permute-start | bytes 294920 | tf_op jit(solution)/shard_map/ppermute | solution.py:438
  141.0 4.9 %collective-permute-start.20 = (bf16[192,256]{1,0:T(8,128)(2,1)S(1)}, bf16[192,256]{1,0:T(8,128)(2,1)S(1)}, u32[]{:S(2)}, u32[]{:S(2)}) collective-permute-start(bf16[192,256]{1,0:T(8,128)(2,1)S(1)} %add_convert_fusion.5), channel_id=1, source_target_pairs={{0,53},{1,54},{2,55},{3,48},{4,49},{5,50},{6,51},{7,52},{8,59},{9,... | collective-permute-start | bytes 294920 | tf_op jit(solution)/shard_map/ppermute | solution.py:442
  143.8 2.1 %collective-permute-start.19 = (bf16[192,256]{1,0:T(8,128)(2,1)S(1)}, bf16[192,256]{1,0:T(8,128)(2,1)S(1)}, u32[]{:S(2)}, u32[]{:S(2)}) collective-permute-start(bf16[192,256]{1,0:T(8,128)(2,1)S(1)} %add_convert_fusion.5), channel_id=1, source_target_pairs={{32,53},{33,54},{34,55},{35,48},{36,49},{37,50},{38,51},{39,52},{4... | collective-permute-start | bytes 294920 | tf_op jit(solution)/shard_map/ppermute | solution.py:442
  144.5 1.4 collective-permute-start.18
  145.2 0.7 collective-permute-start.17
  146.1 19.2 %collective-permute-start.25 = (bf16[192,256]{1,0:T(8,128)(2,1)S(1)}, bf16[192,256]{1,0:T(8,128)(2,1)S(1)}, u32[]{:S(2)}, u32[]{:S(2)}) collective-permute-start(bf16[192,256]{1,0:T(8,128)(2,1)S(1)} %get-tuple-element.63), channel_id=1, source_target_pairs={{0,192},{1,225},{2,2},{3,35},{4,68},{5,101},{6,134},{7,167},{8,0},... | collective-permute-start | bytes 294920 | tf_op jit(solution)/shard_map/ppermute | solution.py:450
  150.1 18.6 %collective-permute-start.26 = (bf16[192,256]{1,0:T(8,128)(2,1)S(1)}, bf16[192,256]{1,0:T(8,128)(2,1)S(1)}, u32[]{:S(2)}, u32[]{:S(2)}) collective-permute-start(bf16[192,256]{1,0:T(8,128)(2,1)S(1)} %select_select_fusion), channel_id=1, source_target_pairs={{0,0},{1,33},{2,66},{3,99},{4,132},{5,165},{6,198},{7,231},{8,192}... | collective-permute-start | bytes 294920 | tf_op jit(solution)/shard_map/ppermute | solution.py:451

commit v5 on v4

--- a/solution.py
+++ b/solution.py
@@ -334,21 +334,8 @@
 LAST_STEP = (-3, 3)
 
 
-def to_x(d, nz):
-    return [
-        (seq_index(x, y, c) * nz + m, seq_index(x + d, y, c) * nz + (m + HELD_AT_X[(x + d) % NX][1]) % nz)
-        for x, y, c in CHIPS
-        for m in range(nz)
-    ]
-
-
-def to_last(d, nz):
-    return [
-        (seq_index(x, y, c) * nz + m, seq_index(x, LAST, c) * nz + (m + LAST_STEP[c]) % nz)
-        for x, y, c in CHIPS
-        for m in range(nz)
-        if (y + d) % NY == LAST
-    ]
+def to_last(d):
+    return [(a, b) for (x, y, c), (a, b) in zip(CHIPS, shift("y", d)) if (y + d) % NY == LAST]
 
 
 def owners(turn, nz):
@@ -357,8 +344,10 @@
         by_x = c == turn
         r = y if by_x else x
         d = HELD_AT_X[x][0] if by_x else HELD_AT_Y[y][0]
-        for j in range(nz):
-            pairs.append((seq_index(x, y, c) * nz + j, (4 * ((j - d) % nz) + r) * nz + j))
+        step = HELD_AT_X[x][1] if by_x else LAST_STEP[c] if y == LAST else 0
+        for m in range(nz):
+            j = (m + step) % nz
+            pairs.append((seq_index(x, y, c) * nz + m, (4 * ((j - d) % nz) + r) * nz + j))
     return pairs
 
 
@@ -435,11 +424,11 @@
     x3 = send_all("x", q3)
     p2 = total(list(tie(p2, q3[0])[0]))
     held = choose([p1[0], p1[1], p2[0], p2[1]], [0, 1, 2, 3], x)
-    x2 = [lax.ppermute(held[d], both, to_x(d, n_z)) for d in (0, 2, 1, 3)]
+    x2 = [held[0]] + send_all("x", held)
     p3 = total([q3[0]] + x3)
 
     p3 = tie(p3, *held)[0]
-    y3 = [lax.ppermute(p3, both, to_last(d, n_z)) for d in (0, 2, 1, 3)]
+    y3 = [p3] + [lax.ppermute(p3, "seq", to_last(d)) for d in (2, 1, 3)]
     held_x = total(x2)
     first = jnp.where(c == 0, held_x, r0)
     second = jnp.where(c == 0, r0, held_x)

time: 170 us -> 168 us (0.988)
  the two profiles are of different devices: /device:TPU:35 before, /device:TPU:13 now
where the time goes in v5:
time: 168 us; the launch traced here: 167 us
  starting transfers between devices  61.2 us (36%)
  Pallas kernels  41.9 us (25%)
  waiting for transfers between devices  29.2 us (17%)
  blocking collectives  28.1 us (17%)
  other arithmetic  3.37 us (2%)
  local copies, waits for them, and re-layouts  2.35 us (1%)
    pallas_call x3, Pallas kernels, weight_terms(): pl.pallas_call(functools.partial(terms_kernel, scale, blocks, len(xs), le...  18.1 us
    all_to_all x3, starting transfers between devices, exchange(): return lax.all_to_all(pieces, 'seq', 0, 0, axis_index_groups=groups[axis])  14.9 us
    all_to_all x1, blocking collectives, per_device(): sums = lax.all_to_all(running_sums(spread), 'seq', 0, 0)  14.2 us
    all_to_all x1, blocking collectives, per_device(): lax.all_to_all(totals.reshape(n_seq, *totals.shape[2:]), 'seq', 0, 0)  13.9 us
    ppermute x1, starting transfers between devices, per_device(): first = lax.ppermute(first, both, owners(0, n_z))  11.8 us
    ppermute x1, waiting for transfers between devices, per_device(): second = lax.ppermute(second, both, owners(1, n_z))  11 us
    ppermute x6, starting transfers between devices, go(): return lax.ppermute(array, 'head', way)  10.8 us
    pallas_call x1, Pallas kernels, query_key_gradients(): pl.pallas_call(functools.partial(query_key_kernel, scaling), grid=(heads,...  7.02 us
  transfers between devices with their start and end apart: 28, of which 11 were waited for; matrix products, arithmetic and copies ran while one was open for 1% of the time, Pallas kernels for 22%

profile of v5, /device:TPU:13, one launch (start us, length us, event | category | flops | bytes accessed | tf_op | source)
XLA Modules:
  0.0 167.1 jit_solution(17779901755638618896)
XLA Ops:
  0.6 0.0 copy-start.9
  0.6 5.4 %states.1 = (f32[4,128,128]{2,1,0:T(8,128)}, f32[4,128,128]{2,1,0:T(8,128)}, bf16[4,8,2,16,128]{4,3,2,1,0:T(8,128)(2,1)}, bf16[3,1024,256]{2,1,0:T(8,128)(2,1)}) custom-call(s32[1]{0:T(128)} %bitcast._, bf16[1024,512]{1,0:T(8,128)(2,1)} %q_ref.3, bf16[1024,512]{1,0:T(8,128)(2,1)} %k_ref.3, bf16[1024,512]{1,0:T(8,128)(2,1)} %v_ref.3, bf16[1024,512]{1,0:T(8,128)(2,1)} %o_ref.3), custom_call_target="tpu_custom_call" | custom-call | flops 1 | bytes 1 | tf_op jit(solution)/shard_map/states/pallas_call | solution.py:70
  6.0 0.7 collective-permute-start
  6.7 1.6 collective-permute-start.3
  8.4 3.9 %collective-permute-start.4 = (bf16[1024,768]{1,0:T(8,128)(2,1)S(1)}, bf16[1024,768]{1,0:T(8,128)(2,1)S(1)}, u32[]{:S(2)}, u32[]{:S(2)}) collective-permute-start(bf16[1024,768]{1,0:T(8,128)(2,1)S(1)} %copy-done.9), channel_id=1, source_target_pairs={{0,7},{1,0},{2,1},{3,2},{4,3},{5,4},{6,5},{7,6},{8,15},{9,8},{10,9... | collective-permute-start | bytes 4718600 | tf_op jit(solution)/shard_map/ppermute | solution.py:374
  12.3 13.9 %all_to_all.25.in_ref = bf16[32,2,16,128]{3,2,1,0:T(8,128)(2,1)} all-to-all(bf16[32,2,16,128]{3,2,1,0:T(8,128)(2,1)} %bitcast.47), channel_id=1, replica_groups=mesh['seq'=32,'head'=8] {'seq'}, dimensions={0} | all-to-all | bytes 524288 | tf_op jit(solution)/shard_map/all_to_all | solution.py:392
  26.2 1.7 %running_sums.1 = bf16[32,3,16,128]{3,2,1,0:T(8,128)(2,1)} custom-call(bf16[32,2,16,128]{3,2,1,0:T(8,128)(2,1)} %all_to_all.25.in_ref), custom_call_target="tpu_custom_call" | custom-call | flops 1 | bytes 1 | tf_op jit(solution)/shard_map/running_sums/pallas_call | solution.py:108
  27.9 14.2 %all_to_all.26 = bf16[32,3,16,128]{3,2,1,0:T(8,128)(2,1)S(1)} all-to-all(bf16[32,3,16,128]{3,2,1,0:T(8,128)(2,1)} %running_sums.1), channel_id=1, replica_groups=mesh['seq'=32,'head'=8] {'seq'}, dimensions={0} | all-to-all | bytes 786432 | tf_op jit(solution)/shard_map/all_to_all | solution.py:393
  42.1 0.0 collective-permute-done.refs_3_.refs_4_.refs_5_
  42.1 4.4 %value_gradient.1.refs_6_ = bf16[2,1024,256]{2,1,0:T(8,128)(2,1)S(1)} custom-call(s32[1]{0:T(128)} %bitcast._, bf16[1024,512]{1,0:T(8,128)(2,1)} %q_ref.3, bf16[1024,512]{1,0:T(8,128)(2,1)} %k_ref.3, bf16[1024,512]{1,0:T(8,128)(2,1)} %o_ref.3, bf16[3,1024,256]{2,1,0:T(8,128)(2,1)} %collective-permute-done.refs_3_.refs_4_.refs_5_, ...), custom_call_target="tpu_custom_call" | custom-call | flops 1 | bytes 1 | tf_op jit(solution)/shard_map/value_gradient/pallas_call | solution.py:166
  46.5 0.0 copy-start.1
  46.5 0.4 collective-permute-done.3.refs_2_.refs_0_
  47.0 0.8 collective-permute-start.5
  47.7 0.1 collective-permute-start.6
  47.8 0.4 collective-permute-start.7
  48.2 2.6 %collective-permute-start.2 = (bf16[2,1024,256]{2,1,0:T(8,128)(2,1)S(1)}, bf16[2,1024,256]{2,1,0:T(8,128)(2,1)}, u32[]{:S(2)}, u32[]{:S(2)}) collective-permute-start(bf16[2,1024,256]{2,1,0:T(8,128)(2,1)S(1)} %value_gradient.1.refs_6_), channel_id=1, source_target_pairs={{0,7},{1,0},{2,1},{3,2},{4,3},{5,4},{6,5},{7,6},{8,15},{9,8},{10,9... | collective-permute-start | bytes 3145736 | tf_op jit(solution)/shard_map/ppermute | solution.py:374
  50.8 4.4 %collective-permute-done.6.refs_3_.refs_1_ = bf16[1024,768]{1,0:T(8,128)(2,1)S(1)} collective-permute-done((bf16[1024,768]{1,0:T(8,128)(2,1)S(1)}, bf16[1024,768]{1,0:T(8,128)(2,1)S(1)}, u32[]{:S(2)}, u32[]{:S(2)}) %collective-permute-start.6) | collective-permute-done | bytes 1572896 | tf_op jit(solution)/shard_map/ppermute | solution.py:377
  55.3 1.2 copy-done.4
  56.4 6.9 %weight_terms.3 = bf16[4,3,192,256]{3,2,1,0:T(8,128)(2,1)} custom-call(bf16[1024,768]{1,0:T(8,128)(2,1)} %refs_0_.2, bf16[1024,768]{1,0:T(8,128)(2,1)} %copy-done.10, bf16[1024,768]{1,0:T(8,128)(2,1)} %copy-done.2, bf16[1024,768]{1,0:T(8,128)(2,1)} %copy-done.4, bf16[1024,768]{1,0:T(8,128)(2,1)} %copy-done.3, ...), custom_call_target="tpu_custom_call" | custom-call | flops 1 | bytes 1 | tf_op jit(solution)/shard_map/weight_terms/pallas_call | solution.py:232
  63.3 4.6 %all-to-all-start.2 = ((bf16[4,3,192,256]{3,2,1,0:T(8,128)(2,1)}), bf16[4,3,192,256]{3,2,1,0:T(8,128)(2,1)S(1)}, u32[]{:S(2)}, u32[]{:S(2)}) async-start(bf16[4,3,192,256]{3,2,1,0:T(8,128)(2,1)} %weight_terms.3), calls=%async_computation.2 | async-start | bytes 2359296 | tf_op jit(solution)/shard_map/all_to_all | solution.py:388
  67.9 7.0 %query_key_gradients.1 = (bf16[1024,512]{1,0:T(8,128)(2,1)}, bf16[1024,512]{1,0:T(8,128)(2,1)}) custom-call(bf16[1024,512]{1,0:T(8,128)(2,1)} %q_ref.3, bf16[1024,512]{1,0:T(8,128)(2,1)} %k_ref.3, bf16[1024,512]{1,0:T(8,128)(2,1)} %v_ref.3, bf16[1024,512]{1,0:T(8,128)(2,1)} %o_ref.3, bf16[4,8,3,16,128]{4,3,2,1,0:T(8,128)(2,1)} %bitcast.45, ...), custom_call_target="tpu_custom_call" | custom-call | flops 1 | bytes 1 | tf_op jit(solution)/shard_map/query_key_gradients/pallas_call | solution.py:203
  74.9 1.7 collective-permute-done.1.refs_5_
  76.6 2.7 %collective-permute-start.9 = (bf16[2,1024,256]{2,1,0:T(8,128)(2,1)}, bf16[2,1024,256]{2,1,0:T(8,128)(2,1)S(1)}, u32[]{:S(2)}, u32[]{:S(2)}) collective-permute-start(bf16[2,1024,256]{2,1,0:T(8,128)(2,1)} %collective-permute-done.2.refs_4_), channel_id=1, source_target_pairs={{0,7},{1,0},{2,1},{3,2},{4,3},{5,4},{6,5},{7,6},{8,15},{9,8},{10,9... | collective-permute-start | bytes 3145736 | tf_op jit(solution)/shard_map/ppermute | solution.py:374
  79.3 5.6 %weight_terms.4 = bf16[4,2,192,256]{3,2,1,0:T(8,128)(2,1)} custom-call(bf16[1024,768]{1,0:T(8,128)(2,1)} %copy-done.2, bf16[1024,768]{1,0:T(8,128)(2,1)} %copy-done.4, bf16[1024,768]{1,0:T(8,128)(2,1)} %copy-done.3, bf16[1024,768]{1,0:T(8,128)(2,1)} %collective-permute-done.7.refs_5_.refs_3_, bf16[2,1024,256]{2,1,0:T(8,128)(2,1)} %collective-permute-done.2.refs_4_, ...), custom_call_target="tpu_custom_call" | custom-call | flops 1 | bytes 1 | tf_op jit(solution)/shard_map/weight_terms/pallas_call | solution.py:232
  84.9 0.1 add_convert_fusion
  85.1 0.0 copy-start.7
  85.1 0.7 copy-done.7
  85.8 2.1 %collective-permute-start.12 = (bf16[192,256]{1,0:T(8,128)(2,1)S(1)}, bf16[192,256]{1,0:T(8,128)(2,1)S(1)}, u32[]{:S(2)}, u32[]{:S(2)}) collective-permute-start(bf16[192,256]{1,0:T(8,128)(2,1)S(1)} %get-tuple-element.69), channel_id=1, source_target_pairs={{16,0},{24,8},{32,16},{40,24},{48,32},{56,40},{80,64},{88,72},{96,... | collective-permute-start | bytes 294920 | tf_op jit(solution)/shard_map/ppermute | solution.py:328
  87.9 3.2 %collective-permute-start.11 = (bf16[192,256]{1,0:T(8,128)(2,1)S(1)}, bf16[192,256]{1,0:T(8,128)(2,1)S(1)}, u32[]{:S(2)}, u32[]{:S(2)}) collective-permute-start(bf16[192,256]{1,0:T(8,128)(2,1)S(1)} %get-tuple-element.70), channel_id=1, source_target_pairs={{0,16},{8,24},{16,32},{24,40},{48,0},{56,8},{64,80},{72,88},{80,96... | collective-permute-start | bytes 294920 | tf_op jit(solution)/shard_map/ppermute | solution.py:328
  91.1 1.3 collective-permute-start.10
  92.4 5.8 %all-to-all-start.3 = ((bf16[4,2,192,256]{3,2,1,0:T(8,128)(2,1)}), bf16[4,2,192,256]{3,2,1,0:T(8,128)(2,1)S(1)}, u32[]{:S(2)}, u32[]{:S(2)}) async-start(bf16[4,2,192,256]{3,2,1,0:T(8,128)(2,1)} %weight_terms.4), calls=%async_computation.3 | async-start | bytes 1572864 | tf_op jit(solution)/shard_map/all_to_all | solution.py:388
  98.2 0.1 collective-permute-done.10
  98.3 3.3 %collective-permute-done.8.refs_5_ = bf16[2,1024,256]{2,1,0:T(8,128)(2,1)S(1)} collective-permute-done((bf16[2,1024,256]{2,1,0:T(8,128)(2,1)}, bf16[2,1024,256]{2,1,0:T(8,128)(2,1)S(1)}, u32[]{:S(2)}, u32[]{:S(2)}) %collective-permute-start.8) | collective-permute-done | bytes 1048608 | tf_op jit(solution)/shard_map/ppermute | solution.py:374
  101.6 1.2 broadcast_select_fusion
  102.8 0.1 copy-done.5
  103.0 0.3 copy-done.6
  103.3 2.1 %collective-permute-start.13 = (bf16[2,1024,256]{2,1,0:T(8,128)(2,1)}, bf16[2,1024,256]{2,1,0:T(8,128)(2,1)}, u32[]{:S(2)}, u32[]{:S(2)}) collective-permute-start(bf16[2,1024,256]{2,1,0:T(8,128)(2,1)} %broadcast_select_fusion), channel_id=1, source_target_pairs={{0,1},{1,2},{2,3},{3,4},{4,5},{5,6},{6,7},{7,0},{8,15},{9,8},{10,9... | collective-permute-start | bytes 3145736 | tf_op jit(solution)/shard_map/ppermute | solution.py:417
  105.4 5.6 %weight_terms.5 = bf16[4,2,192,256]{3,2,1,0:T(8,128)(2,1)} custom-call(bf16[1024,768]{1,0:T(8,128)(2,1)} %copy-done.2, bf16[1024,768]{1,0:T(8,128)(2,1)} %copy-done.4, bf16[1024,768]{1,0:T(8,128)(2,1)} %copy-done.3, bf16[1024,768]{1,0:T(8,128)(2,1)} %collective-permute-done.7.refs_5_.refs_3_, bf16[2,1024,256]{2,1,0:T(8,128)(2,1)} %copy-done.6, ...), custom_call_target="tpu_custom_call" | custom-call | flops 1 | bytes 1 | tf_op jit(solution)/shard_map/weight_terms/pallas_call | solution.py:232
  111.0 4.5 %all-to-all-start.4 = ((bf16[4,2,192,256]{3,2,1,0:T(8,128)(2,1)}), bf16[4,2,192,256]{3,2,1,0:T(8,128)(2,1)S(1)}, u32[]{:S(2)}, u32[]{:S(2)}) async-start(bf16[4,2,192,256]{3,2,1,0:T(8,128)(2,1)} %weight_terms.5), calls=%async_computation.4 | async-start | bytes 1572864 | tf_op jit(solution)/shard_map/all_to_all | solution.py:388
  115.5 0.6 pad_add_fusion.at_ref
  116.1 0.1 fusion
  116.2 0.1 fusion.3
  116.3 1.2 collective-permute-done.13.refs_4_
  117.5 5.3 %last_terms.1 = (bf16[192,256]{1,0:T(8,128)(2,1)}, bf16[192,256]{1,0:T(8,128)(2,1)}, bf16[192,256]{1,0:T(8,128)(2,1)}, bf16[192,256]{1,0:T(8,128)(2,1)}) custom-call(s32[2]{0:T(128)} %pad_add_fusion.at_ref, bf16[1024,768]{1,0:T(8,128)(2,1)} %copy-done.2, bf16[1024,768]{1,0:T(8,128)(2,1)} %copy-done.4, bf16[1024,768]{1,0:T(8,128)(2,1)} %copy-done.3, ...), custom_call_target="tpu_custom_call" | custom-call | flops 1 | bytes 1 | tf_op jit(solution)/shard_map/last_terms/pallas_call | solution.py:271
  122.8 3.6 %all-to-all-done.4 = bf16[4,2,192,256]{3,2,1,0:T(8,128)(2,1)S(1)} async-done(((bf16[4,2,192,256]{3,2,1,0:T(8,128)(2,1)}), bf16[4,2,192,256]{3,2,1,0:T(8,128)(2,1)S(1)}, u32[]{:S(2)}, u32[]{:S(2)}) %all-to-all-start.4) | async-done | bytes 786464 | tf_op jit(solution)/shard_map/all_to_all | solution.py:388
  126.4 0.1 add_convert_fusion.1
  126.5 0.5 collective-permute-start.14
  126.9 1.7 collective-permute-start.15
  128.6 0.1 collective-permute-start.16
  128.7 1.5 collective-permute-start.22
  130.3 0.4 collective-permute-start.21
  130.7 1.2 collective-permute-done.14
  131.8 2.0 %collective-permute-start.20 = (bf16[192,256]{1,0:T(8,128)(2,1)S(1)}, bf16[192,256]{1,0:T(8,128)(2,1)S(1)}, u32[]{:S(2)}, u32[]{:S(2)}) collective-permute-start(bf16[192,256]{1,0:T(8,128)(2,1)S(1)} %select_bitcast_fusion.4), channel_id=1, source_target_pairs={{0,128},{8,136},{16,144},{24,152},{32,160},{40,168},{48,176},{56,1... | collective-permute-start | bytes 294920 | tf_op jit(solution)/shard_map/ppermute | solution.py:314
  133.8 0.1 add_convert_fusion.5
  133.9 0.7 collective-permute-start.19
  134.6 0.7 collective-permute-start.18
  135.2 0.6 collective-permute-done.22
  135.9 3.7 %collective-permute-start.17 = (bf16[192,256]{1,0:T(8,128)(2,1)S(1)}, bf16[192,256]{1,0:T(8,128)(2,1)S(1)}, u32[]{:S(2)}, u32[]{:S(2)}) collective-permute-start(bf16[192,256]{1,0:T(8,128)(2,1)S(1)} %add_convert_fusion.5), channel_id=1, source_target_pairs={{16,48},{24,56},{80,112},{88,120},{144,176},{152,184},{208,240},{2... | collective-permute-start | bytes 294920 | tf_op jit(solution)/shard_map/ppermute | solution.py:431
  139.7 1.6 collective-permute-done.17
  141.2 0.1 select_select_fusion.1
  141.3 11.8 %collective-permute-start.23 = (bf16[192,256]{1,0:T(8,128)(2,1)S(1)}, bf16[192,256]{1,0:T(8,128)(2,1)S(1)}, u32[]{:S(2)}, u32[]{:S(2)}) collective-permute-start(bf16[192,256]{1,0:T(8,128)(2,1)S(1)} %get-tuple-element.63), channel_id=1, source_target_pairs={{0,225},{1,2},{2,35},{3,68},{4,101},{5,134},{6,167},{7,192},{8,0},... | collective-permute-start | bytes 294920 | tf_op jit(solution)/shard_map/ppermute | solution.py:439
  153.2 1.9 %collective-permute-start.24 = (bf16[192,256]{1,0:T(8,128)(2,1)S(1)}, bf16[192,256]{1,0:T(8,128)(2,1)S(1)}, u32[]{:S(2)}, u32[]{:S(2)}) collective-permute-start(bf16[192,256]{1,0:T(8,128)(2,1)S(1)} %select_select_fusion), channel_id=1, source_target_pairs={{0,0},{1,33},{2,66},{3,99},{4,132},{5,165},{6,198},{7,231},{8,225}... | collective-permute-start | bytes 294920 | tf_op jit(solution)/shard_map/ppermute | solution.py:440
  155.2 11.0 %collective-permute-done.24 = bf16[192,256]{1,0:T(8,128)(2,1)S(1)} collective-permute-done((bf16[192,256]{1,0:T(8,128)(2,1)S(1)}, bf16[192,256]{1,0:T(8,128)(2,1)S(1)}, u32[]{:S(2)}, u32[]{:S(2)}) %collective-permute-start.24) | collective-permute-done | bytes 98336 | tf_op jit(solution)/shard_map/ppermute | solution.py:440
  166.3 0.8 maximum_convert_fusion
  (40 shorter events, 0.2 us)
Async XLA Ops:
  0.6 6.1 %copy-start.9 = (bf16[1024,768]{1,0:T(8,128)(2,1)S(1)}, bf16[1024,768]{1,0:T(8,128)(2,1)}, u32[]{:S(2)}) copy-start(bf16[1024,768]{1,0:T(8,128)(2,1)} %refs_0_.2) | copy-start | bytes 4718596
  6.0 36.1 %collective-permute-start = (bf16[3,1024,256]{2,1,0:T(8,128)(2,1)}, bf16[3,1024,256]{2,1,0:T(8,128)(2,1)}, u32[]{:S(2)}, u32[]{:S(2)}) collective-permute-start(bf16[3,1024,256]{2,1,0:T(8,128)(2,1)} %get-tuple-element.33), channel_id=1, source_target_pairs={{0,8},{8,0},{16,24},{24,16},{32,40},{40,32},{48,56},{56,48},{64,72... | collective-permute-start | bytes 4718600 | tf_op jit(solution)/shard_map/ppermute | solution.py:377
  6.7 40.3 %collective-permute-start.3 = (bf16[1024,768]{1,0:T(8,128)(2,1)S(1)}, bf16[1024,768]{1,0:T(8,128)(2,1)S(1)}, u32[]{:S(2)}, u32[]{:S(2)}) collective-permute-start(bf16[1024,768]{1,0:T(8,128)(2,1)S(1)} %copy-done.9), channel_id=1, source_target_pairs={{0,1},{1,2},{2,3},{3,4},{4,5},{5,6},{6,7},{7,0},{8,9},{9,10},{10,1... | collective-permute-start | bytes 4718600 | tf_op jit(solution)/shard_map/ppermute | solution.py:374
  8.4 38.6 %collective-permute-start.4 = (bf16[1024,768]{1,0:T(8,128)(2,1)S(1)}, bf16[1024,768]{1,0:T(8,128)(2,1)S(1)}, u32[]{:S(2)}, u32[]{:S(2)}) collective-permute-start(bf16[1024,768]{1,0:T(8,128)(2,1)S(1)} %copy-done.9), channel_id=1, source_target_pairs={{0,7},{1,0},{2,1},{3,2},{4,3},{5,4},{6,5},{7,6},{8,15},{9,8},{10,9... | collective-permute-start | bytes 4718600 | tf_op jit(solution)/shard_map/ppermute | solution.py:374
  42.1 4.4 %copy-start = (bf16[32,3,16,128]{3,2,1,0:T(8,128)(2,1)}, bf16[32,3,16,128]{3,2,1,0:T(8,128)(2,1)S(1)}, u32[]{:S(2)}) copy-start(bf16[32,3,16,128]{3,2,1,0:T(8,128)(2,1)S(1)} %all_to_all.26) | copy-start | bytes 1179652
  46.5 9.9 %copy-start.1 = (bf16[2,1024,256]{2,1,0:T(8,128)(2,1)}, bf16[2,1024,256]{2,1,0:T(8,128)(2,1)S(1)}, u32[]{:S(2)}) copy-start(bf16[2,1024,256]{2,1,0:T(8,128)(2,1)S(1)} %value_gradient.1.refs_6_) | copy-start | bytes 3145732
  47.0 9.5 %copy-start.2 = (bf16[1024,768]{1,0:T(8,128)(2,1)}, bf16[1024,768]{1,0:T(8,128)(2,1)S(1)}, u32[]{:S(2)}) copy-start(bf16[1024,768]{1,0:T(8,128)(2,1)S(1)} %collective-permute-done.3.refs_2_.refs_0_) | copy-start | bytes 4718596
  47.0 9.5 %copy-start.3 = (bf16[1024,768]{1,0:T(8,128)(2,1)}, bf16[1024,768]{1,0:T(8,128)(2,1)S(1)}, u32[]{:S(2)}) copy-start(bf16[1024,768]{1,0:T(8,128)(2,1)S(1)} %collective-permute-done.4.refs_4_.refs_2_) | copy-start | bytes 4718596
  47.0 3.9 %collective-permute-start.5 = (bf16[1024,768]{1,0:T(8,128)(2,1)S(1)}, bf16[1024,768]{1,0:T(8,128)(2,1)S(1)}, u32[]{:S(2)}, u32[]{:S(2)}) collective-permute-start(bf16[1024,768]{1,0:T(8,128)(2,1)S(1)} %copy-done.9), channel_id=1, source_target_pairs={{0,8},{8,0},{16,24},{24,16},{32,40},{40,32},{48,56},{56,48},{64,72... | collective-permute-start | bytes 4718600 | tf_op jit(solution)/shard_map/ppermute | solution.py:377
  47.7 7.5 %collective-permute-start.6 = (bf16[1024,768]{1,0:T(8,128)(2,1)S(1)}, bf16[1024,768]{1,0:T(8,128)(2,1)S(1)}, u32[]{:S(2)}, u32[]{:S(2)}) collective-permute-start(bf16[1024,768]{1,0:T(8,128)(2,1)S(1)} %collective-permute-done.3.refs_2_.refs_0_), channel_id=1, source_target_pairs={{0,8},{8,0},{16,24},{24,16},{32,40},{40,32},{48,56},{56,48},{64,72... | collective-permute-start | bytes 4718600 | tf_op jit(solution)/shard_map/ppermute | solution.py:377
  47.8 8.6 %collective-permute-start.7 = (bf16[1024,768]{1,0:T(8,128)(2,1)S(1)}, bf16[1024,768]{1,0:T(8,128)(2,1)}, u32[]{:S(2)}, u32[]{:S(2)}) collective-permute-start(bf16[1024,768]{1,0:T(8,128)(2,1)S(1)} %collective-permute-done.4.refs_4_.refs_2_), channel_id=1, source_target_pairs={{0,8},{8,0},{16,24},{24,16},{32,40},{40,32},{48,56},{56,48},{64,72... | collective-permute-start | bytes 4718600 | tf_op jit(solution)/shard_map/ppermute | solution.py:377
  48.2 26.7 %collective-permute-start.2 = (bf16[2,1024,256]{2,1,0:T(8,128)(2,1)S(1)}, bf16[2,1024,256]{2,1,0:T(8,128)(2,1)}, u32[]{:S(2)}, u32[]{:S(2)}) collective-permute-start(bf16[2,1024,256]{2,1,0:T(8,128)(2,1)S(1)} %value_gradient.1.refs_6_), channel_id=1, source_target_pairs={{0,7},{1,0},{2,1},{3,2},{4,3},{5,4},{6,5},{7,6},{8,15},{9,8},{10,9... | collective-permute-start | bytes 3145736 | tf_op jit(solution)/shard_map/ppermute | solution.py:374
  50.8 25.8 %collective-permute-start.1 = (bf16[2,1024,256]{2,1,0:T(8,128)(2,1)S(1)}, bf16[2,1024,256]{2,1,0:T(8,128)(2,1)}, u32[]{:S(2)}, u32[]{:S(2)}) collective-permute-start(bf16[2,1024,256]{2,1,0:T(8,128)(2,1)S(1)} %value_gradient.1.refs_6_), channel_id=1, source_target_pairs={{0,1},{1,2},{2,3},{3,4},{4,5},{5,6},{6,7},{7,0},{8,9},{9,10},{10,1... | collective-permute-start | bytes 3145736 | tf_op jit(solution)/shard_map/ppermute | solution.py:374
  50.8 4.4 %copy-start.10 = (bf16[1024,768]{1,0:T(8,128)(2,1)}, bf16[1024,768]{1,0:T(8,128)(2,1)S(1)}, u32[]{:S(2)}) copy-start(bf16[1024,768]{1,0:T(8,128)(2,1)S(1)} %collective-permute-done.5.refs_1_) | copy-start | bytes 4718596
  55.3 1.2 copy-start.4
  63.3 21.6 %all-to-all-start.2 = ((bf16[4,3,192,256]{3,2,1,0:T(8,128)(2,1)}), bf16[4,3,192,256]{3,2,1,0:T(8,128)(2,1)S(1)}, u32[]{:S(2)}, u32[]{:S(2)}) async-start(bf16[4,3,192,256]{3,2,1,0:T(8,128)(2,1)} %weight_terms.3), calls=%async_computation.2 | async-start | bytes 2359296 | tf_op jit(solution)/shard_map/all_to_all | solution.py:388
  76.6 25.0 %collective-permute-start.8 = (bf16[2,1024,256]{2,1,0:T(8,128)(2,1)}, bf16[2,1024,256]{2,1,0:T(8,128)(2,1)S(1)}, u32[]{:S(2)}, u32[]{:S(2)}) collective-permute-start(bf16[2,1024,256]{2,1,0:T(8,128)(2,1)} %collective-permute-done.1.refs_5_), channel_id=1, source_target_pairs={{0,1},{1,2},{2,3},{3,4},{4,5},{5,6},{6,7},{7,0},{8,9},{9,10},{10,1... | collective-permute-start | bytes 3145736 | tf_op jit(solution)/shard_map/ppermute | solution.py:374
  76.6 25.0 %collective-permute-start.9 = (bf16[2,1024,256]{2,1,0:T(8,128)(2,1)}, bf16[2,1024,256]{2,1,0:T(8,128)(2,1)S(1)}, u32[]{:S(2)}, u32[]{:S(2)}) collective-permute-start(bf16[2,1024,256]{2,1,0:T(8,128)(2,1)} %collective-permute-done.2.refs_4_), channel_id=1, source_target_pairs={{0,7},{1,0},{2,1},{3,2},{4,3},{5,4},{6,5},{7,6},{8,15},{9,8},{10,9... | collective-permute-start | bytes 3145736 | tf_op jit(solution)/shard_map/ppermute | solution.py:374
  85.1 0.7 copy-start.7
  85.8 12.4 %collective-permute-start.12 = (bf16[192,256]{1,0:T(8,128)(2,1)S(1)}, bf16[192,256]{1,0:T(8,128)(2,1)S(1)}, u32[]{:S(2)}, u32[]{:S(2)}) collective-permute-start(bf16[192,256]{1,0:T(8,128)(2,1)S(1)} %get-tuple-element.69), channel_id=1, source_target_pairs={{16,0},{24,8},{32,16},{40,24},{48,32},{56,40},{80,64},{88,72},{96,... | collective-permute-start | bytes 294920 | tf_op jit(solution)/shard_map/ppermute | solution.py:328
  87.9 10.3 %collective-permute-start.11 = (bf16[192,256]{1,0:T(8,128)(2,1)S(1)}, bf16[192,256]{1,0:T(8,128)(2,1)S(1)}, u32[]{:S(2)}, u32[]{:S(2)}) collective-permute-start(bf16[192,256]{1,0:T(8,128)(2,1)S(1)} %get-tuple-element.70), channel_id=1, source_target_pairs={{0,16},{8,24},{16,32},{24,40},{48,0},{56,8},{64,80},{72,88},{80,96... | collective-permute-start | bytes 294920 | tf_op jit(solution)/shard_map/ppermute | solution.py:328
  91.1 7.2 %collective-permute-start.10 = (bf16[192,256]{1,0:T(8,128)(2,1)S(1)}, bf16[192,256]{1,0:T(8,128)(2,1)S(1)}, u32[]{:S(2)}, u32[]{:S(2)}) collective-permute-start(bf16[192,256]{1,0:T(8,128)(2,1)S(1)} %get-tuple-element.71), channel_id=1, source_target_pairs={{0,32},{8,40},{32,0},{40,8},{48,16},{56,24},{64,96},{72,104},{96,6... | collective-permute-start | bytes 294920 | tf_op jit(solution)/shard_map/ppermute | solution.py:328
  92.4 18.6 %all-to-all-start.3 = ((bf16[4,2,192,256]{3,2,1,0:T(8,128)(2,1)}), bf16[4,2,192,256]{3,2,1,0:T(8,128)(2,1)S(1)}, u32[]{:S(2)}, u32[]{:S(2)}) async-start(bf16[4,2,192,256]{3,2,1,0:T(8,128)(2,1)} %weight_terms.4), calls=%async_computation.3 | async-start | bytes 1572864 | tf_op jit(solution)/shard_map/all_to_all | solution.py:388
  101.6 1.4 copy-start.5
  101.6 1.7 copy-start.6
  103.3 14.3 %collective-permute-start.13 = (bf16[2,1024,256]{2,1,0:T(8,128)(2,1)}, bf16[2,1024,256]{2,1,0:T(8,128)(2,1)}, u32[]{:S(2)}, u32[]{:S(2)}) collective-permute-start(bf16[2,1024,256]{2,1,0:T(8,128)(2,1)} %broadcast_select_fusion), channel_id=1, source_target_pairs={{0,1},{1,2},{2,3},{3,4},{4,5},{5,6},{6,7},{7,0},{8,15},{9,8},{10,9... | collective-permute-start | bytes 3145736 | tf_op jit(solution)/shard_map/ppermute | solution.py:417
  111.0 5.2 %copy-start.8 = (bf16[1,3,192,256]{3,2,1,0:T(8,128)(2,1)S(1)}, bf16[1,3,192,256]{3,2,1,0:T(8,128)(2,1)}, u32[]{:S(2)}) copy-start(bf16[1,3,192,256]{3,2,1,0:T(8,128)(2,1)} %copy-done.7) | copy-start | bytes 884740
  111.0 15.4 %all-to-all-start.4 = ((bf16[4,2,192,256]{3,2,1,0:T(8,128)(2,1)}), bf16[4,2,192,256]{3,2,1,0:T(8,128)(2,1)S(1)}, u32[]{:S(2)}, u32[]{:S(2)}) async-start(bf16[4,2,192,256]{3,2,1,0:T(8,128)(2,1)} %weight_terms.5), calls=%async_computation.4 | async-start | bytes 1572864 | tf_op jit(solution)/shard_map/all_to_all | solution.py:388
  122.8 11.0 %copy-start.11 = (bf16[192,256]{1,0:T(8,128)(2,1)S(1)}, bf16[192,256]{1,0:T(8,128)(2,1)}, u32[]{:S(2)}) copy-start(bf16[192,256]{1,0:T(8,128)(2,1)} %get-tuple-element.55) | copy-start | bytes 294916
  126.5 5.4 %collective-permute-start.14 = (bf16[192,256]{1,0:T(8,128)(2,1)}, bf16[192,256]{1,0:T(8,128)(2,1)S(1)}, u32[]{:S(2)}, u32[]{:S(2)}) collective-permute-start(bf16[192,256]{1,0:T(8,128)(2,1)} %get-tuple-element.56), channel_id=1, source_target_pairs={{0,128},{8,136},{16,144},{24,152},{32,160},{40,168},{48,176},{56,1... | collective-permute-start | bytes 294920 | tf_op jit(solution)/shard_map/ppermute | solution.py:314
  126.9 6.9 %collective-permute-start.15 = (bf16[192,256]{1,0:T(8,128)(2,1)}, bf16[192,256]{1,0:T(8,128)(2,1)S(1)}, u32[]{:S(2)}, u32[]{:S(2)}) collective-permute-start(bf16[192,256]{1,0:T(8,128)(2,1)} %get-tuple-element.57), channel_id=1, source_target_pairs={{0,64},{8,72},{16,80},{24,88},{32,96},{40,104},{48,112},{56,120},{... | collective-permute-start | bytes 294920 | tf_op jit(solution)/shard_map/ppermute | solution.py:314
  128.6 5.2 %collective-permute-start.16 = (bf16[192,256]{1,0:T(8,128)(2,1)}, bf16[192,256]{1,0:T(8,128)(2,1)S(1)}, u32[]{:S(2)}, u32[]{:S(2)}) collective-permute-start(bf16[192,256]{1,0:T(8,128)(2,1)} %get-tuple-element.58), channel_id=1, source_target_pairs={{0,192},{8,200},{16,208},{24,216},{32,224},{40,232},{48,240},{56,2... | collective-permute-start | bytes 294920 | tf_op jit(solution)/shard_map/ppermute | solution.py:314
  128.7 7.1 %collective-permute-start.22 = (bf16[192,256]{1,0:T(8,128)(2,1)S(1)}, bf16[192,256]{1,0:T(8,128)(2,1)S(1)}, u32[]{:S(2)}, u32[]{:S(2)}) collective-permute-start(bf16[192,256]{1,0:T(8,128)(2,1)S(1)} %get-tuple-element.67), channel_id=1, source_target_pairs={{0,192},{8,200},{16,208},{24,216},{32,224},{40,232},{48,240},{56,2... | collective-permute-start | bytes 294920 | tf_op jit(solution)/shard_map/ppermute | solution.py:314
  130.3 9.3 %collective-permute-start.21 = (bf16[192,256]{1,0:T(8,128)(2,1)S(1)}, bf16[192,256]{1,0:T(8,128)(2,1)S(1)}, u32[]{:S(2)}, u32[]{:S(2)}) collective-permute-start(bf16[192,256]{1,0:T(8,128)(2,1)S(1)} %get-tuple-element.68), channel_id=1, source_target_pairs={{0,64},{8,72},{16,80},{24,88},{32,96},{40,104},{48,112},{56,120},{... | collective-permute-start | bytes 294920 | tf_op jit(solution)/shard_map/ppermute | solution.py:314
  131.8 7.8 %collective-permute-start.20 = (bf16[192,256]{1,0:T(8,128)(2,1)S(1)}, bf16[192,256]{1,0:T(8,128)(2,1)S(1)}, u32[]{:S(2)}, u32[]{:S(2)}) collective-permute-start(bf16[192,256]{1,0:T(8,128)(2,1)S(1)} %select_bitcast_fusion.4), channel_id=1, source_target_pairs={{0,128},{8,136},{16,144},{24,152},{32,160},{40,168},{48,176},{56,1... | collective-permute-start | bytes 294920 | tf_op jit(solution)/shard_map/ppermute | solution.py:314
  133.9 5.7 %collective-permute-start.19 = (bf16[192,256]{1,0:T(8,128)(2,1)S(1)}, bf16[192,256]{1,0:T(8,128)(2,1)S(1)}, u32[]{:S(2)}, u32[]{:S(2)}) collective-permute-start(bf16[192,256]{1,0:T(8,128)(2,1)S(1)} %add_convert_fusion.5), channel_id=1, source_target_pairs={{0,48},{8,56},{64,112},{72,120},{128,176},{136,184},{192,240},{200... | collective-permute-start | bytes 294920 | tf_op jit(solution)/shard_map/ppermute | solution.py:431
  134.6 5.1 %collective-permute-start.18 = (bf16[192,256]{1,0:T(8,128)(2,1)S(1)}, bf16[192,256]{1,0:T(8,128)(2,1)S(1)}, u32[]{:S(2)}, u32[]{:S(2)}) collective-permute-start(bf16[192,256]{1,0:T(8,128)(2,1)S(1)} %add_convert_fusion.5), channel_id=1, source_target_pairs={{32,48},{40,56},{96,112},{104,120},{160,176},{168,184},{224,240},{... | collective-permute-start | bytes 294920 | tf_op jit(solution)/shard_map/ppermute | solution.py:431
  135.9 5.3 %collective-permute-start.17 = (bf16[192,256]{1,0:T(8,128)(2,1)S(1)}, bf16[192,256]{1,0:T(8,128)(2,1)S(1)}, u32[]{:S(2)}, u32[]{:S(2)}) collective-permute-start(bf16[192,256]{1,0:T(8,128)(2,1)S(1)} %add_convert_fusion.5), channel_id=1, source_target_pairs={{16,48},{24,56},{80,112},{88,120},{144,176},{152,184},{208,240},{2... | collective-permute-start | bytes 294920 | tf_op jit(solution)/shard_map/ppermute | solution.py:431
  141.3 13.9 %collective-permute-start.23 = (bf16[192,256]{1,0:T(8,128)(2,1)S(1)}, bf16[192,256]{1,0:T(8,128)(2,1)S(1)}, u32[]{:S(2)}, u32[]{:S(2)}) collective-permute-start(bf16[192,256]{1,0:T(8,128)(2,1)S(1)} %get-tuple-element.63), channel_id=1, source_target_pairs={{0,225},{1,2},{2,35},{3,68},{4,101},{5,134},{6,167},{7,192},{8,0},... | collective-permute-start | bytes 294920 | tf_op jit(solution)/shard_map/ppermute | solution.py:439
  153.2 13.0 %collective-permute-start.24 = (bf16[192,256]{1,0:T(8,128)(2,1)S(1)}, bf16[192,256]{1,0:T(8,128)(2,1)S(1)}, u32[]{:S(2)}, u32[]{:S(2)}) collective-permute-start(bf16[192,256]{1,0:T(8,128)(2,1)S(1)} %select_select_fusion), channel_id=1, source_target_pairs={{0,0},{1,33},{2,66},{3,99},{4,132},{5,165},{6,198},{7,231},{8,225}... | collective-permute-start | bytes 294920 | tf_op jit(solution)/shard_map/ppermute | solution.py:440

commit v6 on v5

--- a/solution.py
+++ b/solution.py
@@ -329,7 +329,7 @@
 
 
 HELD_AT_X = ((2, 1), (-2, -1), (3, 2), (-3, -2))
-HELD_AT_Y = ((0, 0), (1, 0), (-1, 0), (4, None))
+HELD_AT_Y = ((1, 0), (0, 0), (-1, 0), (4, None))
 LAST = 3
 LAST_STEP = (-3, 3)
 
@@ -410,7 +410,7 @@
     t1 = terms(near, [d1, u1], [(0, 0), (1, 1)])
     p0 = total(list(tie(p0, t1)[0]))
     p1 = exchange("y", t1)
-    c0 = choose([p0[0], p0[1], p0[2]], [0, 1, 2], y)
+    c0 = choose([p0[1], p0[0], p0[2]], [0, 1, 2], y)
     y0 = send_to("y", c0, [0, 1, 2])
 
     u2, d2, *y0 = tie(u2, d2, *y0, t1)[:5]

time: 168 us -> 166 us (0.988)
  the two profiles are of different devices: /device:TPU:13 before, /device:TPU:5 now
where the time goes in v6:
time: 166 us
  starting transfers between devices  65.3 us (39%)
  Pallas kernels  41.9 us (25%)
  blocking collectives  29.1 us (18%)
  waiting for transfers between devices  22.5 us (14%)
  other arithmetic  3.37 us (2%)
  local copies, waits for them, and re-layouts  2.35 us (1%)
    pallas_call x3, Pallas kernels, weight_terms(): pl.pallas_call(functools.partial(terms_kernel, scale, blocks, len(xs), le...  18.1 us
    all_to_all x1, blocking collectives, per_device(): lax.all_to_all(totals.reshape(n_seq, *totals.shape[2:]), 'seq', 0, 0)  14.9 us
    ppermute x1, starting transfers between devices, per_device(): first = lax.ppermute(first, both, owners(0, n_z))  14.5 us
    all_to_all x1, blocking collectives, per_device(): sums = lax.all_to_all(running_sums(spread), 'seq', 0, 0)  14.2 us
    all_to_all x3, starting transfers between devices, exchange(): return lax.all_to_all(pieces, 'seq', 0, 0, axis_index_groups=groups[axis])  13.7 us
    ppermute x6, starting transfers between devices, go(): return lax.ppermute(array, 'head', way)  10.7 us
    ppermute x3, starting transfers between devices, send_to(): lax.ppermute(chosen[d], 'seq', shift_to(axis, targets, d))  8.19 us
    pallas_call x1, Pallas kernels, query_key_gradients(): pl.pallas_call(functools.partial(query_key_kernel, scaling), grid=(heads,...  7.02 us
  transfers between devices with their start and end apart: 28, of which 9 were waited for; matrix products, arithmetic and copies ran while one was open for 1% of the time, Pallas kernels for 22%

profile of v6, /device:TPU:5, one launch (start us, length us, event | category | flops | bytes accessed | tf_op | source)
XLA Modules:
  0.0 165.5 jit_solution(5621939879569445624)
XLA Ops:
  0.6 0.0 copy-start.9
  0.6 5.4 %states.1 = (f32[4,128,128]{2,1,0:T(8,128)}, f32[4,128,128]{2,1,0:T(8,128)}, bf16[4,8,2,16,128]{4,3,2,1,0:T(8,128)(2,1)}, bf16[3,1024,256]{2,1,0:T(8,128)(2,1)}) custom-call(s32[1]{0:T(128)} %bitcast._, bf16[1024,512]{1,0:T(8,128)(2,1)} %q_ref.3, bf16[1024,512]{1,0:T(8,128)(2,1)} %k_ref.3, bf16[1024,512]{1,0:T(8,128)(2,1)} %v_ref.3, bf16[1024,512]{1,0:T(8,128)(2,1)} %o_ref.3), custom_call_target="tpu_custom_call" | custom-call | flops 1 | bytes 1 | tf_op jit(solution)/shard_map/states/pallas_call | solution.py:70
  6.0 0.7 collective-permute-start
  6.7 1.7 %collective-permute-start.3 = (bf16[1024,768]{1,0:T(8,128)(2,1)S(1)}, bf16[1024,768]{1,0:T(8,128)(2,1)S(1)}, u32[]{:S(2)}, u32[]{:S(2)}) collective-permute-start(bf16[1024,768]{1,0:T(8,128)(2,1)S(1)} %copy-done.9), channel_id=1, source_target_pairs={{0,1},{1,2},{2,3},{3,4},{4,5},{5,6},{6,7},{7,0},{8,9},{9,10},{10,1... | collective-permute-start | bytes 4718600 | tf_op jit(solution)/shard_map/ppermute | solution.py:374
  8.4 3.9 %collective-permute-start.4 = (bf16[1024,768]{1,0:T(8,128)(2,1)S(1)}, bf16[1024,768]{1,0:T(8,128)(2,1)S(1)}, u32[]{:S(2)}, u32[]{:S(2)}) collective-permute-start(bf16[1024,768]{1,0:T(8,128)(2,1)S(1)} %copy-done.9), channel_id=1, source_target_pairs={{0,7},{1,0},{2,1},{3,2},{4,3},{5,4},{6,5},{7,6},{8,15},{9,8},{10,9... | collective-permute-start | bytes 4718600 | tf_op jit(solution)/shard_map/ppermute | solution.py:374
  12.3 14.9 %all_to_all.25.in_ref = bf16[32,2,16,128]{3,2,1,0:T(8,128)(2,1)} all-to-all(bf16[32,2,16,128]{3,2,1,0:T(8,128)(2,1)} %bitcast.47), channel_id=1, replica_groups=mesh['seq'=32,'head'=8] {'seq'}, dimensions={0} | all-to-all | bytes 524288 | tf_op jit(solution)/shard_map/all_to_all | solution.py:392
  27.2 1.7 %running_sums.1 = bf16[32,3,16,128]{3,2,1,0:T(8,128)(2,1)} custom-call(bf16[32,2,16,128]{3,2,1,0:T(8,128)(2,1)} %all_to_all.25.in_ref), custom_call_target="tpu_custom_call" | custom-call | flops 1 | bytes 1 | tf_op jit(solution)/shard_map/running_sums/pallas_call | solution.py:108
  28.9 14.2 %all_to_all.26 = bf16[32,3,16,128]{3,2,1,0:T(8,128)(2,1)S(1)} all-to-all(bf16[32,3,16,128]{3,2,1,0:T(8,128)(2,1)} %running_sums.1), channel_id=1, replica_groups=mesh['seq'=32,'head'=8] {'seq'}, dimensions={0} | all-to-all | bytes 786432 | tf_op jit(solution)/shard_map/all_to_all | solution.py:393
  43.1 4.4 %value_gradient.1.refs_6_ = bf16[2,1024,256]{2,1,0:T(8,128)(2,1)S(1)} custom-call(s32[1]{0:T(128)} %bitcast._, bf16[1024,512]{1,0:T(8,128)(2,1)} %q_ref.3, bf16[1024,512]{1,0:T(8,128)(2,1)} %k_ref.3, bf16[1024,512]{1,0:T(8,128)(2,1)} %o_ref.3, bf16[3,1024,256]{2,1,0:T(8,128)(2,1)} %collective-permute-done.refs_3_.refs_4_.refs_5_, ...), custom_call_target="tpu_custom_call" | custom-call | flops 1 | bytes 1 | tf_op jit(solution)/shard_map/value_gradient/pallas_call | solution.py:166
  47.5 0.0 copy-start.1
  47.5 0.0 collective-permute-done.3.refs_2_.refs_0_
  47.6 0.3 collective-permute-start.5
  47.8 0.3 collective-permute-start.6
  48.2 0.2 collective-permute-start.7
  48.3 2.5 %collective-permute-start.2 = (bf16[2,1024,256]{2,1,0:T(8,128)(2,1)S(1)}, bf16[2,1024,256]{2,1,0:T(8,128)(2,1)}, u32[]{:S(2)}, u32[]{:S(2)}) collective-permute-start(bf16[2,1024,256]{2,1,0:T(8,128)(2,1)S(1)} %value_gradient.1.refs_6_), channel_id=1, source_target_pairs={{0,7},{1,0},{2,1},{3,2},{4,3},{5,4},{6,5},{7,6},{8,15},{9,8},{10,9... | collective-permute-start | bytes 3145736 | tf_op jit(solution)/shard_map/ppermute | solution.py:374
  50.8 0.3 collective-permute-done.5.refs_1_
  51.1 4.5 %collective-permute-done.6.refs_3_.refs_1_ = bf16[1024,768]{1,0:T(8,128)(2,1)S(1)} collective-permute-done((bf16[1024,768]{1,0:T(8,128)(2,1)S(1)}, bf16[1024,768]{1,0:T(8,128)(2,1)S(1)}, u32[]{:S(2)}, u32[]{:S(2)}) %collective-permute-start.6) | collective-permute-done | bytes 1572896 | tf_op jit(solution)/shard_map/ppermute | solution.py:377
  55.6 1.2 copy-done.4
  56.8 6.9 %weight_terms.3 = bf16[4,3,192,256]{3,2,1,0:T(8,128)(2,1)} custom-call(bf16[1024,768]{1,0:T(8,128)(2,1)} %refs_0_.2, bf16[1024,768]{1,0:T(8,128)(2,1)} %copy-done.10, bf16[1024,768]{1,0:T(8,128)(2,1)} %copy-done.2, bf16[1024,768]{1,0:T(8,128)(2,1)} %copy-done.4, bf16[1024,768]{1,0:T(8,128)(2,1)} %copy-done.3, ...), custom_call_target="tpu_custom_call" | custom-call | flops 1 | bytes 1 | tf_op jit(solution)/shard_map/weight_terms/pallas_call | solution.py:232
  63.6 5.4 %all-to-all-start.2 = ((bf16[4,3,192,256]{3,2,1,0:T(8,128)(2,1)}), bf16[4,3,192,256]{3,2,1,0:T(8,128)(2,1)S(1)}, u32[]{:S(2)}, u32[]{:S(2)}) async-start(bf16[4,3,192,256]{3,2,1,0:T(8,128)(2,1)} %weight_terms.3), calls=%async_computation.2 | async-start | bytes 2359296 | tf_op jit(solution)/shard_map/all_to_all | solution.py:388
  69.1 7.0 %query_key_gradients.1 = (bf16[1024,512]{1,0:T(8,128)(2,1)}, bf16[1024,512]{1,0:T(8,128)(2,1)}) custom-call(bf16[1024,512]{1,0:T(8,128)(2,1)} %q_ref.3, bf16[1024,512]{1,0:T(8,128)(2,1)} %k_ref.3, bf16[1024,512]{1,0:T(8,128)(2,1)} %v_ref.3, bf16[1024,512]{1,0:T(8,128)(2,1)} %o_ref.3, bf16[4,8,3,16,128]{4,3,2,1,0:T(8,128)(2,1)} %bitcast.45, ...), custom_call_target="tpu_custom_call" | custom-call | flops 1 | bytes 1 | tf_op jit(solution)/shard_map/query_key_gradients/pallas_call | solution.py:203
  76.1 0.0 collective-permute-done.2.refs_4_
  76.1 0.5 collective-permute-done.1.refs_5_
  76.6 2.7 %collective-permute-start.9 = (bf16[2,1024,256]{2,1,0:T(8,128)(2,1)}, bf16[2,1024,256]{2,1,0:T(8,128)(2,1)S(1)}, u32[]{:S(2)}, u32[]{:S(2)}) collective-permute-start(bf16[2,1024,256]{2,1,0:T(8,128)(2,1)} %collective-permute-done.2.refs_4_), channel_id=1, source_target_pairs={{0,7},{1,0},{2,1},{3,2},{4,3},{5,4},{6,5},{7,6},{8,15},{9,8},{10,9... | collective-permute-start | bytes 3145736 | tf_op jit(solution)/shard_map/ppermute | solution.py:374
  79.3 5.6 %weight_terms.4 = bf16[4,2,192,256]{3,2,1,0:T(8,128)(2,1)} custom-call(bf16[1024,768]{1,0:T(8,128)(2,1)} %copy-done.2, bf16[1024,768]{1,0:T(8,128)(2,1)} %copy-done.4, bf16[1024,768]{1,0:T(8,128)(2,1)} %copy-done.3, bf16[1024,768]{1,0:T(8,128)(2,1)} %collective-permute-done.7.refs_5_.refs_3_, bf16[2,1024,256]{2,1,0:T(8,128)(2,1)} %collective-permute-done.2.refs_4_, ...), custom_call_target="tpu_custom_call" | custom-call | flops 1 | bytes 1 | tf_op jit(solution)/shard_map/weight_terms/pallas_call | solution.py:232
  84.9 0.0 all-to-all-done.2
  84.9 0.1 add_convert_fusion
  85.1 0.0 copy-start.7
  85.1 0.7 copy-done.7
  85.8 1.3 collective-permute-start.12
  87.1 4.0 %collective-permute-start.11 = (bf16[192,256]{1,0:T(8,128)(2,1)S(1)}, bf16[192,256]{1,0:T(8,128)(2,1)S(1)}, u32[]{:S(2)}, u32[]{:S(2)}) collective-permute-start(bf16[192,256]{1,0:T(8,128)(2,1)S(1)} %get-tuple-element.70), channel_id=1, source_target_pairs={{0,16},{8,24},{16,32},{24,40},{48,0},{56,8},{64,80},{72,88},{80,96... | collective-permute-start | bytes 294920 | tf_op jit(solution)/shard_map/ppermute | solution.py:328
  91.1 2.9 %collective-permute-start.10 = (bf16[192,256]{1,0:T(8,128)(2,1)S(1)}, bf16[192,256]{1,0:T(8,128)(2,1)S(1)}, u32[]{:S(2)}, u32[]{:S(2)}) collective-permute-start(bf16[192,256]{1,0:T(8,128)(2,1)S(1)} %get-tuple-element.71), channel_id=1, source_target_pairs={{0,32},{8,40},{32,0},{40,8},{48,16},{56,24},{64,96},{72,104},{96,6... | collective-permute-start | bytes 294920 | tf_op jit(solution)/shard_map/ppermute | solution.py:328
  94.0 4.0 %all-to-all-start.3 = ((bf16[4,2,192,256]{3,2,1,0:T(8,128)(2,1)}), bf16[4,2,192,256]{3,2,1,0:T(8,128)(2,1)S(1)}, u32[]{:S(2)}, u32[]{:S(2)}) async-start(bf16[4,2,192,256]{3,2,1,0:T(8,128)(2,1)} %weight_terms.4), calls=%async_computation.3 | async-start | bytes 1572864 | tf_op jit(solution)/shard_map/all_to_all | solution.py:388
  98.0 3.6 %collective-permute-done.8.refs_5_ = bf16[2,1024,256]{2,1,0:T(8,128)(2,1)S(1)} collective-permute-done((bf16[2,1024,256]{2,1,0:T(8,128)(2,1)}, bf16[2,1024,256]{2,1,0:T(8,128)(2,1)S(1)}, u32[]{:S(2)}, u32[]{:S(2)}) %collective-permute-start.8) | collective-permute-done | bytes 1048608 | tf_op jit(solution)/shard_map/ppermute | solution.py:374
  101.6 1.2 broadcast_select_fusion
  102.8 0.1 copy-done.5
  103.0 0.3 copy-done.6
  103.3 2.1 %collective-permute-start.13 = (bf16[2,1024,256]{2,1,0:T(8,128)(2,1)}, bf16[2,1024,256]{2,1,0:T(8,128)(2,1)}, u32[]{:S(2)}, u32[]{:S(2)}) collective-permute-start(bf16[2,1024,256]{2,1,0:T(8,128)(2,1)} %broadcast_select_fusion), channel_id=1, source_target_pairs={{0,1},{1,2},{2,3},{3,4},{4,5},{5,6},{6,7},{7,0},{8,15},{9,8},{10,9... | collective-permute-start | bytes 3145736 | tf_op jit(solution)/shard_map/ppermute | solution.py:417
  105.4 5.6 %weight_terms.5 = bf16[4,2,192,256]{3,2,1,0:T(8,128)(2,1)} custom-call(bf16[1024,768]{1,0:T(8,128)(2,1)} %copy-done.2, bf16[1024,768]{1,0:T(8,128)(2,1)} %copy-done.4, bf16[1024,768]{1,0:T(8,128)(2,1)} %copy-done.3, bf16[1024,768]{1,0:T(8,128)(2,1)} %collective-permute-done.7.refs_5_.refs_3_, bf16[2,1024,256]{2,1,0:T(8,128)(2,1)} %copy-done.6, ...), custom_call_target="tpu_custom_call" | custom-call | flops 1 | bytes 1 | tf_op jit(solution)/shard_map/weight_terms/pallas_call | solution.py:232
  111.0 4.3 %all-to-all-start.4 = ((bf16[4,2,192,256]{3,2,1,0:T(8,128)(2,1)}), bf16[4,2,192,256]{3,2,1,0:T(8,128)(2,1)S(1)}, u32[]{:S(2)}, u32[]{:S(2)}) async-start(bf16[4,2,192,256]{3,2,1,0:T(8,128)(2,1)} %weight_terms.5), calls=%async_computation.4 | async-start | bytes 1572864 | tf_op jit(solution)/shard_map/all_to_all | solution.py:388
  115.3 0.6 pad_add_fusion.at_ref
  115.9 0.1 fusion
  116.0 0.1 fusion.3
  116.1 1.4 collective-permute-done.13.refs_4_
  117.5 5.3 %last_terms.1 = (bf16[192,256]{1,0:T(8,128)(2,1)}, bf16[192,256]{1,0:T(8,128)(2,1)}, bf16[192,256]{1,0:T(8,128)(2,1)}, bf16[192,256]{1,0:T(8,128)(2,1)}) custom-call(s32[2]{0:T(128)} %pad_add_fusion.at_ref, bf16[1024,768]{1,0:T(8,128)(2,1)} %copy-done.2, bf16[1024,768]{1,0:T(8,128)(2,1)} %copy-done.4, bf16[1024,768]{1,0:T(8,128)(2,1)} %copy-done.3, ...), custom_call_target="tpu_custom_call" | custom-call | flops 1 | bytes 1 | tf_op jit(solution)/shard_map/last_terms/pallas_call | solution.py:271
  122.8 4.6 %all-to-all-done.4 = bf16[4,2,192,256]{3,2,1,0:T(8,128)(2,1)S(1)} async-done(((bf16[4,2,192,256]{3,2,1,0:T(8,128)(2,1)}), bf16[4,2,192,256]{3,2,1,0:T(8,128)(2,1)S(1)}, u32[]{:S(2)}, u32[]{:S(2)}) %all-to-all-start.4) | async-done | bytes 786464 | tf_op jit(solution)/shard_map/all_to_all | solution.py:388
  127.4 0.1 add_convert_fusion.1
  127.5 0.5 collective-permute-start.14
  128.0 1.7 %collective-permute-start.15 = (bf16[192,256]{1,0:T(8,128)(2,1)}, bf16[192,256]{1,0:T(8,128)(2,1)S(1)}, u32[]{:S(2)}, u32[]{:S(2)}) collective-permute-start(bf16[192,256]{1,0:T(8,128)(2,1)} %get-tuple-element.57), channel_id=1, source_target_pairs={{0,64},{8,72},{16,80},{24,88},{32,96},{40,104},{48,112},{56,120},{... | collective-permute-start | bytes 294920 | tf_op jit(solution)/shard_map/ppermute | solution.py:314
  129.6 0.1 collective-permute-start.16
  129.8 1.5 collective-permute-start.22
  131.3 0.4 collective-permute-start.21
  131.7 1.2 collective-permute-done.14
  132.9 2.0 %collective-permute-start.20 = (bf16[192,256]{1,0:T(8,128)(2,1)S(1)}, bf16[192,256]{1,0:T(8,128)(2,1)S(1)}, u32[]{:S(2)}, u32[]{:S(2)}) collective-permute-start(bf16[192,256]{1,0:T(8,128)(2,1)S(1)} %select_bitcast_fusion.4), channel_id=1, source_target_pairs={{0,128},{8,136},{16,144},{24,152},{32,160},{40,168},{48,176},{56,1... | collective-permute-start | bytes 294920 | tf_op jit(solution)/shard_map/ppermute | solution.py:314
  134.8 0.1 add_convert_fusion.5
  134.9 2.8 %collective-permute-start.19 = (bf16[192,256]{1,0:T(8,128)(2,1)S(1)}, bf16[192,256]{1,0:T(8,128)(2,1)S(1)}, u32[]{:S(2)}, u32[]{:S(2)}) collective-permute-start(bf16[192,256]{1,0:T(8,128)(2,1)S(1)} %add_convert_fusion.5), channel_id=1, source_target_pairs={{0,48},{8,56},{64,112},{72,120},{128,176},{136,184},{192,240},{200... | collective-permute-start | bytes 294920 | tf_op jit(solution)/shard_map/ppermute | solution.py:431
  137.7 0.7 collective-permute-start.18
  138.4 0.7 collective-permute-start.17
  139.1 0.2 collective-permute-done.19
  139.3 0.1 select_select_fusion.1
  139.5 14.5 %collective-permute-start.23 = (bf16[192,256]{1,0:T(8,128)(2,1)S(1)}, bf16[192,256]{1,0:T(8,128)(2,1)S(1)}, u32[]{:S(2)}, u32[]{:S(2)}) collective-permute-start(bf16[192,256]{1,0:T(8,128)(2,1)S(1)} %get-tuple-element.63), channel_id=1, source_target_pairs={{0,225},{1,2},{2,35},{3,68},{4,101},{5,134},{6,167},{7,192},{8,224... | collective-permute-start | bytes 294920 | tf_op jit(solution)/shard_map/ppermute | solution.py:439
  153.9 4.4 %collective-permute-start.24 = (bf16[192,256]{1,0:T(8,128)(2,1)S(1)}, bf16[192,256]{1,0:T(8,128)(2,1)S(1)}, u32[]{:S(2)}, u32[]{:S(2)}) collective-permute-start(bf16[192,256]{1,0:T(8,128)(2,1)S(1)} %select_select_fusion), channel_id=1, source_target_pairs={{0,224},{1,1},{2,34},{3,67},{4,100},{5,133},{6,166},{7,199},{8,225... | collective-permute-start | bytes 294920 | tf_op jit(solution)/shard_map/ppermute | solution.py:440
  158.4 6.3 %collective-permute-done.24 = bf16[192,256]{1,0:T(8,128)(2,1)S(1)} collective-permute-done((bf16[192,256]{1,0:T(8,128)(2,1)S(1)}, bf16[192,256]{1,0:T(8,128)(2,1)S(1)}, u32[]{:S(2)}, u32[]{:S(2)}) %collective-permute-start.24) | collective-permute-done | bytes 98336 | tf_op jit(solution)/shard_map/ppermute | solution.py:440
  164.7 0.8 maximum_convert_fusion
  (40 shorter events, 0.2 us)
Async XLA Ops:
  0.6 6.1 %copy-start.9 = (bf16[1024,768]{1,0:T(8,128)(2,1)S(1)}, bf16[1024,768]{1,0:T(8,128)(2,1)}, u32[]{:S(2)}) copy-start(bf16[1024,768]{1,0:T(8,128)(2,1)} %refs_0_.2) | copy-start | bytes 4718596
  6.0 37.1 %collective-permute-start = (bf16[3,1024,256]{2,1,0:T(8,128)(2,1)}, bf16[3,1024,256]{2,1,0:T(8,128)(2,1)}, u32[]{:S(2)}, u32[]{:S(2)}) collective-permute-start(bf16[3,1024,256]{2,1,0:T(8,128)(2,1)} %get-tuple-element.33), channel_id=1, source_target_pairs={{0,8},{8,0},{16,24},{24,16},{32,40},{40,32},{48,56},{56,48},{64,72... | collective-permute-start | bytes 4718600 | tf_op jit(solution)/shard_map/ppermute | solution.py:377
  6.7 40.8 %collective-permute-start.3 = (bf16[1024,768]{1,0:T(8,128)(2,1)S(1)}, bf16[1024,768]{1,0:T(8,128)(2,1)S(1)}, u32[]{:S(2)}, u32[]{:S(2)}) collective-permute-start(bf16[1024,768]{1,0:T(8,128)(2,1)S(1)} %copy-done.9), channel_id=1, source_target_pairs={{0,1},{1,2},{2,3},{3,4},{4,5},{5,6},{6,7},{7,0},{8,9},{9,10},{10,1... | collective-permute-start | bytes 4718600 | tf_op jit(solution)/shard_map/ppermute | solution.py:374
  8.4 39.2 %collective-permute-start.4 = (bf16[1024,768]{1,0:T(8,128)(2,1)S(1)}, bf16[1024,768]{1,0:T(8,128)(2,1)S(1)}, u32[]{:S(2)}, u32[]{:S(2)}) collective-permute-start(bf16[1024,768]{1,0:T(8,128)(2,1)S(1)} %copy-done.9), channel_id=1, source_target_pairs={{0,7},{1,0},{2,1},{3,2},{4,3},{5,4},{6,5},{7,6},{8,15},{9,8},{10,9... | collective-permute-start | bytes 4718600 | tf_op jit(solution)/shard_map/ppermute | solution.py:374
  43.1 4.4 %copy-start = (bf16[32,3,16,128]{3,2,1,0:T(8,128)(2,1)}, bf16[32,3,16,128]{3,2,1,0:T(8,128)(2,1)S(1)}, u32[]{:S(2)}) copy-start(bf16[32,3,16,128]{3,2,1,0:T(8,128)(2,1)S(1)} %all_to_all.26) | copy-start | bytes 1179652
  47.5 9.2 %copy-start.1 = (bf16[2,1024,256]{2,1,0:T(8,128)(2,1)}, bf16[2,1024,256]{2,1,0:T(8,128)(2,1)S(1)}, u32[]{:S(2)}) copy-start(bf16[2,1024,256]{2,1,0:T(8,128)(2,1)S(1)} %value_gradient.1.refs_6_) | copy-start | bytes 3145732
  47.5 9.2 %copy-start.2 = (bf16[1024,768]{1,0:T(8,128)(2,1)}, bf16[1024,768]{1,0:T(8,128)(2,1)S(1)}, u32[]{:S(2)}) copy-start(bf16[1024,768]{1,0:T(8,128)(2,1)S(1)} %collective-permute-done.3.refs_2_.refs_0_) | copy-start | bytes 4718596
  47.6 9.2 %copy-start.3 = (bf16[1024,768]{1,0:T(8,128)(2,1)}, bf16[1024,768]{1,0:T(8,128)(2,1)S(1)}, u32[]{:S(2)}) copy-start(bf16[1024,768]{1,0:T(8,128)(2,1)S(1)} %collective-permute-done.4.refs_4_.refs_2_) | copy-start | bytes 4718596
  47.6 3.5 %collective-permute-start.5 = (bf16[1024,768]{1,0:T(8,128)(2,1)S(1)}, bf16[1024,768]{1,0:T(8,128)(2,1)S(1)}, u32[]{:S(2)}, u32[]{:S(2)}) collective-permute-start(bf16[1024,768]{1,0:T(8,128)(2,1)S(1)} %copy-done.9), channel_id=1, source_target_pairs={{0,8},{8,0},{16,24},{24,16},{32,40},{40,32},{48,56},{56,48},{64,72... | collective-permute-start | bytes 4718600 | tf_op jit(solution)/shard_map/ppermute | solution.py:377
  47.8 7.7 %collective-permute-start.6 = (bf16[1024,768]{1,0:T(8,128)(2,1)S(1)}, bf16[1024,768]{1,0:T(8,128)(2,1)S(1)}, u32[]{:S(2)}, u32[]{:S(2)}) collective-permute-start(bf16[1024,768]{1,0:T(8,128)(2,1)S(1)} %collective-permute-done.3.refs_2_.refs_0_), channel_id=1, source_target_pairs={{0,8},{8,0},{16,24},{24,16},{32,40},{40,32},{48,56},{56,48},{64,72... | collective-permute-start | bytes 4718600 | tf_op jit(solution)/shard_map/ppermute | solution.py:377
  48.2 8.6 %collective-permute-start.7 = (bf16[1024,768]{1,0:T(8,128)(2,1)S(1)}, bf16[1024,768]{1,0:T(8,128)(2,1)}, u32[]{:S(2)}, u32[]{:S(2)}) collective-permute-start(bf16[1024,768]{1,0:T(8,128)(2,1)S(1)} %collective-permute-done.4.refs_4_.refs_2_), channel_id=1, source_target_pairs={{0,8},{8,0},{16,24},{24,16},{32,40},{40,32},{48,56},{56,48},{64,72... | collective-permute-start | bytes 4718600 | tf_op jit(solution)/shard_map/ppermute | solution.py:377
  48.3 27.7 %collective-permute-start.2 = (bf16[2,1024,256]{2,1,0:T(8,128)(2,1)S(1)}, bf16[2,1024,256]{2,1,0:T(8,128)(2,1)}, u32[]{:S(2)}, u32[]{:S(2)}) collective-permute-start(bf16[2,1024,256]{2,1,0:T(8,128)(2,1)S(1)} %value_gradient.1.refs_6_), channel_id=1, source_target_pairs={{0,7},{1,0},{2,1},{3,2},{4,3},{5,4},{6,5},{7,6},{8,15},{9,8},{10,9... | collective-permute-start | bytes 3145736 | tf_op jit(solution)/shard_map/ppermute | solution.py:374
  50.8 25.8 %collective-permute-start.1 = (bf16[2,1024,256]{2,1,0:T(8,128)(2,1)S(1)}, bf16[2,1024,256]{2,1,0:T(8,128)(2,1)}, u32[]{:S(2)}, u32[]{:S(2)}) collective-permute-start(bf16[2,1024,256]{2,1,0:T(8,128)(2,1)S(1)} %value_gradient.1.refs_6_), channel_id=1, source_target_pairs={{0,1},{1,2},{2,3},{3,4},{4,5},{5,6},{6,7},{7,0},{8,9},{9,10},{10,1... | collective-permute-start | bytes 3145736 | tf_op jit(solution)/shard_map/ppermute | solution.py:374
  51.1 4.5 %copy-start.10 = (bf16[1024,768]{1,0:T(8,128)(2,1)}, bf16[1024,768]{1,0:T(8,128)(2,1)S(1)}, u32[]{:S(2)}) copy-start(bf16[1024,768]{1,0:T(8,128)(2,1)S(1)} %collective-permute-done.5.refs_1_) | copy-start | bytes 4718596
  55.6 1.2 copy-start.4
  63.6 21.3 %all-to-all-start.2 = ((bf16[4,3,192,256]{3,2,1,0:T(8,128)(2,1)}), bf16[4,3,192,256]{3,2,1,0:T(8,128)(2,1)S(1)}, u32[]{:S(2)}, u32[]{:S(2)}) async-start(bf16[4,3,192,256]{3,2,1,0:T(8,128)(2,1)} %weight_terms.3), calls=%async_computation.2 | async-start | bytes 2359296 | tf_op jit(solution)/shard_map/all_to_all | solution.py:388
  76.6 25.0 %collective-permute-start.8 = (bf16[2,1024,256]{2,1,0:T(8,128)(2,1)}, bf16[2,1024,256]{2,1,0:T(8,128)(2,1)S(1)}, u32[]{:S(2)}, u32[]{:S(2)}) collective-permute-start(bf16[2,1024,256]{2,1,0:T(8,128)(2,1)} %collective-permute-done.1.refs_5_), channel_id=1, source_target_pairs={{0,1},{1,2},{2,3},{3,4},{4,5},{5,6},{6,7},{7,0},{8,9},{9,10},{10,1... | collective-permute-start | bytes 3145736 | tf_op jit(solution)/shard_map/ppermute | solution.py:374
  76.6 25.0 %collective-permute-start.9 = (bf16[2,1024,256]{2,1,0:T(8,128)(2,1)}, bf16[2,1024,256]{2,1,0:T(8,128)(2,1)S(1)}, u32[]{:S(2)}, u32[]{:S(2)}) collective-permute-start(bf16[2,1024,256]{2,1,0:T(8,128)(2,1)} %collective-permute-done.2.refs_4_), channel_id=1, source_target_pairs={{0,7},{1,0},{2,1},{3,2},{4,3},{5,4},{6,5},{7,6},{8,15},{9,8},{10,9... | collective-permute-start | bytes 3145736 | tf_op jit(solution)/shard_map/ppermute | solution.py:374
  85.1 0.7 copy-start.7
  85.8 12.2 %collective-permute-start.12 = (bf16[192,256]{1,0:T(8,128)(2,1)S(1)}, bf16[192,256]{1,0:T(8,128)(2,1)S(1)}, u32[]{:S(2)}, u32[]{:S(2)}) collective-permute-start(bf16[192,256]{1,0:T(8,128)(2,1)S(1)} %get-tuple-element.69), channel_id=1, source_target_pairs={{16,0},{24,8},{32,16},{40,24},{48,32},{56,40},{80,64},{88,72},{96,... | collective-permute-start | bytes 294920 | tf_op jit(solution)/shard_map/ppermute | solution.py:328
  87.1 10.9 %collective-permute-start.11 = (bf16[192,256]{1,0:T(8,128)(2,1)S(1)}, bf16[192,256]{1,0:T(8,128)(2,1)S(1)}, u32[]{:S(2)}, u32[]{:S(2)}) collective-permute-start(bf16[192,256]{1,0:T(8,128)(2,1)S(1)} %get-tuple-element.70), channel_id=1, source_target_pairs={{0,16},{8,24},{16,32},{24,40},{48,0},{56,8},{64,80},{72,88},{80,96... | collective-permute-start | bytes 294920 | tf_op jit(solution)/shard_map/ppermute | solution.py:328
  91.1 6.9 %collective-permute-start.10 = (bf16[192,256]{1,0:T(8,128)(2,1)S(1)}, bf16[192,256]{1,0:T(8,128)(2,1)S(1)}, u32[]{:S(2)}, u32[]{:S(2)}) collective-permute-start(bf16[192,256]{1,0:T(8,128)(2,1)S(1)} %get-tuple-element.71), channel_id=1, source_target_pairs={{0,32},{8,40},{32,0},{40,8},{48,16},{56,24},{64,96},{72,104},{96,6... | collective-permute-start | bytes 294920 | tf_op jit(solution)/shard_map/ppermute | solution.py:328
  94.0 16.9 %all-to-all-start.3 = ((bf16[4,2,192,256]{3,2,1,0:T(8,128)(2,1)}), bf16[4,2,192,256]{3,2,1,0:T(8,128)(2,1)S(1)}, u32[]{:S(2)}, u32[]{:S(2)}) async-start(bf16[4,2,192,256]{3,2,1,0:T(8,128)(2,1)} %weight_terms.4), calls=%async_computation.3 | async-start | bytes 1572864 | tf_op jit(solution)/shard_map/all_to_all | solution.py:388
  101.6 1.4 copy-start.5
  101.6 1.7 %copy-start.6 = (bf16[2,1024,256]{2,1,0:T(8,128)(2,1)}, bf16[2,1024,256]{2,1,0:T(8,128)(2,1)S(1)}, u32[]{:S(2)}) copy-start(bf16[2,1024,256]{2,1,0:T(8,128)(2,1)S(1)} %collective-permute-done.9.refs_4_) | copy-start | bytes 3145732
  103.3 14.3 %collective-permute-start.13 = (bf16[2,1024,256]{2,1,0:T(8,128)(2,1)}, bf16[2,1024,256]{2,1,0:T(8,128)(2,1)}, u32[]{:S(2)}, u32[]{:S(2)}) collective-permute-start(bf16[2,1024,256]{2,1,0:T(8,128)(2,1)} %broadcast_select_fusion), channel_id=1, source_target_pairs={{0,1},{1,2},{2,3},{3,4},{4,5},{5,6},{6,7},{7,0},{8,15},{9,8},{10,9... | collective-permute-start | bytes 3145736 | tf_op jit(solution)/shard_map/ppermute | solution.py:417
  111.0 5.1 %copy-start.8 = (bf16[1,3,192,256]{3,2,1,0:T(8,128)(2,1)S(1)}, bf16[1,3,192,256]{3,2,1,0:T(8,128)(2,1)}, u32[]{:S(2)}) copy-start(bf16[1,3,192,256]{3,2,1,0:T(8,128)(2,1)} %copy-done.7) | copy-start | bytes 884740
  111.0 16.4 %all-to-all-start.4 = ((bf16[4,2,192,256]{3,2,1,0:T(8,128)(2,1)}), bf16[4,2,192,256]{3,2,1,0:T(8,128)(2,1)S(1)}, u32[]{:S(2)}, u32[]{:S(2)}) async-start(bf16[4,2,192,256]{3,2,1,0:T(8,128)(2,1)} %weight_terms.5), calls=%async_computation.4 | async-start | bytes 1572864 | tf_op jit(solution)/shard_map/all_to_all | solution.py:388
  122.8 12.0 %copy-start.11 = (bf16[192,256]{1,0:T(8,128)(2,1)S(1)}, bf16[192,256]{1,0:T(8,128)(2,1)}, u32[]{:S(2)}) copy-start(bf16[192,256]{1,0:T(8,128)(2,1)} %get-tuple-element.55) | copy-start | bytes 294916
  127.5 5.4 %collective-permute-start.14 = (bf16[192,256]{1,0:T(8,128)(2,1)}, bf16[192,256]{1,0:T(8,128)(2,1)S(1)}, u32[]{:S(2)}, u32[]{:S(2)}) collective-permute-start(bf16[192,256]{1,0:T(8,128)(2,1)} %get-tuple-element.56), channel_id=1, source_target_pairs={{0,128},{8,136},{16,144},{24,152},{32,160},{40,168},{48,176},{56,1... | collective-permute-start | bytes 294920 | tf_op jit(solution)/shard_map/ppermute | solution.py:314
  128.0 6.9 %collective-permute-start.15 = (bf16[192,256]{1,0:T(8,128)(2,1)}, bf16[192,256]{1,0:T(8,128)(2,1)S(1)}, u32[]{:S(2)}, u32[]{:S(2)}) collective-permute-start(bf16[192,256]{1,0:T(8,128)(2,1)} %get-tuple-element.57), channel_id=1, source_target_pairs={{0,64},{8,72},{16,80},{24,88},{32,96},{40,104},{48,112},{56,120},{... | collective-permute-start | bytes 294920 | tf_op jit(solution)/shard_map/ppermute | solution.py:314
  129.6 5.2 %collective-permute-start.16 = (bf16[192,256]{1,0:T(8,128)(2,1)}, bf16[192,256]{1,0:T(8,128)(2,1)S(1)}, u32[]{:S(2)}, u32[]{:S(2)}) collective-permute-start(bf16[192,256]{1,0:T(8,128)(2,1)} %get-tuple-element.58), channel_id=1, source_target_pairs={{0,192},{8,200},{16,208},{24,216},{32,224},{40,232},{48,240},{56,2... | collective-permute-start | bytes 294920 | tf_op jit(solution)/shard_map/ppermute | solution.py:314
  129.8 8.6 %collective-permute-start.22 = (bf16[192,256]{1,0:T(8,128)(2,1)S(1)}, bf16[192,256]{1,0:T(8,128)(2,1)S(1)}, u32[]{:S(2)}, u32[]{:S(2)}) collective-permute-start(bf16[192,256]{1,0:T(8,128)(2,1)S(1)} %get-tuple-element.67), channel_id=1, source_target_pairs={{0,192},{8,200},{16,208},{24,216},{32,224},{40,232},{48,240},{56,2... | collective-permute-start | bytes 294920 | tf_op jit(solution)/shard_map/ppermute | solution.py:314
  131.3 7.8 %collective-permute-start.21 = (bf16[192,256]{1,0:T(8,128)(2,1)S(1)}, bf16[192,256]{1,0:T(8,128)(2,1)S(1)}, u32[]{:S(2)}, u32[]{:S(2)}) collective-permute-start(bf16[192,256]{1,0:T(8,128)(2,1)S(1)} %get-tuple-element.68), channel_id=1, source_target_pairs={{0,64},{8,72},{16,80},{24,88},{32,96},{40,104},{48,112},{56,120},{... | collective-permute-start | bytes 294920 | tf_op jit(solution)/shard_map/ppermute | solution.py:314
  132.9 6.2 %collective-permute-start.20 = (bf16[192,256]{1,0:T(8,128)(2,1)S(1)}, bf16[192,256]{1,0:T(8,128)(2,1)S(1)}, u32[]{:S(2)}, u32[]{:S(2)}) collective-permute-start(bf16[192,256]{1,0:T(8,128)(2,1)S(1)} %select_bitcast_fusion.4), channel_id=1, source_target_pairs={{0,128},{8,136},{16,144},{24,152},{32,160},{40,168},{48,176},{56,1... | collective-permute-start | bytes 294920 | tf_op jit(solution)/shard_map/ppermute | solution.py:314
  134.9 4.4 %collective-permute-start.19 = (bf16[192,256]{1,0:T(8,128)(2,1)S(1)}, bf16[192,256]{1,0:T(8,128)(2,1)S(1)}, u32[]{:S(2)}, u32[]{:S(2)}) collective-permute-start(bf16[192,256]{1,0:T(8,128)(2,1)S(1)} %add_convert_fusion.5), channel_id=1, source_target_pairs={{0,48},{8,56},{64,112},{72,120},{128,176},{136,184},{192,240},{200... | collective-permute-start | bytes 294920 | tf_op jit(solution)/shard_map/ppermute | solution.py:431
  137.7 1.6 collective-permute-start.18
  138.4 0.9 collective-permute-start.17
  139.5 19.0 %collective-permute-start.23 = (bf16[192,256]{1,0:T(8,128)(2,1)S(1)}, bf16[192,256]{1,0:T(8,128)(2,1)S(1)}, u32[]{:S(2)}, u32[]{:S(2)}) collective-permute-start(bf16[192,256]{1,0:T(8,128)(2,1)S(1)} %get-tuple-element.63), channel_id=1, source_target_pairs={{0,225},{1,2},{2,35},{3,68},{4,101},{5,134},{6,167},{7,192},{8,224... | collective-permute-start | bytes 294920 | tf_op jit(solution)/shard_map/ppermute | solution.py:439
  153.9 10.7 %collective-permute-start.24 = (bf16[192,256]{1,0:T(8,128)(2,1)S(1)}, bf16[192,256]{1,0:T(8,128)(2,1)S(1)}, u32[]{:S(2)}, u32[]{:S(2)}) collective-permute-start(bf16[192,256]{1,0:T(8,128)(2,1)S(1)} %select_select_fusion), channel_id=1, source_target_pairs={{0,224},{1,1},{2,34},{3,67},{4,100},{5,133},{6,166},{7,199},{8,225... | collective-permute-start | bytes 294920 | tf_op jit(solution)/shard_map/ppermute | solution.py:440

commit v7 on v6

--- a/solution.py
+++ b/solution.py
@@ -279,7 +279,7 @@
             out_specs=[pl.BlockSpec(shape, lambda r, s: (0, 0))] * 4,
         ),
         out_shape=[jax.ShapeDtypeStruct(shape, BF16)] * 4,
-        compiler_params=params(),
+        compiler_params=params(52),
         cost_estimate=QUICK,
         name="last_terms",
     )(at, *xs, v)

time: 166 us -> 166 us (level)
  transfers between devices with their start and end apart: 28 -> 28, of which waited for: 9 -> 9; matrix products, arithmetic and copies ran while one was open for 1% -> 2% of each run, Pallas kernels for 22% -> 21%
where the time goes in v7:
time: 166 us; the launch traced here: 165 us
  starting transfers between devices  65.5 us (39%)
  Pallas kernels  40.5 us (24%)
  blocking collectives  29.1 us (18%)
  waiting for transfers between devices  22.7 us (14%)
  other arithmetic  4.02 us (2%)
  local copies, waits for them, and re-layouts  2.41 us (1%)
    pallas_call x3, Pallas kernels, weight_terms(): pl.pallas_call(functools.partial(terms_kernel, scale, blocks, len(xs), le...  18.1 us
    all_to_all x1, blocking collectives, per_device(): lax.all_to_all(totals.reshape(n_seq, *totals.shape[2:]), 'seq', 0, 0)  14.9 us
    ppermute x1, starting transfers between devices, per_device(): first = lax.ppermute(first, both, owners(0, n_z))  14.3 us
    all_to_all x1, blocking collectives, per_device(): sums = lax.all_to_all(running_sums(spread), 'seq', 0, 0)  14.2 us
    all_to_all x3, starting transfers between devices, exchange(): return lax.all_to_all(pieces, 'seq', 0, 0, axis_index_groups=groups[axis])  13.9 us
    ppermute x6, starting transfers between devices, go(): return lax.ppermute(array, 'head', way)  10.7 us
    ppermute x3, starting transfers between devices, send_to(): lax.ppermute(chosen[d], 'seq', shift_to(axis, targets, d))  8.19 us
    pallas_call x1, Pallas kernels, query_key_gradients(): pl.pallas_call(functools.partial(query_key_kernel, scaling), grid=(heads,...  7.03 us
  transfers between devices with their start and end apart: 28, of which 9 were waited for; matrix products, arithmetic and copies ran while one was open for 2% of the time, Pallas kernels for 21%

profile of v7, /device:TPU:5, one launch (start us, length us, event | category | flops | bytes accessed | tf_op | source)
XLA Modules:
  0.0 165.2 jit_solution(13544012182046729611)
XLA Ops:
  0.6 0.0 copy-start.9
  0.6 5.4 %states.1 = (f32[4,128,128]{2,1,0:T(8,128)}, f32[4,128,128]{2,1,0:T(8,128)}, bf16[4,8,2,16,128]{4,3,2,1,0:T(8,128)(2,1)}, bf16[3,1024,256]{2,1,0:T(8,128)(2,1)}) custom-call(s32[1]{0:T(128)} %bitcast._, bf16[1024,512]{1,0:T(8,128)(2,1)} %q_ref.3, bf16[1024,512]{1,0:T(8,128)(2,1)} %k_ref.3, bf16[1024,512]{1,0:T(8,128)(2,1)} %v_ref.3, bf16[1024,512]{1,0:T(8,128)(2,1)} %o_ref.3), custom_call_target="tpu_custom_call" | custom-call | flops 1 | bytes 1 | tf_op jit(solution)/shard_map/states/pallas_call | solution.py:70
  6.0 0.7 collective-permute-start
  6.7 1.7 %collective-permute-start.3 = (bf16[1024,768]{1,0:T(8,128)(2,1)S(1)}, bf16[1024,768]{1,0:T(8,128)(2,1)S(1)}, u32[]{:S(2)}, u32[]{:S(2)}) collective-permute-start(bf16[1024,768]{1,0:T(8,128)(2,1)S(1)} %copy-done.9), channel_id=1, source_target_pairs={{0,1},{1,2},{2,3},{3,4},{4,5},{5,6},{6,7},{7,0},{8,9},{9,10},{10,1... | collective-permute-start | bytes 4718600 | tf_op jit(solution)/shard_map/ppermute | solution.py:374
  8.4 3.9 %collective-permute-start.4 = (bf16[1024,768]{1,0:T(8,128)(2,1)S(1)}, bf16[1024,768]{1,0:T(8,128)(2,1)S(1)}, u32[]{:S(2)}, u32[]{:S(2)}) collective-permute-start(bf16[1024,768]{1,0:T(8,128)(2,1)S(1)} %copy-done.9), channel_id=1, source_target_pairs={{0,7},{1,0},{2,1},{3,2},{4,3},{5,4},{6,5},{7,6},{8,15},{9,8},{10,9... | collective-permute-start | bytes 4718600 | tf_op jit(solution)/shard_map/ppermute | solution.py:374
  12.3 14.9 %all_to_all.25.in_ref = bf16[32,2,16,128]{3,2,1,0:T(8,128)(2,1)} all-to-all(bf16[32,2,16,128]{3,2,1,0:T(8,128)(2,1)} %bitcast.47), channel_id=1, replica_groups=mesh['seq'=32,'head'=8] {'seq'}, dimensions={0} | all-to-all | bytes 524288 | tf_op jit(solution)/shard_map/all_to_all | solution.py:392
  27.2 1.7 %running_sums.1 = bf16[32,3,16,128]{3,2,1,0:T(8,128)(2,1)} custom-call(bf16[32,2,16,128]{3,2,1,0:T(8,128)(2,1)} %all_to_all.25.in_ref), custom_call_target="tpu_custom_call" | custom-call | flops 1 | bytes 1 | tf_op jit(solution)/shard_map/running_sums/pallas_call | solution.py:108
  28.9 14.2 %all_to_all.26 = bf16[32,3,16,128]{3,2,1,0:T(8,128)(2,1)S(1)} all-to-all(bf16[32,3,16,128]{3,2,1,0:T(8,128)(2,1)} %running_sums.1), channel_id=1, replica_groups=mesh['seq'=32,'head'=8] {'seq'}, dimensions={0} | all-to-all | bytes 786432 | tf_op jit(solution)/shard_map/all_to_all | solution.py:393
  43.1 0.0 collective-permute-done.refs_3_.refs_4_.refs_5_
  43.1 4.4 %value_gradient.1.refs_6_ = bf16[2,1024,256]{2,1,0:T(8,128)(2,1)S(1)} custom-call(s32[1]{0:T(128)} %bitcast._, bf16[1024,512]{1,0:T(8,128)(2,1)} %q_ref.3, bf16[1024,512]{1,0:T(8,128)(2,1)} %k_ref.3, bf16[1024,512]{1,0:T(8,128)(2,1)} %o_ref.3, bf16[3,1024,256]{2,1,0:T(8,128)(2,1)} %collective-permute-done.refs_3_.refs_4_.refs_5_, ...), custom_call_target="tpu_custom_call" | custom-call | flops 1 | bytes 1 | tf_op jit(solution)/shard_map/value_gradient/pallas_call | solution.py:166
  47.5 0.0 copy-start.1
  47.6 0.0 collective-permute-done.4.refs_4_.refs_2_
  47.6 0.3 collective-permute-start.5
  47.8 0.3 collective-permute-start.6
  48.2 0.2 collective-permute-start.7
  48.3 2.5 %collective-permute-start.2 = (bf16[2,1024,256]{2,1,0:T(8,128)(2,1)S(1)}, bf16[2,1024,256]{2,1,0:T(8,128)(2,1)}, u32[]{:S(2)}, u32[]{:S(2)}) collective-permute-start(bf16[2,1024,256]{2,1,0:T(8,128)(2,1)S(1)} %value_gradient.1.refs_6_), channel_id=1, source_target_pairs={{0,7},{1,0},{2,1},{3,2},{4,3},{5,4},{6,5},{7,6},{8,15},{9,8},{10,9... | collective-permute-start | bytes 3145736 | tf_op jit(solution)/shard_map/ppermute | solution.py:374
  50.8 0.0 collective-permute-start.1
  50.8 0.3 collective-permute-done.5.refs_1_
  51.1 4.5 %collective-permute-done.6.refs_3_.refs_1_ = bf16[1024,768]{1,0:T(8,128)(2,1)S(1)} collective-permute-done((bf16[1024,768]{1,0:T(8,128)(2,1)S(1)}, bf16[1024,768]{1,0:T(8,128)(2,1)S(1)}, u32[]{:S(2)}, u32[]{:S(2)}) %collective-permute-start.6) | collective-permute-done | bytes 1572896 | tf_op jit(solution)/shard_map/ppermute | solution.py:377
  55.6 1.2 copy-done.4
  56.8 6.9 %weight_terms.3 = bf16[4,3,192,256]{3,2,1,0:T(8,128)(2,1)} custom-call(bf16[1024,768]{1,0:T(8,128)(2,1)} %refs_0_.2, bf16[1024,768]{1,0:T(8,128)(2,1)} %copy-done.10, bf16[1024,768]{1,0:T(8,128)(2,1)} %copy-done.2, bf16[1024,768]{1,0:T(8,128)(2,1)} %copy-done.4, bf16[1024,768]{1,0:T(8,128)(2,1)} %copy-done.3, ...), custom_call_target="tpu_custom_call" | custom-call | flops 1 | bytes 1 | tf_op jit(solution)/shard_map/weight_terms/pallas_call | solution.py:232
  63.7 5.4 %all-to-all-start.2 = ((bf16[4,3,192,256]{3,2,1,0:T(8,128)(2,1)}), bf16[4,3,192,256]{3,2,1,0:T(8,128)(2,1)S(1)}, u32[]{:S(2)}, u32[]{:S(2)}) async-start(bf16[4,3,192,256]{3,2,1,0:T(8,128)(2,1)} %weight_terms.3), calls=%async_computation.2 | async-start | bytes 2359296 | tf_op jit(solution)/shard_map/all_to_all | solution.py:388
  69.1 7.0 %query_key_gradients.1 = (bf16[1024,512]{1,0:T(8,128)(2,1)}, bf16[1024,512]{1,0:T(8,128)(2,1)}) custom-call(bf16[1024,512]{1,0:T(8,128)(2,1)} %q_ref.3, bf16[1024,512]{1,0:T(8,128)(2,1)} %k_ref.3, bf16[1024,512]{1,0:T(8,128)(2,1)} %v_ref.3, bf16[1024,512]{1,0:T(8,128)(2,1)} %o_ref.3, bf16[4,8,3,16,128]{4,3,2,1,0:T(8,128)(2,1)} %bitcast.45, ...), custom_call_target="tpu_custom_call" | custom-call | flops 1 | bytes 1 | tf_op jit(solution)/shard_map/query_key_gradients/pallas_call | solution.py:203
  76.1 0.5 collective-permute-done.1.refs_5_
  76.6 2.7 %collective-permute-start.9 = (bf16[2,1024,256]{2,1,0:T(8,128)(2,1)}, bf16[2,1024,256]{2,1,0:T(8,128)(2,1)S(1)}, u32[]{:S(2)}, u32[]{:S(2)}) collective-permute-start(bf16[2,1024,256]{2,1,0:T(8,128)(2,1)} %collective-permute-done.2.refs_4_), channel_id=1, source_target_pairs={{0,7},{1,0},{2,1},{3,2},{4,3},{5,4},{6,5},{7,6},{8,15},{9,8},{10,9... | collective-permute-start | bytes 3145736 | tf_op jit(solution)/shard_map/ppermute | solution.py:374
  79.3 5.6 %weight_terms.4 = bf16[4,2,192,256]{3,2,1,0:T(8,128)(2,1)} custom-call(bf16[1024,768]{1,0:T(8,128)(2,1)} %copy-done.2, bf16[1024,768]{1,0:T(8,128)(2,1)} %copy-done.4, bf16[1024,768]{1,0:T(8,128)(2,1)} %copy-done.3, bf16[1024,768]{1,0:T(8,128)(2,1)} %collective-permute-done.7.refs_5_.refs_3_, bf16[2,1024,256]{2,1,0:T(8,128)(2,1)} %collective-permute-done.2.refs_4_, ...), custom_call_target="tpu_custom_call" | custom-call | flops 1 | bytes 1 | tf_op jit(solution)/shard_map/weight_terms/pallas_call | solution.py:232
  84.9 0.1 add_convert_fusion
  85.0 0.0 copy-start.7
  85.0 0.7 copy-done.7
  85.8 1.3 collective-permute-start.12
  87.1 4.0 %collective-permute-start.11 = (bf16[192,256]{1,0:T(8,128)(2,1)S(1)}, bf16[192,256]{1,0:T(8,128)(2,1)S(1)}, u32[]{:S(2)}, u32[]{:S(2)}) collective-permute-start(bf16[192,256]{1,0:T(8,128)(2,1)S(1)} %get-tuple-element.70), channel_id=1, source_target_pairs={{0,16},{8,24},{16,32},{24,40},{48,0},{56,8},{64,80},{72,88},{80,96... | collective-permute-start | bytes 294920 | tf_op jit(solution)/shard_map/ppermute | solution.py:328
  91.1 2.9 %collective-permute-start.10 = (bf16[192,256]{1,0:T(8,128)(2,1)S(1)}, bf16[192,256]{1,0:T(8,128)(2,1)S(1)}, u32[]{:S(2)}, u32[]{:S(2)}) collective-permute-start(bf16[192,256]{1,0:T(8,128)(2,1)S(1)} %get-tuple-element.71), channel_id=1, source_target_pairs={{0,32},{8,40},{32,0},{40,8},{48,16},{56,24},{64,96},{72,104},{96,6... | collective-permute-start | bytes 294920 | tf_op jit(solution)/shard_map/ppermute | solution.py:328
  94.0 4.2 %all-to-all-start.3 = ((bf16[4,2,192,256]{3,2,1,0:T(8,128)(2,1)}), bf16[4,2,192,256]{3,2,1,0:T(8,128)(2,1)}, u32[]{:S(2)}, u32[]{:S(2)}) async-start(bf16[4,2,192,256]{3,2,1,0:T(8,128)(2,1)} %weight_terms.4), calls=%async_computation.3 | async-start | bytes 1572864 | tf_op jit(solution)/shard_map/all_to_all | solution.py:388
  98.2 3.3 %collective-permute-done.8.refs_5_ = bf16[2,1024,256]{2,1,0:T(8,128)(2,1)S(1)} collective-permute-done((bf16[2,1024,256]{2,1,0:T(8,128)(2,1)}, bf16[2,1024,256]{2,1,0:T(8,128)(2,1)S(1)}, u32[]{:S(2)}, u32[]{:S(2)}) %collective-permute-start.8) | collective-permute-done | bytes 1048608 | tf_op jit(solution)/shard_map/ppermute | solution.py:374
  101.6 1.2 broadcast_select_fusion
  102.8 0.1 copy-done.5
  102.8 0.4 copy-done.6
  103.3 2.0 %collective-permute-start.13 = (bf16[2,1024,256]{2,1,0:T(8,128)(2,1)}, bf16[2,1024,256]{2,1,0:T(8,128)(2,1)S(1)}, u32[]{:S(2)}, u32[]{:S(2)}) collective-permute-start(bf16[2,1024,256]{2,1,0:T(8,128)(2,1)} %broadcast_select_fusion), channel_id=1, source_target_pairs={{0,1},{1,2},{2,3},{3,4},{4,5},{5,6},{6,7},{7,0},{8,15},{9,8},{10,9... | collective-permute-start | bytes 3145736 | tf_op jit(solution)/shard_map/ppermute | solution.py:417
  105.3 5.6 %weight_terms.5 = bf16[4,2,192,256]{3,2,1,0:T(8,128)(2,1)} custom-call(bf16[1024,768]{1,0:T(8,128)(2,1)} %copy-done.2, bf16[1024,768]{1,0:T(8,128)(2,1)} %copy-done.4, bf16[1024,768]{1,0:T(8,128)(2,1)} %copy-done.3, bf16[1024,768]{1,0:T(8,128)(2,1)} %collective-permute-done.7.refs_5_.refs_3_, bf16[2,1024,256]{2,1,0:T(8,128)(2,1)} %copy-done.6, ...), custom_call_target="tpu_custom_call" | custom-call | flops 1 | bytes 1 | tf_op jit(solution)/shard_map/weight_terms/pallas_call | solution.py:232
  110.9 4.3 %all-to-all-start.4 = ((bf16[4,2,192,256]{3,2,1,0:T(8,128)(2,1)}), bf16[4,2,192,256]{3,2,1,0:T(8,128)(2,1)S(1)}, u32[]{:S(2)}, u32[]{:S(2)}) async-start(bf16[4,2,192,256]{3,2,1,0:T(8,128)(2,1)} %weight_terms.5), calls=%async_computation.4 | async-start | bytes 1572864 | tf_op jit(solution)/shard_map/all_to_all | solution.py:388
  115.2 0.1 pad_add_fusion.at_ref
  115.3 1.3 fusion
  116.6 0.1 fusion.3
  116.7 0.7 collective-permute-done.13.refs_4_
  117.4 3.9 %last_terms.1 = (bf16[192,256]{1,0:T(8,128)(2,1)S(1)}, bf16[192,256]{1,0:T(8,128)(2,1)S(1)}, bf16[192,256]{1,0:T(8,128)(2,1)S(1)}, bf16[192,256]{1,0:T(8,128)(2,1)S(1)}) custom-call(s32[2]{0:T(128)S(1)} %pad_add_fusion.at_ref, bf16[1024,768]{1,0:T(8,128)(2,1)} %copy-done.2, bf16[1024,768]{1,0:T(8,128)(2,1)} %copy-done.4, bf16[1024,768]{1,0:T(8,128)(2,1)} %copy-done.3, ...), custom_call_target="tpu_custom_call" | custom-call | flops 1 | bytes 1 | tf_op jit(solution)/shard_map/last_terms/pallas_call | solution.py:271
  121.3 5.9 %all-to-all-done.4 = bf16[4,2,192,256]{3,2,1,0:T(8,128)(2,1)S(1)} async-done(((bf16[4,2,192,256]{3,2,1,0:T(8,128)(2,1)}), bf16[4,2,192,256]{3,2,1,0:T(8,128)(2,1)S(1)}, u32[]{:S(2)}, u32[]{:S(2)}) %all-to-all-start.4) | async-done | bytes 786464 | tf_op jit(solution)/shard_map/all_to_all | solution.py:388
  127.2 0.1 add_convert_fusion.1
  127.3 0.5 collective-permute-start.14
  127.8 1.6 collective-permute-start.15
  129.4 0.1 collective-permute-start.16
  129.6 1.5 collective-permute-start.22
  131.1 0.4 collective-permute-start.21
  131.5 1.0 collective-permute-done.14
  132.4 2.2 %collective-permute-start.20 = (bf16[192,256]{1,0:T(8,128)(2,1)S(1)}, bf16[192,256]{1,0:T(8,128)(2,1)S(1)}, u32[]{:S(2)}, u32[]{:S(2)}) collective-permute-start(bf16[192,256]{1,0:T(8,128)(2,1)S(1)} %select_bitcast_fusion.4), channel_id=1, source_target_pairs={{0,128},{8,136},{16,144},{24,152},{32,160},{40,168},{48,176},{56,1... | collective-permute-start | bytes 294920 | tf_op jit(solution)/shard_map/ppermute | solution.py:314
  134.6 0.1 add_convert_fusion.5
  134.7 2.8 %collective-permute-start.19 = (bf16[192,256]{1,0:T(8,128)(2,1)S(1)}, bf16[192,256]{1,0:T(8,128)(2,1)S(1)}, u32[]{:S(2)}, u32[]{:S(2)}) collective-permute-start(bf16[192,256]{1,0:T(8,128)(2,1)S(1)} %add_convert_fusion.5), channel_id=1, source_target_pairs={{0,48},{8,56},{64,112},{72,120},{128,176},{136,184},{192,240},{200... | collective-permute-start | bytes 294920 | tf_op jit(solution)/shard_map/ppermute | solution.py:431
  137.5 0.7 collective-permute-start.18
  138.2 0.7 collective-permute-start.17
  138.9 0.2 collective-permute-done.19
  139.1 0.1 select_select_fusion.1
  139.3 14.3 %collective-permute-start.23 = (bf16[192,256]{1,0:T(8,128)(2,1)S(1)}, bf16[192,256]{1,0:T(8,128)(2,1)S(1)}, u32[]{:S(2)}, u32[]{:S(2)}) collective-permute-start(bf16[192,256]{1,0:T(8,128)(2,1)S(1)} %get-tuple-element.63), channel_id=1, source_target_pairs={{0,225},{1,2},{2,35},{3,68},{4,101},{5,134},{6,167},{7,192},{8,224... | collective-permute-start | bytes 294920 | tf_op jit(solution)/shard_map/ppermute | solution.py:439
  153.6 4.4 %collective-permute-start.24 = (bf16[192,256]{1,0:T(8,128)(2,1)S(1)}, bf16[192,256]{1,0:T(8,128)(2,1)S(1)}, u32[]{:S(2)}, u32[]{:S(2)}) collective-permute-start(bf16[192,256]{1,0:T(8,128)(2,1)S(1)} %select_select_fusion), channel_id=1, source_target_pairs={{0,224},{1,1},{2,34},{3,67},{4,100},{5,133},{6,166},{7,199},{8,225... | collective-permute-start | bytes 294920 | tf_op jit(solution)/shard_map/ppermute | solution.py:440
  158.0 6.3 %collective-permute-done.24 = bf16[192,256]{1,0:T(8,128)(2,1)S(1)} collective-permute-done((bf16[192,256]{1,0:T(8,128)(2,1)S(1)}, bf16[192,256]{1,0:T(8,128)(2,1)S(1)}, u32[]{:S(2)}, u32[]{:S(2)}) %collective-permute-start.24) | collective-permute-done | bytes 98336 | tf_op jit(solution)/shard_map/ppermute | solution.py:440
  164.4 0.8 maximum_convert_fusion
  (38 shorter events, 0.2 us)
Async XLA Ops:
  0.6 6.1 %copy-start.9 = (bf16[1024,768]{1,0:T(8,128)(2,1)S(1)}, bf16[1024,768]{1,0:T(8,128)(2,1)}, u32[]{:S(2)}) copy-start(bf16[1024,768]{1,0:T(8,128)(2,1)} %refs_0_.2) | copy-start | bytes 4718596
  6.0 37.1 %collective-permute-start = (bf16[3,1024,256]{2,1,0:T(8,128)(2,1)}, bf16[3,1024,256]{2,1,0:T(8,128)(2,1)}, u32[]{:S(2)}, u32[]{:S(2)}) collective-permute-start(bf16[3,1024,256]{2,1,0:T(8,128)(2,1)} %get-tuple-element.33), channel_id=1, source_target_pairs={{0,8},{8,0},{16,24},{24,16},{32,40},{40,32},{48,56},{56,48},{64,72... | collective-permute-start | bytes 4718600 | tf_op jit(solution)/shard_map/ppermute | solution.py:377
  6.7 40.8 %collective-permute-start.3 = (bf16[1024,768]{1,0:T(8,128)(2,1)S(1)}, bf16[1024,768]{1,0:T(8,128)(2,1)S(1)}, u32[]{:S(2)}, u32[]{:S(2)}) collective-permute-start(bf16[1024,768]{1,0:T(8,128)(2,1)S(1)} %copy-done.9), channel_id=1, source_target_pairs={{0,1},{1,2},{2,3},{3,4},{4,5},{5,6},{6,7},{7,0},{8,9},{9,10},{10,1... | collective-permute-start | bytes 4718600 | tf_op jit(solution)/shard_map/ppermute | solution.py:374
  8.4 39.2 %collective-permute-start.4 = (bf16[1024,768]{1,0:T(8,128)(2,1)S(1)}, bf16[1024,768]{1,0:T(8,128)(2,1)S(1)}, u32[]{:S(2)}, u32[]{:S(2)}) collective-permute-start(bf16[1024,768]{1,0:T(8,128)(2,1)S(1)} %copy-done.9), channel_id=1, source_target_pairs={{0,7},{1,0},{2,1},{3,2},{4,3},{5,4},{6,5},{7,6},{8,15},{9,8},{10,9... | collective-permute-start | bytes 4718600 | tf_op jit(solution)/shard_map/ppermute | solution.py:374
  43.1 4.4 %copy-start = (bf16[32,3,16,128]{3,2,1,0:T(8,128)(2,1)}, bf16[32,3,16,128]{3,2,1,0:T(8,128)(2,1)S(1)}, u32[]{:S(2)}) copy-start(bf16[32,3,16,128]{3,2,1,0:T(8,128)(2,1)S(1)} %all_to_all.26) | copy-start | bytes 1179652
  47.5 9.2 %copy-start.1 = (bf16[2,1024,256]{2,1,0:T(8,128)(2,1)}, bf16[2,1024,256]{2,1,0:T(8,128)(2,1)S(1)}, u32[]{:S(2)}) copy-start(bf16[2,1024,256]{2,1,0:T(8,128)(2,1)S(1)} %value_gradient.1.refs_6_) | copy-start | bytes 3145732
  47.5 9.2 %copy-start.2 = (bf16[1024,768]{1,0:T(8,128)(2,1)}, bf16[1024,768]{1,0:T(8,128)(2,1)S(1)}, u32[]{:S(2)}) copy-start(bf16[1024,768]{1,0:T(8,128)(2,1)S(1)} %collective-permute-done.3.refs_2_.refs_0_) | copy-start | bytes 4718596
  47.6 9.2 %copy-start.3 = (bf16[1024,768]{1,0:T(8,128)(2,1)}, bf16[1024,768]{1,0:T(8,128)(2,1)S(1)}, u32[]{:S(2)}) copy-start(bf16[1024,768]{1,0:T(8,128)(2,1)S(1)} %collective-permute-done.4.refs_4_.refs_2_) | copy-start | bytes 4718596
  47.6 3.5 %collective-permute-start.5 = (bf16[1024,768]{1,0:T(8,128)(2,1)S(1)}, bf16[1024,768]{1,0:T(8,128)(2,1)S(1)}, u32[]{:S(2)}, u32[]{:S(2)}) collective-permute-start(bf16[1024,768]{1,0:T(8,128)(2,1)S(1)} %copy-done.9), channel_id=1, source_target_pairs={{0,8},{8,0},{16,24},{24,16},{32,40},{40,32},{48,56},{56,48},{64,72... | collective-permute-start | bytes 4718600 | tf_op jit(solution)/shard_map/ppermute | solution.py:377
  47.8 7.7 %collective-permute-start.6 = (bf16[1024,768]{1,0:T(8,128)(2,1)S(1)}, bf16[1024,768]{1,0:T(8,128)(2,1)S(1)}, u32[]{:S(2)}, u32[]{:S(2)}) collective-permute-start(bf16[1024,768]{1,0:T(8,128)(2,1)S(1)} %collective-permute-done.3.refs_2_.refs_0_), channel_id=1, source_target_pairs={{0,8},{8,0},{16,24},{24,16},{32,40},{40,32},{48,56},{56,48},{64,72... | collective-permute-start | bytes 4718600 | tf_op jit(solution)/shard_map/ppermute | solution.py:377
  48.2 8.6 %collective-permute-start.7 = (bf16[1024,768]{1,0:T(8,128)(2,1)S(1)}, bf16[1024,768]{1,0:T(8,128)(2,1)}, u32[]{:S(2)}, u32[]{:S(2)}) collective-permute-start(bf16[1024,768]{1,0:T(8,128)(2,1)S(1)} %collective-permute-done.4.refs_4_.refs_2_), channel_id=1, source_target_pairs={{0,8},{8,0},{16,24},{24,16},{32,40},{40,32},{48,56},{56,48},{64,72... | collective-permute-start | bytes 4718600 | tf_op jit(solution)/shard_map/ppermute | solution.py:377
  48.3 27.8 %collective-permute-start.2 = (bf16[2,1024,256]{2,1,0:T(8,128)(2,1)S(1)}, bf16[2,1024,256]{2,1,0:T(8,128)(2,1)}, u32[]{:S(2)}, u32[]{:S(2)}) collective-permute-start(bf16[2,1024,256]{2,1,0:T(8,128)(2,1)S(1)} %value_gradient.1.refs_6_), channel_id=1, source_target_pairs={{0,7},{1,0},{2,1},{3,2},{4,3},{5,4},{6,5},{7,6},{8,15},{9,8},{10,9... | collective-permute-start | bytes 3145736 | tf_op jit(solution)/shard_map/ppermute | solution.py:374
  50.8 25.8 %collective-permute-start.1 = (bf16[2,1024,256]{2,1,0:T(8,128)(2,1)S(1)}, bf16[2,1024,256]{2,1,0:T(8,128)(2,1)}, u32[]{:S(2)}, u32[]{:S(2)}) collective-permute-start(bf16[2,1024,256]{2,1,0:T(8,128)(2,1)S(1)} %value_gradient.1.refs_6_), channel_id=1, source_target_pairs={{0,1},{1,2},{2,3},{3,4},{4,5},{5,6},{6,7},{7,0},{8,9},{9,10},{10,1... | collective-permute-start | bytes 3145736 | tf_op jit(solution)/shard_map/ppermute | solution.py:374
  51.1 4.5 %copy-start.10 = (bf16[1024,768]{1,0:T(8,128)(2,1)}, bf16[1024,768]{1,0:T(8,128)(2,1)S(1)}, u32[]{:S(2)}) copy-start(bf16[1024,768]{1,0:T(8,128)(2,1)S(1)} %collective-permute-done.5.refs_1_) | copy-start | bytes 4718596
  55.6 1.2 copy-start.4
  63.7 21.2 %all-to-all-start.2 = ((bf16[4,3,192,256]{3,2,1,0:T(8,128)(2,1)}), bf16[4,3,192,256]{3,2,1,0:T(8,128)(2,1)S(1)}, u32[]{:S(2)}, u32[]{:S(2)}) async-start(bf16[4,3,192,256]{3,2,1,0:T(8,128)(2,1)} %weight_terms.3), calls=%async_computation.2 | async-start | bytes 2359296 | tf_op jit(solution)/shard_map/all_to_all | solution.py:388
  76.6 25.0 %collective-permute-start.8 = (bf16[2,1024,256]{2,1,0:T(8,128)(2,1)}, bf16[2,1024,256]{2,1,0:T(8,128)(2,1)S(1)}, u32[]{:S(2)}, u32[]{:S(2)}) collective-permute-start(bf16[2,1024,256]{2,1,0:T(8,128)(2,1)} %collective-permute-done.1.refs_5_), channel_id=1, source_target_pairs={{0,1},{1,2},{2,3},{3,4},{4,5},{5,6},{6,7},{7,0},{8,9},{9,10},{10,1... | collective-permute-start | bytes 3145736 | tf_op jit(solution)/shard_map/ppermute | solution.py:374
  76.6 25.0 %collective-permute-start.9 = (bf16[2,1024,256]{2,1,0:T(8,128)(2,1)}, bf16[2,1024,256]{2,1,0:T(8,128)(2,1)S(1)}, u32[]{:S(2)}, u32[]{:S(2)}) collective-permute-start(bf16[2,1024,256]{2,1,0:T(8,128)(2,1)} %collective-permute-done.2.refs_4_), channel_id=1, source_target_pairs={{0,7},{1,0},{2,1},{3,2},{4,3},{5,4},{6,5},{7,6},{8,15},{9,8},{10,9... | collective-permute-start | bytes 3145736 | tf_op jit(solution)/shard_map/ppermute | solution.py:374
  85.0 0.7 copy-start.7
  85.8 12.4 %collective-permute-start.12 = (bf16[192,256]{1,0:T(8,128)(2,1)S(1)}, bf16[192,256]{1,0:T(8,128)(2,1)S(1)}, u32[]{:S(2)}, u32[]{:S(2)}) collective-permute-start(bf16[192,256]{1,0:T(8,128)(2,1)S(1)} %get-tuple-element.69), channel_id=1, source_target_pairs={{16,0},{24,8},{32,16},{40,24},{48,32},{56,40},{80,64},{88,72},{96,... | collective-permute-start | bytes 294920 | tf_op jit(solution)/shard_map/ppermute | solution.py:328
  87.1 11.1 %collective-permute-start.11 = (bf16[192,256]{1,0:T(8,128)(2,1)S(1)}, bf16[192,256]{1,0:T(8,128)(2,1)S(1)}, u32[]{:S(2)}, u32[]{:S(2)}) collective-permute-start(bf16[192,256]{1,0:T(8,128)(2,1)S(1)} %get-tuple-element.70), channel_id=1, source_target_pairs={{0,16},{8,24},{16,32},{24,40},{48,0},{56,8},{64,80},{72,88},{80,96... | collective-permute-start | bytes 294920 | tf_op jit(solution)/shard_map/ppermute | solution.py:328
  91.1 7.2 %collective-permute-start.10 = (bf16[192,256]{1,0:T(8,128)(2,1)S(1)}, bf16[192,256]{1,0:T(8,128)(2,1)S(1)}, u32[]{:S(2)}, u32[]{:S(2)}) collective-permute-start(bf16[192,256]{1,0:T(8,128)(2,1)S(1)} %get-tuple-element.71), channel_id=1, source_target_pairs={{0,32},{8,40},{32,0},{40,8},{48,16},{56,24},{64,96},{72,104},{96,6... | collective-permute-start | bytes 294920 | tf_op jit(solution)/shard_map/ppermute | solution.py:328
  94.0 16.9 %all-to-all-start.3 = ((bf16[4,2,192,256]{3,2,1,0:T(8,128)(2,1)}), bf16[4,2,192,256]{3,2,1,0:T(8,128)(2,1)}, u32[]{:S(2)}, u32[]{:S(2)}) async-start(bf16[4,2,192,256]{3,2,1,0:T(8,128)(2,1)} %weight_terms.4), calls=%async_computation.3 | async-start | bytes 1572864 | tf_op jit(solution)/shard_map/all_to_all | solution.py:388
  101.6 1.3 copy-start.5
  101.6 1.7 %copy-start.6 = (bf16[2,1024,256]{2,1,0:T(8,128)(2,1)}, bf16[2,1024,256]{2,1,0:T(8,128)(2,1)S(1)}, u32[]{:S(2)}) copy-start(bf16[2,1024,256]{2,1,0:T(8,128)(2,1)S(1)} %collective-permute-done.9.refs_4_) | copy-start | bytes 3145732
  103.3 14.2 %collective-permute-start.13 = (bf16[2,1024,256]{2,1,0:T(8,128)(2,1)}, bf16[2,1024,256]{2,1,0:T(8,128)(2,1)S(1)}, u32[]{:S(2)}, u32[]{:S(2)}) collective-permute-start(bf16[2,1024,256]{2,1,0:T(8,128)(2,1)} %broadcast_select_fusion), channel_id=1, source_target_pairs={{0,1},{1,2},{2,3},{3,4},{4,5},{5,6},{6,7},{7,0},{8,15},{9,8},{10,9... | collective-permute-start | bytes 3145736 | tf_op jit(solution)/shard_map/ppermute | solution.py:417
  110.9 5.7 %copy-start.8 = (bf16[1,3,192,256]{3,2,1,0:T(8,128)(2,1)S(1)}, bf16[1,3,192,256]{3,2,1,0:T(8,128)(2,1)}, u32[]{:S(2)}) copy-start(bf16[1,3,192,256]{3,2,1,0:T(8,128)(2,1)} %copy-done.7) | copy-start | bytes 884740
  110.9 16.3 %all-to-all-start.4 = ((bf16[4,2,192,256]{3,2,1,0:T(8,128)(2,1)}), bf16[4,2,192,256]{3,2,1,0:T(8,128)(2,1)S(1)}, u32[]{:S(2)}, u32[]{:S(2)}) async-start(bf16[4,2,192,256]{3,2,1,0:T(8,128)(2,1)} %weight_terms.5), calls=%async_computation.4 | async-start | bytes 1572864 | tf_op jit(solution)/shard_map/all_to_all | solution.py:388
  127.3 5.2 %collective-permute-start.14 = (bf16[192,256]{1,0:T(8,128)(2,1)S(1)}, bf16[192,256]{1,0:T(8,128)(2,1)S(1)}, u32[]{:S(2)}, u32[]{:S(2)}) collective-permute-start(bf16[192,256]{1,0:T(8,128)(2,1)S(1)} %get-tuple-element.56), channel_id=1, source_target_pairs={{0,128},{8,136},{16,144},{24,152},{32,160},{40,168},{48,176},{56,1... | collective-permute-start | bytes 294920 | tf_op jit(solution)/shard_map/ppermute | solution.py:314
  127.8 6.9 %collective-permute-start.15 = (bf16[192,256]{1,0:T(8,128)(2,1)S(1)}, bf16[192,256]{1,0:T(8,128)(2,1)S(1)}, u32[]{:S(2)}, u32[]{:S(2)}) collective-permute-start(bf16[192,256]{1,0:T(8,128)(2,1)S(1)} %get-tuple-element.57), channel_id=1, source_target_pairs={{0,64},{8,72},{16,80},{24,88},{32,96},{40,104},{48,112},{56,120},{... | collective-permute-start | bytes 294920 | tf_op jit(solution)/shard_map/ppermute | solution.py:314
  129.4 5.2 %collective-permute-start.16 = (bf16[192,256]{1,0:T(8,128)(2,1)S(1)}, bf16[192,256]{1,0:T(8,128)(2,1)S(1)}, u32[]{:S(2)}, u32[]{:S(2)}) collective-permute-start(bf16[192,256]{1,0:T(8,128)(2,1)S(1)} %get-tuple-element.58), channel_id=1, source_target_pairs={{0,192},{8,200},{16,208},{24,216},{32,224},{40,232},{48,240},{56,2... | collective-permute-start | bytes 294920 | tf_op jit(solution)/shard_map/ppermute | solution.py:314
  129.6 8.6 %collective-permute-start.22 = (bf16[192,256]{1,0:T(8,128)(2,1)S(1)}, bf16[192,256]{1,0:T(8,128)(2,1)S(1)}, u32[]{:S(2)}, u32[]{:S(2)}) collective-permute-start(bf16[192,256]{1,0:T(8,128)(2,1)S(1)} %get-tuple-element.67), channel_id=1, source_target_pairs={{0,192},{8,200},{16,208},{24,216},{32,224},{40,232},{48,240},{56,2... | collective-permute-start | bytes 294920 | tf_op jit(solution)/shard_map/ppermute | solution.py:314
  131.1 7.8 %collective-permute-start.21 = (bf16[192,256]{1,0:T(8,128)(2,1)S(1)}, bf16[192,256]{1,0:T(8,128)(2,1)S(1)}, u32[]{:S(2)}, u32[]{:S(2)}) collective-permute-start(bf16[192,256]{1,0:T(8,128)(2,1)S(1)} %get-tuple-element.68), channel_id=1, source_target_pairs={{0,64},{8,72},{16,80},{24,88},{32,96},{40,104},{48,112},{56,120},{... | collective-permute-start | bytes 294920 | tf_op jit(solution)/shard_map/ppermute | solution.py:314
  132.4 6.4 %collective-permute-start.20 = (bf16[192,256]{1,0:T(8,128)(2,1)S(1)}, bf16[192,256]{1,0:T(8,128)(2,1)S(1)}, u32[]{:S(2)}, u32[]{:S(2)}) collective-permute-start(bf16[192,256]{1,0:T(8,128)(2,1)S(1)} %select_bitcast_fusion.4), channel_id=1, source_target_pairs={{0,128},{8,136},{16,144},{24,152},{32,160},{40,168},{48,176},{56,1... | collective-permute-start | bytes 294920 | tf_op jit(solution)/shard_map/ppermute | solution.py:314
  134.7 4.4 %collective-permute-start.19 = (bf16[192,256]{1,0:T(8,128)(2,1)S(1)}, bf16[192,256]{1,0:T(8,128)(2,1)S(1)}, u32[]{:S(2)}, u32[]{:S(2)}) collective-permute-start(bf16[192,256]{1,0:T(8,128)(2,1)S(1)} %add_convert_fusion.5), channel_id=1, source_target_pairs={{0,48},{8,56},{64,112},{72,120},{128,176},{136,184},{192,240},{200... | collective-permute-start | bytes 294920 | tf_op jit(solution)/shard_map/ppermute | solution.py:431
  137.5 1.6 collective-permute-start.18
  138.2 0.9 collective-permute-start.17
  139.3 18.8 %collective-permute-start.23 = (bf16[192,256]{1,0:T(8,128)(2,1)S(1)}, bf16[192,256]{1,0:T(8,128)(2,1)S(1)}, u32[]{:S(2)}, u32[]{:S(2)}) collective-permute-start(bf16[192,256]{1,0:T(8,128)(2,1)S(1)} %get-tuple-element.63), channel_id=1, source_target_pairs={{0,225},{1,2},{2,35},{3,68},{4,101},{5,134},{6,167},{7,192},{8,224... | collective-permute-start | bytes 294920 | tf_op jit(solution)/shard_map/ppermute | solution.py:439
  153.6 10.7 %collective-permute-start.24 = (bf16[192,256]{1,0:T(8,128)(2,1)S(1)}, bf16[192,256]{1,0:T(8,128)(2,1)S(1)}, u32[]{:S(2)}, u32[]{:S(2)}) collective-permute-start(bf16[192,256]{1,0:T(8,128)(2,1)S(1)} %select_select_fusion), channel_id=1, source_target_pairs={{0,224},{1,1},{2,34},{3,67},{4,100},{5,133},{6,166},{7,199},{8,225... | collective-permute-start | bytes 294920 | tf_op jit(solution)/shard_map/ppermute | solution.py:440
